TPU v7x, 256 devices: a whole 4x4x8 slice. The times are simulated.
256 devices in a mesh: dp: 4 (over x), context: 4 (over y), tensor: 16 (over z, core).
Axes of the slice: x: 4, y: 4, z: 8, core: 2. Of those that a mesh axis runs over, the one named last changes fastest.
Arguments:
- head_inputs: bfloat16 [4, 1024, 16384], P('dp', 'context', 'tensor'), may hold values from -6 to 6
- gate_inputs: bfloat16 [4, 1024, 16384], P('dp', 'context', 'tensor'), may hold values from -6 to 6
- step_raw: float32 [4, 1024, 256], P('dp', 'context', 'tensor'), may hold values from -4 to 4
- state_write: bfloat16 [4, 1024, 1024], P('dp', 'context', 'tensor'), may hold values from -1 to 1
- state_read: bfloat16 [4, 1024, 1024], P('dp', 'context', 'tensor'), may hold values from -1 to 1
- log_rate: float32 [256], P('tensor'), may hold values from -12 to -2
- skip_gain: float32 [256], P('tensor'), may hold values from 0.5 to 1.5
- step_bias: float32 [256], P('tensor'), may hold values from -1 to 1
- grad_gated: bfloat16 [4, 1024, 16384], P('dp', 'context', 'tensor'), may hold values from -6 to 6
Outputs:
- grad_inputs: bfloat16 [4, 1024, 16384], P('dp', 'context', 'tensor')
- grad_gates: bfloat16 [4, 1024, 16384], P('dp', 'context', 'tensor')
- grad_write: float32 [4, 1024, 1024], P('dp', 'context', 'tensor')
- grad_read: float32 [4, 1024, 1024], P('dp', 'context', 'tensor')
- grad_step: float32 [4, 1024, 256], P('dp', 'context', 'tensor')
- grad_rate: float32 [256], P('tensor')
- grad_skip: float32 [256], P('tensor')
- grad_bias: float32 [256], P('tensor')
All inputs are finite; a program needn't handle non-finite values.
Results may differ from a plain program's by a relative error of at most 0.015.
Values may be sent and summed in bfloat16 or wider, within the bound.
No kernel may reach another device: no remote copies, remote signals or barrier semaphores. Data moves between devices by JAX's collectives and lax.ppermute only.
A program may use at most 64 MiB of HBM per device.

v0:
```python
import jax
import jax.numpy as jnp
from jax import lax
from jax.sharding import PartitionSpec as P

HEADS = 256
HEAD_DIM = 64
GROUPS = 8
STATE = 128
STRETCH = 128


HIGHEST = lax.Precision.HIGHEST


def swapped(block, axis, apart):
    count = lax.axis_size(axis)
    route = []
    for low in range(count):
        high = low | 1 << apart
        if high != low and high < count:
            route += [(low, high), (high, low)]
    return lax.ppermute(block, axis, route)


def passed_along(array, axis, by):
    length = lax.axis_size(axis)
    pairs = [(i, i + by) for i in range(length) if 0 <= i + by < length]
    return lax.ppermute(array, axis, pairs)


def local_forward(values_in, gates_in, raw_steps, writes, reads, rate_log, skips, bias, incoming):
    rows_here = values_in.shape[0]
    heads_here = rate_log.shape[0]
    group_count = writes.shape[1] // STATE
    per_group = heads_here // group_count
    blocks = rows_here // STRETCH
    values = values_in.reshape(blocks, STRETCH, group_count, per_group, HEAD_DIM)
    gates = gates_in.reshape(blocks, STRETCH, group_count, per_group, HEAD_DIM)
    step_sizes = jax.nn.softplus(raw_steps + bias).reshape(blocks, STRETCH, group_count, per_group)
    write_keys = writes.reshape(blocks, STRETCH, group_count, STATE)
    read_keys = reads.reshape(blocks, STRETCH, group_count, STATE)
    decay_rates = jnp.exp(rate_log).reshape(group_count, per_group)
    skip_gain = skips.reshape(group_count, per_group)
    value_half = values.astype(jnp.bfloat16)
    write_half = write_keys.astype(jnp.bfloat16)
    log_decay = -decay_rates * step_sizes
    running = jnp.cumsum(log_decay, axis=1)
    closing = running[:, -1]
    by_head = jnp.moveaxis(running, 1, -1)
    causal = lax.broadcasted_iota(jnp.int32, (STRETCH, STRETCH), 0) >= lax.broadcasted_iota(
        jnp.int32, (STRETCH, STRETCH), 1
    )
    spread = by_head[..., :, None] - by_head[..., None, :]
    damping = jnp.exp(jnp.where(causal, spread, -jnp.inf))
    intersection = jnp.einsum(
        "btgn,bsgn->bgts",
        read_keys.astype(jnp.bfloat16),
        write_half,
        preferred_element_type=jnp.float32,
    )
    weights = (
        damping * intersection[:, :, None] * jnp.moveaxis(step_sizes, 1, -1)[..., None, :]
    ).astype(jnp.bfloat16)
    within = jnp.einsum(
        "bgkts,bsgkp->btgkp", weights, value_half, preferred_element_type=jnp.float32
    )
    leftover = ((jnp.exp(closing[:, None] - running) * step_sizes)[..., None] * values).astype(
        jnp.bfloat16
    )
    block_states = jnp.einsum(
        "bsgkp,bsgn->bgkpn", leftover, write_half, preferred_element_type=jnp.float32
    )
    block_totals = jnp.exp(closing)
    carried = incoming
    starts = []
    for block in range(blocks):
        starts.append(carried)
        carried = block_totals[block][..., None, None] * carried + block_states[block]
    stacked = jnp.stack(starts, axis=0)
    earlier = (
        jnp.einsum("btgn,bgkpn->btgkp", read_keys, stacked, precision=HIGHEST)
        * jnp.exp(running)[..., None]
    )
    output = (within + earlier + skip_gain[..., None] * values) * jax.nn.silu(gates)
    return (output.reshape(rows_here, heads_here * HEAD_DIM), carried)


def body(
    head_inputs,
    gate_inputs,
    step_raw,
    state_write,
    state_read,
    log_rate,
    skip_gain,
    step_bias,
    grad_gated,
):
    rows_here = head_inputs.shape[1]
    heads_here = log_rate.shape[0]
    tensor_count = lax.axis_size("tensor")
    per_group = HEADS // GROUPS
    group_count = max(1, heads_here // per_group)
    inner_heads = heads_here // group_count
    group_span = max(1, tensor_count // GROUPS)
    levels = group_span.bit_length() - 1
    position = lax.axis_index("tensor")
    own_write = state_write[0]
    own_read = state_read[0]
    write_group = own_write
    read_group = own_read
    level = 0
    other_write, other_read = swapped((write_group, read_group), "tensor", level)
    leading = position >> level & 1 == 0
    write_group = jnp.where(
        leading,
        jnp.concatenate([write_group, other_write], axis=1),
        jnp.concatenate([other_write, write_group], axis=1),
    )
    read_group = jnp.where(
        leading,
        jnp.concatenate([read_group, other_read], axis=1),
        jnp.concatenate([other_read, read_group], axis=1),
    )
    writes = write_group.astype(jnp.float32)
    reads = read_group.astype(jnp.float32)
    step_sizes = jax.nn.softplus(step_raw[0] + step_bias).reshape(
        rows_here, group_count, inner_heads
    )
    running = jnp.cumsum(-jnp.exp(log_rate).reshape(group_count, inner_heads) * step_sizes, axis=0)
    closing = running[-1]
    totals = jnp.exp(closing)
    values_full = head_inputs[0].astype(jnp.float32)
    gates_full = gate_inputs[0].astype(jnp.float32)
    values = values_full.reshape(rows_here, group_count, inner_heads, HEAD_DIM)
    upstream = (grad_gated[0].astype(jnp.float32) * jax.nn.silu(gates_full)).reshape(
        rows_here, group_count, inner_heads, HEAD_DIM
    )
    scaled_values = ((jnp.exp(closing[None] - running) * step_sizes)[..., None] * values).astype(
        jnp.bfloat16
    )
    local_state = jnp.einsum(
        "tgkp,tgn->gkpn",
        scaled_values,
        write_group.reshape(rows_here, group_count, STATE),
        preferred_element_type=jnp.float32,
    )
    scaled_upstream = jnp.exp(running)[..., None] * upstream
    local_adjoint = jnp.einsum(
        "tgkp,tgn->gkpn",
        scaled_upstream,
        reads.reshape(rows_here, group_count, STATE),
        precision=HIGHEST,
    )
    zero_state = jnp.zeros_like(local_state)

    def forward_link(rounds, incoming):
        return passed_along(
            (totals[..., None, None] * incoming + local_state).astype(jnp.bfloat16), "context", 1
        ).astype(jnp.float32)

    state_in = lax.fori_loop(0, lax.axis_size("context") - 1, forward_link, zero_state)

    def backward_link(rounds, incoming):
        return passed_along(
            (totals[..., None, None] * incoming + local_adjoint).astype(jnp.bfloat16), "context", -1
        ).astype(jnp.float32)

    adjoint_end = lax.fori_loop(0, lax.axis_size("context") - 1, backward_link, zero_state)
    outputs, pullback = jax.vjp(
        local_forward,
        values_full,
        gates_full,
        step_raw[0],
        writes,
        reads,
        log_rate,
        skip_gain,
        step_bias,
        state_in,
    )
    grads = pullback((grad_gated[0].astype(jnp.float32), adjoint_end))
    (
        grad_values,
        grad_gate_part,
        grad_steps,
        grad_writes,
        grad_reads,
        grad_rates,
        grad_skips,
        grad_biases,
        unused_state,
    ) = grads
    out_write = grad_writes
    out_read = grad_reads
    for level in reversed(range(levels)):
        half_width = out_write.shape[1] // 2
        upper_half = position >> level & 1 == 1
        keep_write = jnp.where(upper_half, out_write[:, half_width:], out_write[:, :half_width])
        send_write = jnp.where(upper_half, out_write[:, :half_width], out_write[:, half_width:])
        keep_read = jnp.where(upper_half, out_read[:, half_width:], out_read[:, :half_width])
        send_read = jnp.where(upper_half, out_read[:, :half_width], out_read[:, half_width:])
        got_write, got_read = (
            swapped(send_write.astype(jnp.bfloat16), "tensor", level).astype(send_write.dtype),
            swapped(send_read.astype(jnp.bfloat16), "tensor", level).astype(send_read.dtype),
        )
        out_write = keep_write + got_write
        out_read = keep_read + got_read
    sum_rate, sum_skip, sum_bias = lax.psum(
        (grad_rates, grad_skips, grad_biases), ("dp", "context")
    )
    return (
        grad_values.astype(jnp.bfloat16)[None],
        grad_gate_part.astype(jnp.bfloat16)[None],
        out_write[None],
        out_read[None],
        grad_steps[None],
        sum_rate,
        sum_skip,
        sum_bias,
    )


def solution(mesh):
    return jax.shard_map(
        body,
        mesh=mesh,
        in_specs=(
            P("dp", "context", "tensor"),
            P("dp", "context", "tensor"),
            P("dp", "context", "tensor"),
            P("dp", "context", "tensor"),
            P("dp", "context", "tensor"),
            P("tensor"),
            P("tensor"),
            P("tensor"),
            P("dp", "context", "tensor"),
        ),
        out_specs=(
            P("dp", "context", "tensor"),
            P("dp", "context", "tensor"),
            P("dp", "context", "tensor"),
            P("dp", "context", "tensor"),
            P("dp", "context", "tensor"),
            P("tensor"),
            P("tensor"),
            P("tensor"),
        ),
        check_vma=False,
    )
```

profile of v0, /device:TPU:224, one launch (start us, length us, event | category | flops | bytes accessed | tf_op | source)
XLA Modules:
  0.0 146.2 jit_solution(2033740747716153693)
XLA Ops:
  1.2 0.7 squeeze.10
  2.0 0.7 squeeze.11
  2.7 0.7 exponential_negate_fusion
  3.4 0.9 broadcast_multiply_fusion
  5.0 1.4 fusion.99
  7.0 0.8 slice_reduce_fusion.1
  9.8 0.7 bitcast_exponential_fusion
  11.7 0.7 copy.328
  12.6 1.5 %reshape.984 = f32[2,128,1,16,64]{1,0,2,4,3:T(2,128)} reshape(bf16[1,256,1024]{1,2,0:T(8,128)(2,1)S(1)} %copy.264) | data formatting | bytes 1572864 | tf_op jit(solution)/shard_map/convert_element_type | solution.py:183
  14.1 1.1 convert_element_type.335
  15.2 1.5 %reshape.985 = f32[2,128,1,16,64]{1,0,2,4,3:T(2,128)} reshape(bf16[1,256,1024]{1,2,0:T(8,128)(2,1)S(1)} %copy.265) | data formatting | bytes 1572864 | tf_op jit(solution)/shard_map/convert_element_type | solution.py:135
  16.7 1.1 convert_element_type.336
  17.7 1.5 %reshape.989 = f32[2,128,1,16,64]{1,0,2,4,3:T(2,128)} reshape(bf16[1,256,1024]{1,2,0:T(8,128)(2,1)S(1)} %copy.288) | data formatting | bytes 1572864 | tf_op jit(solution)/shard_map/convert_element_type | solution.py:134
  19.9 0.7 copy.285
  20.7 0.7 reduce_sum.148
  21.4 0.9 copy.329
  22.9 1.1 maximum_select_fusion.1
  24.0 0.8 fusion.109
  24.9 1.1 convolution_bitcast_fusion.2
  26.1 1.7 %convolution_bitcast_fusion.3 = f32[1,16,64,128]{3,2,1,0:T(8,128)S(1)} fusion(f32[256,16,64]{0,2,1:T(8,128)S(1)} %bitcast.286, f32[256,16,64]{0,2,1:T(8,128)S(1)} %bitcast.287, f32[256,16]{0,1:T(8,128)S(1)} %bitcast.308, bf16[256,64]{0,1:T(8,128)(2,1)} %collective-permute-done.2, bf16[256,64]{0,1:T(8,128)(2,1)S(1)} %bitcast.303, pred[]{:T(512)S(6)} %eq.34), kind=kOutput, calls=%fused_computation.39 | convolution fusion | flops 404520960 | bytes 2703361 | tf_op jit(solution)/shard_map/tgkp,tgn->gkpn/dot_general | solution.py:150
  27.8 28.6 %while.22 = (s32[]{:T(128)}, f32[1,16,64,128]{3,2,1,0:T(8,128)S(1)}, f32[1,16]{1,0:T(1,128)S(1)}, f32[1,16,64,128]{3,2,1,0:T(8,128)S(1)}, s32[]{:T(128)}, /*index=5*/s32[]{:T(128)}) while((s32[]{:T(128)}, f32[1,16,64,128]{3,2,1,0:T(8,128)S(1)}, f32[1,16]{1,0:T(1,128)S(1)}, f32[1,16,64,128]{3,2,1,0:T(8,128)S(1)}, s32[]{:T(128)}, ...), condition=%wide.region_4.5_spmd.clone, body=%wide.region_3.4_spmd.clone.sunk | while | flops 655363 | bytes 3145911 | solution.py:170
  27.9 1.3 collective-permute-start
  29.2 8.9 %collective-permute-done = bf16[1,16,64,128]{3,2,1,0:T(8,128)(2,1)S(1)} collective-permute-done((bf16[1,16,64,128]{3,2,1,0:T(8,128)(2,1)S(1)}, bf16[1,16,64,128]{3,2,1,0:T(8,128)(2,1)S(1)}, u32[]{:S(2)}, u32[]{:S(2)}) %collective-permute-start) | collective-permute-done | bytes 262176 | tf_op jit(solution)/shard_map/while/body/eval_jaxpr/ppermute | solution.py:29
  38.3 1.3 collective-permute-start
  39.6 8.1 %collective-permute-done = bf16[1,16,64,128]{3,2,1,0:T(8,128)(2,1)S(1)} collective-permute-done((bf16[1,16,64,128]{3,2,1,0:T(8,128)(2,1)S(1)}, bf16[1,16,64,128]{3,2,1,0:T(8,128)(2,1)S(1)}, u32[]{:S(2)}, u32[]{:S(2)}) %collective-permute-start) | collective-permute-done | bytes 262176 | tf_op jit(solution)/shard_map/while/body/eval_jaxpr/ppermute | solution.py:29
  47.9 1.3 collective-permute-start
  49.2 7.1 %collective-permute-done = bf16[1,16,64,128]{3,2,1,0:T(8,128)(2,1)S(1)} collective-permute-done((bf16[1,16,64,128]{3,2,1,0:T(8,128)(2,1)S(1)}, bf16[1,16,64,128]{3,2,1,0:T(8,128)(2,1)S(1)}, u32[]{:S(2)}, u32[]{:S(2)}) %collective-permute-start) | collective-permute-done | bytes 262176 | tf_op jit(solution)/shard_map/while/body/eval_jaxpr/ppermute | solution.py:29
  56.4 24.6 %while.23 = (s32[]{:T(128)}, f32[1,16,64,128]{3,2,1,0:T(8,128)S(1)}, f32[1,16]{1,0:T(1,128)S(1)}, f32[1,16,64,128]{3,2,1,0:T(8,128)S(1)}, s32[]{:T(128)}, /*index=5*/s32[]{:T(128)}) while((s32[]{:T(128)}, f32[1,16,64,128]{3,2,1,0:T(8,128)S(1)}, f32[1,16]{1,0:T(1,128)S(1)}, f32[1,16,64,128]{3,2,1,0:T(8,128)S(1)}, s32[]{:T(128)}, ...), condition=%wide.region_6.7_spmd.clone, body=%wide.region_5.6_spmd.clone.sunk | while | flops 655363 | bytes 3145911 | solution.py:163
  56.6 3.5 %collective-permute-start.1 = (bf16[1,16,64,128]{3,2,1,0:T(8,128)(2,1)S(1)}, bf16[1,16,64,128]{3,2,1,0:T(8,128)(2,1)S(1)}, u32[]{:S(2)}, u32[]{:S(2)}) collective-permute-start(bf16[1,16,64,128]{3,2,1,0:T(8,128)(2,1)S(1)} %fusion.123), channel_id=1, source_target_pairs={{0,16},{16,32},{32,48},{1,17},{17,33},{33,49},{2,18},{18,34},{34,5... | collective-permute-start | bytes 786440 | tf_op jit(solution)/shard_map/while/body/eval_jaxpr/ppermute | solution.py:29
  60.1 3.9 %collective-permute-done.1 = bf16[1,16,64,128]{3,2,1,0:T(8,128)(2,1)S(1)} collective-permute-done((bf16[1,16,64,128]{3,2,1,0:T(8,128)(2,1)S(1)}, bf16[1,16,64,128]{3,2,1,0:T(8,128)(2,1)S(1)}, u32[]{:S(2)}, u32[]{:S(2)}) %collective-permute-start.1) | collective-permute-done | bytes 262176 | tf_op jit(solution)/shard_map/while/body/eval_jaxpr/ppermute | solution.py:29
  64.1 4.4 %collective-permute-start.1 = (bf16[1,16,64,128]{3,2,1,0:T(8,128)(2,1)S(1)}, bf16[1,16,64,128]{3,2,1,0:T(8,128)(2,1)S(1)}, u32[]{:S(2)}, u32[]{:S(2)}) collective-permute-start(bf16[1,16,64,128]{3,2,1,0:T(8,128)(2,1)S(1)} %fusion.123), channel_id=1, source_target_pairs={{0,16},{16,32},{32,48},{1,17},{17,33},{33,49},{2,18},{18,34},{34,5... | collective-permute-start | bytes 786440 | tf_op jit(solution)/shard_map/while/body/eval_jaxpr/ppermute | solution.py:29
  68.5 4.0 %collective-permute-done.1 = bf16[1,16,64,128]{3,2,1,0:T(8,128)(2,1)S(1)} collective-permute-done((bf16[1,16,64,128]{3,2,1,0:T(8,128)(2,1)S(1)}, bf16[1,16,64,128]{3,2,1,0:T(8,128)(2,1)S(1)}, u32[]{:S(2)}, u32[]{:S(2)}) %collective-permute-start.1) | collective-permute-done | bytes 262176 | tf_op jit(solution)/shard_map/while/body/eval_jaxpr/ppermute | solution.py:29
  72.7 4.4 %collective-permute-start.1 = (bf16[1,16,64,128]{3,2,1,0:T(8,128)(2,1)S(1)}, bf16[1,16,64,128]{3,2,1,0:T(8,128)(2,1)S(1)}, u32[]{:S(2)}, u32[]{:S(2)}) collective-permute-start(bf16[1,16,64,128]{3,2,1,0:T(8,128)(2,1)S(1)} %fusion.123), channel_id=1, source_target_pairs={{0,16},{16,32},{32,48},{1,17},{17,33},{33,49},{2,18},{18,34},{34,5... | collective-permute-start | bytes 786440 | tf_op jit(solution)/shard_map/while/body/eval_jaxpr/ppermute | solution.py:29
  77.1 3.9 %collective-permute-done.1 = bf16[1,16,64,128]{3,2,1,0:T(8,128)(2,1)S(1)} collective-permute-done((bf16[1,16,64,128]{3,2,1,0:T(8,128)(2,1)S(1)}, bf16[1,16,64,128]{3,2,1,0:T(8,128)(2,1)S(1)}, u32[]{:S(2)}, u32[]{:S(2)}) %collective-permute-start.1) | collective-permute-done | bytes 262176 | tf_op jit(solution)/shard_map/while/body/eval_jaxpr/ppermute | solution.py:29
  81.5 0.8 copy-done.1
  82.6 1.6 %multiply_reduce_fusion.1 = (f32[2,128,16]{1,2,0:T(8,128)}, f32[2,128,1,16,64]{1,4,3,0,2:T(8,128)S(1)}, f32[2,128,1,16,64]{1,4,3,0,2:T(8,128)S(1)}) fusion(f32[2,128,1,16,64]{1,0,2,4,3:T(2,128)S(1)} %copy-done.2, f32[2,128,1,16,64]{1,0,2,4,3:T(2,128)S(1)} %copy-done.1, bf16[2,128,128]{2,1,0:T(8,128)(2,1)S(1)} %get-tuple-element.178, ...), kind=kOutput, calls=%fused_computation.61 | convolution fusion | flops 404746240 | bytes 5324800 | tf_op jit(solution)/shard_map/jvp(btgn,bgkpn->btgkp)/dot_general | solution.py:82
  84.2 2.7 %fusion.12 = (f32[2,16,128]{2,1,0:T(8,128)}, f32[2,16,128]{2,1,0:T(8,128)}, f32[2,16,128]{2,1,0:T(8,128)}, bf16[2,128,128]{2,1,0:T(8,128)(2,1)S(1)}) fusion(f32[2,16,128]{2,1,0:T(8,128)S(1)} %copy-done.20, f32[2,128,128]{2,1,0:T(8,128)S(1)} %copy-done.11, f32[2,16,128]{2,1,0:T(8,128)S(1)} %copy-done.21, pred[128,128]{1,0:T(8,128)(4,1)S(1)} %copy-done.23, ...), kind=kOutput, calls=%fused_computation.18 | convolution fusion | flops 74403840 | bytes 1867776 | tf_op jit(solution)/shard_map/transpose(jvp(bgkts,bsgkp->btgkp))/dot_general | solution.py:65
  87.0 1.8 %fusion.24 = f32[2,128,128]{2,1,0:T(8,128)S(1)} fusion(f32[2,128,128]{2,1,0:T(8,128)S(1)} %fusion.26, f32[2,128,1,16,64]{1,4,3,0,2:T(8,128)S(1)} %get-tuple-element.154, f32[1,1,16,64,128]{4,3,2,1,0:T(8,128)S(1)} %bitcast.282, f32[1,1,16,64,128]{4,3,2,1,0:T(8,128)S(1)} %bitcast.277, f32[2,128,16]{1,2,0:T(8,128)S(1)} %get-tuple-element.167), kind=kOutput, calls=%fused_computation.42 | convolution fusion | flops 403210240 | bytes 2375680 | tf_op jit(solution)/shard_map/transpose(jvp(btgn,bgkpn->btgkp))/dot_general | solution.py:82
  89.7 0.9 copy-done
  91.4 1.5 %fusion.32 = bf16[2,128,1,16,64]{1,4,3,0,2:T(8,128)(2,1)S(1)} fusion(f32[2,128,1,16,64]{1,4,3,0,2:T(8,128)S(1)} %get-tuple-element.171, f32[2,128,1,16,64]{1,0,2,4,3:T(2,128)S(1)} %copy-done, f32[2,128,1,16,64]{1,0,2,4,3:T(2,128)S(1)} %copy-done.1, f32[2,128,1,16,64]{1,0,2,4,3:T(2,128)S(1)} %copy-done.2, f32[2,16,128]{2,1,0:T(8,128)S(1)} %copy-done.20, ...), kind=kOutput, calls=%fused_computation.52 | convolution fusion | flops 73662464 | bytes 5439552 | tf_op jit(solution)/shard_map/jvp(bgkts,bsgkp->btgkp)/dot_general | solution.py:65
  92.9 1.3 fusion.20
  94.7 2.2 %fusion.108 = f32[2,128,1,16]{3,2,1,0:T(1,128)S(1)} fusion(f32[2,128,1,16]{3,2,1,0:T(1,128)S(1)} %copy.309), kind=kOutput, calls=%fused_computation.182 | output fusion | flops 520192 | bytes 32768 | tf_op jit(solution)/shard_map/transpose(jvp(jit(cumsum)))/reduce_window_sum | solution.py:48
  99.5 40.8 %all-reduce.5 = (f32[16]{0:T(128)}, f32[16]{0:T(128)}, f32[16]{0:T(128)}) all-reduce(f32[16]{0:T(128)S(1)} %negate_multiply_fusion, f32[16]{0:T(128)S(1)} %copy-done.32, f32[16]{0:T(128)S(1)} %get-tuple-element.149), channel_id=1, replica_groups=mesh['dp'=4,'context'=4,'tensor'=16] {'dp','context'}, use_global_device_ids=true, to_apply=%region_18.19 | all-reduce | flops 48 | bytes 384 | tf_op jit(solution)/shard_map/psum | solution.py:210
  140.3 0.8 copy.325
  141.1 1.5 %reshape.1000 = bf16[1,256,1024]{2,1,0:T(8,128)(2,1)} reshape(bf16[2,128,1,16,64]{4,3,1,0,2:T(8,128)(2,1)S(1)} %copy.325) | data formatting | bytes 1048576
  142.6 0.8 copy.327
  143.4 1.5 %reshape.1001 = bf16[1,256,1024]{2,1,0:T(8,128)(2,1)} reshape(bf16[2,128,1,16,64]{4,3,1,0,2:T(8,128)(2,1)S(1)} %copy.327) | data formatting | bytes 1048576
  144.9 0.6 add_bitcast_fusion.1
  (146 shorter events, 13.7 us)
Async XLA Ops:
  0.6 7.8 %copy-start.5 = (bf16[1,256,1024]{2,1,0:T(8,128)(2,1)S(1)}, bf16[1,256,1024]{2,1,0:T(8,128)(2,1)}, u32[]{:S(2)}) copy-start(bf16[1,256,1024]{2,1,0:T(8,128)(2,1)} %param.13) | copy-start | bytes 1572868
  0.6 8.0 %copy-start.6 = (bf16[1,256,1024]{2,1,0:T(8,128)(2,1)S(1)}, bf16[1,256,1024]{2,1,0:T(8,128)(2,1)}, u32[]{:S(2)}) copy-start(bf16[1,256,1024]{2,1,0:T(8,128)(2,1)} %param.14) | copy-start | bytes 1572868
  0.7 21.6 %collective-permute-start.3 = (bf16[256,64]{0,1:T(8,128)(2,1)}, bf16[256,64]{0,1:T(8,128)(2,1)S(1)}, u32[]{:S(2)}, u32[]{:S(2)}) collective-permute-start(bf16[256,64]{0,1:T(8,128)(2,1)} %bitcast.292), channel_id=1, source_target_pairs={{0,1},{1,0},{2,3},{3,2},{4,5},{5,4},{6,7},{7,6},{8,9},{9,8},{10,11... | collective-permute-start | bytes 98312 | tf_op jit(solution)/shard_map/ppermute | solution.py:23
  0.8 20.6 %collective-permute-start.2 = (bf16[256,64]{0,1:T(8,128)(2,1)}, bf16[256,64]{0,1:T(8,128)(2,1)}, u32[]{:S(2)}, u32[]{:S(2)}) collective-permute-start(bf16[256,64]{0,1:T(8,128)(2,1)} %bitcast.302), channel_id=1, source_target_pairs={{0,1},{1,0},{2,3},{3,2},{4,5},{5,4},{6,7},{7,6},{8,9},{9,8},{10,11... | collective-permute-start | bytes 98312 | tf_op jit(solution)/shard_map/ppermute | solution.py:23
  3.4 3.3 %copy-start.28 = (f32[16]{0:T(128)}, f32[16]{0:T(128)S(1)}, u32[]{:S(2)}) copy-start(f32[16]{0:T(128)S(1)} %exponential_negate_fusion) | copy-start | bytes 196
  6.7 3.1 %copy-start.18 = (f32[2,1,1,16]{3,2,1,0:T(1,128)}, f32[2,1,1,16]{3,2,1,0:T(1,128)S(1)}, u32[]{:S(2)}) copy-start(f32[2,1,1,16]{3,2,1,0:T(1,128)S(1)} %get-tuple-element.164) | copy-start | bytes 388
  8.4 1.0 copy-start.7
  8.6 1.2 copy-start.14
  9.7 1.9 %copy-start.9 = (bf16[1,256,64]{1,2,0:T(8,128)(2,1)S(1)}, bf16[1,256,64]{1,2,0:T(8,128)(2,1)}, u32[]{:S(2)}) copy-start(bf16[1,256,64]{1,2,0:T(8,128)(2,1)} %param.16) | copy-start | bytes 98308
  9.7 2.0 %copy-start.16 = (bf16[1,256,64]{1,2,0:T(8,128)(2,1)S(1)}, bf16[1,256,64]{1,2,0:T(8,128)(2,1)}, u32[]{:S(2)}) copy-start(bf16[1,256,64]{1,2,0:T(8,128)(2,1)} %param.17) | copy-start | bytes 98308
  22.3 0.6 copy-start.10
  22.9 3.1 %copy-start.4 = (f32[1,256,1024]{1,2,0:T(8,128)S(1)}, f32[1,256,1024]{1,2,0:T(8,128)}, u32[]{:S(2)}) copy-start(f32[1,256,1024]{1,2,0:T(8,128)} %convert_element_type.336) | copy-start | bytes 3145732
  24.0 2.0 %copy-start.3 = (f32[1,256,1024]{1,2,0:T(8,128)S(1)}, f32[1,256,1024]{1,2,0:T(8,128)}, u32[]{:S(2)}) copy-start(f32[1,256,1024]{1,2,0:T(8,128)} %convert_element_type.335) | copy-start | bytes 3145732
  24.0 2.0 %copy-start.17 = (bf16[1,256,64]{1,2,0:T(8,128)(2,1)S(1)}, bf16[1,256,64]{1,2,0:T(8,128)(2,1)}, u32[]{:S(2)}) copy-start(bf16[1,256,64]{1,2,0:T(8,128)(2,1)} %param.17) | copy-start | bytes 98308
  24.0 2.0 %copy-start.24 = (f32[256,1,16]{0,2,1:T(8,128)S(1)}, f32[256,1,16]{0,2,1:T(8,128)}, u32[]{:S(2)}) copy-start(f32[256,1,16]{0,2,1:T(8,128)} %copy.393) | copy-start | bytes 49156
  26.0 1.7 %copy-start.13 = (f32[16]{0:T(128)S(1)}, f32[16]{0:T(128)}, u32[]{:S(2)}) copy-start(f32[16]{0:T(128)} %get-tuple-element.129) | copy-start | bytes 196
  27.9 10.2 %collective-permute-start = (bf16[1,16,64,128]{3,2,1,0:T(8,128)(2,1)S(1)}, bf16[1,16,64,128]{3,2,1,0:T(8,128)(2,1)S(1)}, u32[]{:S(2)}, u32[]{:S(2)}) collective-permute-start(bf16[1,16,64,128]{3,2,1,0:T(8,128)(2,1)S(1)} %fusion.122), channel_id=1, source_target_pairs={{16,0},{32,16},{48,32},{17,1},{33,17},{49,33},{18,2},{34,18},{50,3... | collective-permute-start | bytes 786440 | tf_op jit(solution)/shard_map/while/body/eval_jaxpr/ppermute | solution.py:29
  38.3 9.4 %collective-permute-start = (bf16[1,16,64,128]{3,2,1,0:T(8,128)(2,1)S(1)}, bf16[1,16,64,128]{3,2,1,0:T(8,128)(2,1)S(1)}, u32[]{:S(2)}, u32[]{:S(2)}) collective-permute-start(bf16[1,16,64,128]{3,2,1,0:T(8,128)(2,1)S(1)} %fusion.122), channel_id=1, source_target_pairs={{16,0},{32,16},{48,32},{17,1},{33,17},{49,33},{18,2},{34,18},{50,3... | collective-permute-start | bytes 786440 | tf_op jit(solution)/shard_map/while/body/eval_jaxpr/ppermute | solution.py:29
  47.9 8.4 %collective-permute-start = (bf16[1,16,64,128]{3,2,1,0:T(8,128)(2,1)S(1)}, bf16[1,16,64,128]{3,2,1,0:T(8,128)(2,1)S(1)}, u32[]{:S(2)}, u32[]{:S(2)}) collective-permute-start(bf16[1,16,64,128]{3,2,1,0:T(8,128)(2,1)S(1)} %fusion.122), channel_id=1, source_target_pairs={{16,0},{32,16},{48,32},{17,1},{33,17},{49,33},{18,2},{34,18},{50,3... | collective-permute-start | bytes 786440 | tf_op jit(solution)/shard_map/while/body/eval_jaxpr/ppermute | solution.py:29
  56.4 24.7 %copy-start.12 = (f32[2,128,16]{1,2,0:T(8,128)S(1)}, f32[2,128,16]{1,2,0:T(8,128)}, u32[]{:S(2)}) copy-start(f32[2,128,16]{1,2,0:T(8,128)} %get-tuple-element.168) | copy-start | bytes 49156
  56.4 24.7 %copy-start.31 = (f32[16]{0:T(128)S(1)}, f32[16]{0:T(128)}, u32[]{:S(2)}) copy-start(f32[16]{0:T(128)} %get-tuple-element.170) | copy-start | bytes 196
  56.6 7.4 %collective-permute-start.1 = (bf16[1,16,64,128]{3,2,1,0:T(8,128)(2,1)S(1)}, bf16[1,16,64,128]{3,2,1,0:T(8,128)(2,1)S(1)}, u32[]{:S(2)}, u32[]{:S(2)}) collective-permute-start(bf16[1,16,64,128]{3,2,1,0:T(8,128)(2,1)S(1)} %fusion.123), channel_id=1, source_target_pairs={{0,16},{16,32},{32,48},{1,17},{17,33},{33,49},{2,18},{18,34},{34,5... | collective-permute-start | bytes 786440 | tf_op jit(solution)/shard_map/while/body/eval_jaxpr/ppermute | solution.py:29
  64.1 8.4 %collective-permute-start.1 = (bf16[1,16,64,128]{3,2,1,0:T(8,128)(2,1)S(1)}, bf16[1,16,64,128]{3,2,1,0:T(8,128)(2,1)S(1)}, u32[]{:S(2)}, u32[]{:S(2)}) collective-permute-start(bf16[1,16,64,128]{3,2,1,0:T(8,128)(2,1)S(1)} %fusion.123), channel_id=1, source_target_pairs={{0,16},{16,32},{32,48},{1,17},{17,33},{33,49},{2,18},{18,34},{34,5... | collective-permute-start | bytes 786440 | tf_op jit(solution)/shard_map/while/body/eval_jaxpr/ppermute | solution.py:29
  72.7 8.3 %collective-permute-start.1 = (bf16[1,16,64,128]{3,2,1,0:T(8,128)(2,1)S(1)}, bf16[1,16,64,128]{3,2,1,0:T(8,128)(2,1)S(1)}, u32[]{:S(2)}, u32[]{:S(2)}) collective-permute-start(bf16[1,16,64,128]{3,2,1,0:T(8,128)(2,1)S(1)} %fusion.123), channel_id=1, source_target_pairs={{0,16},{16,32},{32,48},{1,17},{17,33},{33,49},{2,18},{18,34},{34,5... | collective-permute-start | bytes 786440 | tf_op jit(solution)/shard_map/while/body/eval_jaxpr/ppermute | solution.py:29
  81.1 1.2 copy-start.1
  81.1 1.5 %copy-start.2 = (f32[2,128,1,16,64]{1,0,2,4,3:T(2,128)S(1)}, f32[2,128,1,16,64]{1,0,2,4,3:T(2,128)}, u32[]{:S(2)}) copy-start(f32[2,128,1,16,64]{1,0,2,4,3:T(2,128)} %reshape.985) | copy-start | bytes 3145732
  82.6 1.6 %copy-start.11 = (f32[2,128,128]{2,1,0:T(8,128)S(1)}, f32[2,128,128]{2,1,0:T(8,128)}, u32[]{:S(2)}) copy-start(f32[2,128,128]{2,1,0:T(8,128)} %fusion.109) | copy-start | bytes 393220
  82.6 1.6 %copy-start.20 = (f32[2,16,128]{2,1,0:T(8,128)S(1)}, f32[2,16,128]{2,1,0:T(8,128)}, u32[]{:S(2)}) copy-start(f32[2,16,128]{2,1,0:T(8,128)} %get-tuple-element.165) | copy-start | bytes 49156
  82.6 1.6 %copy-start.21 = (f32[2,16,128]{2,1,0:T(8,128)S(1)}, f32[2,16,128]{2,1,0:T(8,128)}, u32[]{:S(2)}) copy-start(f32[2,16,128]{2,1,0:T(8,128)} %copy.285) | copy-start | bytes 49156
  82.6 1.6 %copy-start.23 = (pred[128,128]{1,0:T(8,128)(4,1)S(1)}, pred[128,128]{1,0:T(8,128)(4,1)}, u32[]{:S(2)}) copy-start(pred[128,128]{1,0:T(8,128)(4,1)} %iota_compare_fusion) | copy-start | bytes 49156
  87.0 1.9 %copy-start.30 = (f32[16]{0:T(128)S(1)}, f32[16]{0:T(128)}, u32[]{:S(2)}) copy-start(f32[16]{0:T(128)} %get-tuple-element.169) | copy-start | bytes 196
  89.3 1.2 copy-start
  90.6 0.7 copy-start.15
  90.6 0.7 copy-start.19
  90.6 0.8 copy-start.33
  92.9 1.5 %copy-start.25 = (f32[2,128,16]{1,2,0:T(8,128)S(1)}, f32[2,128,16]{1,2,0:T(8,128)}, u32[]{:S(2)}) copy-start(f32[2,128,16]{1,2,0:T(8,128)} %get-tuple-element.153) | copy-start | bytes 49156
  92.9 1.5 %copy-start.26 = (f32[2,16,128]{2,1,0:T(8,128)S(1)}, f32[2,16,128]{2,1,0:T(8,128)}, u32[]{:S(2)}) copy-start(f32[2,16,128]{2,1,0:T(8,128)} %get-tuple-element.124) | copy-start | bytes 49156
  92.9 1.5 %copy-start.27 = (f32[2,16,128]{2,1,0:T(8,128)S(1)}, f32[2,16,128]{2,1,0:T(8,128)}, u32[]{:S(2)}) copy-start(f32[2,16,128]{2,1,0:T(8,128)} %get-tuple-element.125) | copy-start | bytes 49156
  94.3 2.7 %copy-start.8 = (f32[1,256,16]{1,2,0:T(8,128)S(1)}, f32[1,256,16]{1,2,0:T(8,128)}, u32[]{:S(2)}) copy-start(f32[1,256,16]{1,2,0:T(8,128)} %param.15) | copy-start | bytes 49156
  94.3 3.0 %copy-start.22 = (f32[2,16,128]{2,1,0:T(8,128)S(1)}, f32[2,16,128]{2,1,0:T(8,128)}, u32[]{:S(2)}) copy-start(f32[2,16,128]{2,1,0:T(8,128)} %get-tuple-element.126) | copy-start | bytes 49156
  94.3 3.0 %copy-start.29 = (f32[16]{0:T(128)S(1)}, f32[16]{0:T(128)}, u32[]{:S(2)}) copy-start(f32[16]{0:T(128)} %copy-done.28) | copy-start | bytes 196
  97.5 0.8 copy-start.34
  97.6 1.9 %copy-start.32 = (f32[16]{0:T(128)S(1)}, f32[16]{0:T(128)}, u32[]{:S(2)}) copy-start(f32[16]{0:T(128)} %reduce_sum.148) | copy-start | bytes 196
  97.9 47.1 %collective-permute-start.4 = (bf16[256,64]{0,1:T(8,128)(2,1)S(1)}, bf16[256,64]{0,1:T(8,128)(2,1)S(1)}, u32[]{:S(2)}, u32[]{:S(2)}) collective-permute-start(bf16[256,64]{0,1:T(8,128)(2,1)S(1)} %select_convert_fusion.1), channel_id=1, source_target_pairs={{0,1},{1,0},{2,3},{3,2},{4,5},{5,4},{6,7},{7,6},{8,9},{9,8},{10,11... | collective-permute-start | bytes 98312 | tf_op jit(solution)/shard_map/ppermute | solution.py:23
  99.0 46.6 %collective-permute-start.5 = (bf16[256,64]{0,1:T(8,128)(2,1)S(1)}, bf16[256,64]{0,1:T(8,128)(2,1)S(1)}, u32[]{:S(2)}, u32[]{:S(2)}) collective-permute-start(bf16[256,64]{0,1:T(8,128)(2,1)S(1)} %select_convert_fusion), channel_id=1, source_target_pairs={{0,1},{1,0},{2,3},{3,2},{4,5},{5,4},{6,7},{7,6},{8,9},{9,8},{10,11... | collective-permute-start | bytes 98312 | tf_op jit(solution)/shard_map/ppermute | solution.py:23
where the time goes:
time: 147 us; the launch traced here: 146 us
  blocking collectives  40.8 us (28%)
  waiting for transfers between devices  35.8 us (24%)
  local copies, waits for them, and re-layouts  21.2 us (14%)
  starting transfers between devices  17.4 us (12%)
  other arithmetic  15 us (10%)
  matrix products  14.4 us (10%)
    psum x1, blocking collectives, body(): lax.psum((grad_rates, grad_skips, grad_biases), ('dp', 'context'))  40.8 us
    ppermute x6, waiting for transfers between devices, passed_along(): return lax.ppermute(array, axis, pairs)  35.8 us
    ppermute x6, starting transfers between devices, passed_along(): return lax.ppermute(array, axis, pairs)  16.2 us
    unnamed x84, local copies, waits for them, and re-layouts  10.1 us
    dot_general x3, matrix products, local_forward(): jnp.einsum('bgkts,bsgkp->btgkp', weights, value_half, preferred_element_t...  5.47 us
    dot_general x2, matrix products, local_forward(): jnp.einsum('btgn,bgkpn->btgkp', read_keys, stacked, precision=HIGHEST)  3.4 us
  transfers between devices with their start and end apart: 10, of which 6 were waited for; matrix products, arithmetic and copies ran while one was open for 18% of the time, Pallas kernels for 0%

commit v1 on v0

v1 whole, which is shorter than its diff:
```python
import functools
import math

import jax
import jax.numpy as jnp
from jax import lax
from jax.experimental import pallas as pl
from jax.experimental.pallas import tpu as pltpu
from jax.sharding import PartitionSpec as P

HEAD_DIM = 64
STATE = 128
BLOCK = 128
LOG2E = math.log2(math.e)
F32 = jnp.float32
BF16 = jnp.bfloat16
TILE = 256


def dot(a, b, dims=((1,), (0,))):
    return lax.dot_general(a, b, (dims, ((), ())), preferred_element_type=F32)


def pieces(v, count):
    out = []
    for _ in range(count):
        part = v.astype(BF16)
        out.append(part)
        v = v - part.astype(F32)
    return out


def split_dot_left(exact, v, count):
    return sum(dot(exact, part) for part in pieces(v, count))


def split_dot_right(v, exact, count):
    return sum(dot(part, exact) for part in pieces(v, count))


def expander(heads, lo, size):
    head = lax.broadcasted_iota(jnp.int32, (heads, size), 0)
    column = lax.broadcasted_iota(jnp.int32, (heads, size), 1) + lo
    return ((column >= head * HEAD_DIM) & (column < (head + 1) * HEAD_DIM)).astype(BF16)


def selector(heads, lo, size):
    head = lax.broadcasted_iota(jnp.int32, (size, heads), 1)
    column = lax.broadcasted_iota(jnp.int32, (size, heads), 0) + lo
    return ((column >= head * HEAD_DIM) & (column < (head + 1) * HEAD_DIM)).astype(BF16)


def triangle(rows, lower):
    i = lax.broadcasted_iota(jnp.int32, (rows, rows), 0)
    j = lax.broadcasted_iota(jnp.int32, (rows, rows), 1)
    return ((i >= j) if lower else (i <= j)).astype(BF16)


def softplus(z):
    return jnp.maximum(z, 0.0) + jnp.log(1.0 + jnp.exp(-jnp.abs(z)))


def both(own_ref, other_ref):
    return jnp.concatenate([own_ref[...], other_ref[...]], axis=1)


def kernel_local(
    x_ref, g_ref, dy_ref, raw_ref, bias_ref, rate_ref, wo_ref, wt_ref, ro_ref, rt_ref,
    up_ref, down_ref, ua_ref, xb_ref, al_ref, be_ref, wide_ref, small_ref,
    al_e, be_e,
):
    rows, cols = x_ref.shape
    heads = raw_ref.shape[1]
    step = softplus(raw_ref[...] + bias_ref[...])
    log2_decay = step * (-LOG2E * jnp.exp(rate_ref[...]))
    run = split_dot_left(triangle(rows, True), log2_decay, 3)
    mid0 = run[BLOCK // 2 - 1 : BLOCK // 2]
    mid1 = run[BLOCK + BLOCK // 2 - 1 : BLOCK + BLOCK // 2]
    end = run[rows - 1 : rows]
    row = lax.broadcasted_iota(jnp.int32, (rows, heads), 0)
    rel = run - jnp.where(row < BLOCK, mid0, mid1)
    al = jnp.exp2(rel)
    be = jnp.exp2(-rel) * step
    al_ref[...] = al
    be_ref[...] = be
    small = jnp.exp2(
        jnp.concatenate([mid0, mid1, end - mid0, end - mid1, mid1 - mid0, end, end, end], axis=0)
    )
    small_ref[...] = small
    for lo in range(0, cols, TILE):
        wide = expander(heads, lo, TILE)
        here = pl.ds(lo, TILE)
        al_e[:, here] = split_dot_right(al, wide, 2)
        be_e[:, here] = split_dot_right(be, wide, 2)
        wide_ref[:, here] = split_dot_right(small, wide, 3)
    writes = both(wo_ref, wt_ref).astype(F32).T.astype(BF16)
    reads = both(ro_ref, rt_ref).astype(F32).T.astype(BF16)
    place = lax.axis_index("context")
    last = lax.axis_size("context") - 1
    tail = pl.ds(cols, 8)
    for lo in range(0, cols, BLOCK):
        here = pl.ds(lo, BLOCK)
        state = None
        adjoint = None
        for b in range(rows // BLOCK):
            at = pl.ds(b * BLOCK, BLOCK)
            g = g_ref[at, here].astype(F32)
            u = dy_ref[at, here].astype(F32) * g / (1.0 + jnp.exp(-g))
            ua = (u * al_e[at, here]).astype(BF16)
            xb = (x_ref[at, here].astype(F32) * be_e[at, here]).astype(BF16)
            ua_ref[at, here] = ua
            xb_ref[at, here] = xb
            s = dot(writes[:, b * BLOCK : (b + 1) * BLOCK], xb) * wide_ref[2 + b : 3 + b, here]
            a = dot(reads[:, b * BLOCK : (b + 1) * BLOCK], ua) * wide_ref[b : b + 1, here]
            state = s if state is None else state + s
            adjoint = a if adjoint is None else adjoint + a
        state = state.astype(BF16)
        adjoint = adjoint.astype(BF16)
        up_ref[here, :] = jnp.where(place == last, adjoint, state)
        down_ref[here, :] = jnp.where(place == 0, state, adjoint)
    total = jnp.concatenate(
        [wide_ref[5:6, pl.ds(lo, BLOCK)] for lo in range(0, cols, BLOCK)], axis=0
    )
    totals = jnp.concatenate([p.astype(F32) for p in pieces(total, 2)], axis=0).astype(BF16)
    up_ref[pl.ds(cols, 16), :] = totals
    down_ref[pl.ds(cols, 16), :] = totals


def kernel_within(
    x_ref, g_ref, dy_ref, skip_ref, wo_ref, wt_ref, ro_ref, rt_ref,
    ua_ref, xb_ref, al_ref, be_ref, wide_ref,
    gate_ref, gate_f_ref, in_ref, in_f_ref, dr_ref, dw_ref, p_ref, q_ref, skip_out_ref,
    al_e, be_e, skip_e,
):
    rows, cols = x_ref.shape
    heads = skip_ref.shape[1]
    for lo in range(0, cols, TILE):
        wide = expander(heads, lo, TILE)
        here = pl.ds(lo, TILE)
        al_e[:, here] = split_dot_right(al_ref[...], wide, 2)
        be_e[:, here] = split_dot_right(be_ref[...], wide, 2)
        skip_e[:, here] = split_dot_right(jnp.broadcast_to(skip_ref[...], (8, heads)), wide, 3)
    writes = both(wo_ref, wt_ref)
    reads = both(ro_ref, rt_ref)
    w = [writes[:BLOCK], writes[BLOCK:]]
    r = [reads[:BLOCK], reads[BLOCK:]]
    i = lax.broadcasted_iota(jnp.int32, (BLOCK, BLOCK), 0)
    j = lax.broadcasted_iota(jnp.int32, (BLOCK, BLOCK), 1)
    nt = ((1,), (1,))
    i00 = jnp.where(i >= j, dot(r[0], w[0], nt), 0.0)
    i11 = jnp.where(i >= j, dot(r[1], w[1], nt), 0.0)
    i10 = dot(r[1], w[0], nt)
    t00, t11, t10 = i00.T.astype(BF16), i11.T.astype(BF16), i10.T.astype(BF16)
    i00, i11, i10 = i00.astype(BF16), i11.astype(BF16), i10.astype(BF16)
    m00 = jnp.zeros((BLOCK, BLOCK), F32)
    m11 = m00
    m10 = m00
    first = pl.ds(0, BLOCK)
    second = pl.ds(BLOCK, BLOCK)
    p = [jnp.zeros((BLOCK, heads), F32)] * 2
    q = [jnp.zeros((BLOCK, heads), F32)] * 2
    skips = jnp.zeros((8, heads), F32)
    for lo in range(0, cols, BLOCK):
        here = pl.ds(lo, BLOCK)
        sel = selector(heads, lo, BLOCK)
        link = wide_ref[4:5, here]
        ua = [ua_ref[first, here], ua_ref[second, here]]
        xb = [xb_ref[first, here], xb_ref[second, here]]
        m00 += dot(ua[0], xb[0], nt)
        m11 += dot(ua[1], xb[1], nt)
        m10 += dot(ua[1], (xb[0].astype(F32) * link).astype(BF16), nt)
        v = [dot(i00, xb[0]), dot(i11, xb[1]) + link * dot(i10, xb[0])]
        z = [dot(t00, ua[0]) + link * dot(t10, ua[1]), dot(t11, ua[1])]
        skip = skip_e[0:1, here]
        for b in range(2):
            at = pl.ds(b * BLOCK, BLOCK)
            p[b] += split_dot_right(ua[b].astype(F32) * v[b], sel, 2)
            q[b] += split_dot_right(xb[b].astype(F32) * z[b], sel, 2)
            g = g_ref[at, here].astype(F32)
            dy = dy_ref[at, here].astype(F32)
            x = x_ref[at, here].astype(F32)
            sig = 1.0 / (1.0 + jnp.exp(-g))
            u = dy * g * sig
            up = dy * sig * (1.0 + g * (1.0 - sig))
            al = al_e[at, here]
            be = be_e[at, here]
            gate_ref[at, here] = (up * (al * v[b] + skip * x)).astype(BF16)
            gate_f_ref[at, here] = (up * al * wide_ref[b : b + 1, here]).astype(BF16)
            in_ref[at, here] = (be * z[b] + skip * u).astype(BF16)
            in_f_ref[at, here] = (be * wide_ref[2 + b : 3 + b, here]).astype(BF16)
            ux = jnp.sum((u * x).reshape(BLOCK // 8, 8, BLOCK), axis=0)
            skips += split_dot_right(ux, sel, 3)
    for b in range(2):
        p_ref[pl.ds(b * BLOCK, BLOCK), :] = p[b]
        q_ref[pl.ds(b * BLOCK, BLOCK), :] = q[b]
    skip_out_ref[...] = skips
    m00 = jnp.where(i >= j, m00, 0.0)
    m11 = jnp.where(i >= j, m11, 0.0)
    n00, n11, n10 = m00.T.astype(BF16), m11.T.astype(BF16), m10.T.astype(BF16)
    m00, m11, m10 = m00.astype(BF16), m11.astype(BF16), m10.astype(BF16)
    dr_ref[first, :] = dot(m00, w[0])
    dr_ref[second, :] = dot(m10, w[0]) + dot(m11, w[1])
    dw_ref[first, :] = dot(n00, r[0]) + dot(n10, r[1])
    dw_ref[second, :] = dot(n11, r[1])


def kernel_steps(
    a_ref, b_ref, c_ref, d_ref, wo_ref, wt_ref, ro_ref, rt_ref, ua_ref, xb_ref, p_ref, q_ref,
    small_ref, raw_ref, bias_ref, rate_ref, skips_ref,
    state_ref, adjoint_ref, step_ref, sums_ref,
):
    rows, cols = ua_ref.shape
    heads = raw_ref.shape[1]
    place = lax.axis_index("context")
    last = lax.axis_size("context") - 1
    writes = both(wo_ref, wt_ref)
    reads = both(ro_ref, rt_ref)
    p = jnp.zeros((rows, heads), F32)
    q = jnp.zeros((rows, heads), F32)
    cross = jnp.zeros((8, heads), F32)

    def total(ref, k):
        hi = ref[pl.ds(cols, 8), :].astype(F32)[k : k + 1]
        lo = ref[pl.ds(cols + 8, 8), :].astype(F32)[k : k + 1]
        return hi + lo

    def masked(keep, v):
        return jnp.where(keep, v, 0.0)

    for k in range(cols // BLOCK):
        here = pl.ds(k * BLOCK, BLOCK)
        ta, tb, tc, td = (total(ref, k) for ref in (a_ref, b_ref, c_ref, d_ref))
        got_a, got_b, got_c, got_d = (
            ref[here, :].astype(F32) for ref in (a_ref, b_ref, c_ref, d_ref)
        )
        state = (
            masked(place >= 1, 1.0) * got_a
            + masked(place >= 2, ta) * got_c
            + masked(place >= 3, ta * tc) * got_b
        )
        adjoint = (
            masked(place <= last - 1, 1.0) * got_b
            + masked(place <= last - 2, tb) * got_d
            + masked(place <= last - 3, tb * td) * got_a
        )
        sel = selector(heads, k * BLOCK, BLOCK)
        both_sum = jnp.sum((state * adjoint).reshape(STATE // 8, 8, BLOCK), axis=0)
        cross += split_dot_right(both_sum, sel, 2)
        state = state.astype(BF16)
        adjoint = adjoint.astype(BF16)
        state_ref[:, here] = state
        adjoint_ref[:, here] = adjoint
        p += split_dot_right(ua_ref[:, here].astype(F32) * dot(reads, state), sel, 2)
        q += split_dot_right(xb_ref[:, here].astype(F32) * dot(writes, adjoint), sel, 2)
    row = lax.broadcasted_iota(jnp.int32, (rows, heads), 0)
    p = p * jnp.where(row < BLOCK, small_ref[0:1], small_ref[1:2])
    q = q * jnp.where(row < BLOCK, small_ref[2:3], small_ref[3:4])
    ends = jnp.sum(q, axis=0, keepdims=True) + small_ref[5:6] * jnp.sum(
        cross, axis=0, keepdims=True
    )
    q = q + q_ref[...]
    flow = split_dot_left(triangle(rows, False), p + p_ref[...] - q, 3) + ends
    z = raw_ref[...] + bias_ref[...]
    step = softplus(z)
    rate = jnp.exp(rate_ref[...])
    grad = (q / step - rate * flow) / (1.0 + jnp.exp(-z))
    step_ref[...] = grad
    sum_rate = jnp.sum(flow * step, axis=0, keepdims=True) * -rate
    sum_bias = jnp.sum(grad, axis=0, keepdims=True)
    sum_skip = jnp.sum(skips_ref[...], axis=0, keepdims=True)
    index = lax.broadcasted_iota(jnp.int32, (8, heads), 0)
    sums_ref[...] = jnp.where(
        index == 0, sum_rate, jnp.where(index == 1, sum_skip, jnp.where(index == 2, sum_bias, 0.0))
    )


def kernel_last(
    state_ref, adjoint_ref, wo_ref, wt_ref, ro_ref, rt_ref, ua_ref, xb_ref, wide_ref,
    gate_ref, gate_f_ref, in_ref, in_f_ref, dr_ref, dw_ref,
    grad_in_ref, grad_gate_ref, keep_w_ref, keep_r_ref, send_ref,
):
    rows, cols = ua_ref.shape
    half = wo_ref.shape[1]
    nt = ((1,), (1,))
    writes = both(wo_ref, wt_ref)
    reads = both(ro_ref, rt_ref)
    for b in range(2):
        at = pl.ds(b * BLOCK, BLOCK)
        dr = dr_ref[at, :]
        dw = dw_ref[at, :]
        for lo in range(0, cols, BLOCK):
            here = pl.ds(lo, BLOCK)
            s = state_ref[:, here]
            a = adjoint_ref[:, here]
            scaled_s = (s.astype(F32) * wide_ref[b : b + 1, here]).astype(BF16)
            scaled_a = (a.astype(F32) * wide_ref[2 + b : 3 + b, here]).astype(BF16)
            dr += dot(ua_ref[at, here], scaled_s, nt)
            dw += dot(xb_ref[at, here], scaled_a, nt)
            v = dot(reads[b * BLOCK : (b + 1) * BLOCK], s)
            z = dot(writes[b * BLOCK : (b + 1) * BLOCK], a)
            grad_gate_ref[at, here] = (
                gate_ref[at, here].astype(F32) + gate_f_ref[at, here].astype(F32) * v
            ).astype(BF16)
            grad_in_ref[at, here] = (
                in_ref[at, here].astype(F32) + in_f_ref[at, here].astype(F32) * z
            ).astype(BF16)
        keep_w_ref[at, :] = dw[:, :half]
        keep_r_ref[at, :] = dr[:, :half]
        send_ref[at, :] = jnp.concatenate([dw[:, half:], dr[:, half:]], axis=1).astype(BF16)


def call(kernel, outs, args, scratch=(), us=3.0):
    shapes = [jax.ShapeDtypeStruct(s, d) for s, d in outs]
    return pl.pallas_call(
        kernel,
        out_shape=shapes,
        in_specs=[pl.BlockSpec(memory_space=pltpu.VMEM)] * len(args),
        out_specs=[pl.BlockSpec(memory_space=pltpu.VMEM)] * len(outs),
        scratch_shapes=list(scratch),
        compiler_params=pltpu.CompilerParams(vmem_limit_bytes=40 * 1024 * 1024),
        cost_estimate=pl.CostEstimate(
            flops=int(us * 1e9), bytes_accessed=int(us * 1e6), transcendentals=0
        ),
    )(*args)


def cycle(array, axis, by):
    count = lax.axis_size(axis)
    return lax.ppermute(array, axis, [(i, (i + by) % count) for i in range(count)])


def swap(array):
    count = lax.axis_size("tensor")
    return lax.ppermute(array, "tensor", [(i, i ^ 1) for i in range(count)])


def all_sum(array, axis):
    count = lax.axis_size(axis)
    return sum([cycle(array, axis, by) for by in range(1, count)], array)


def body(
    head_inputs,
    gate_inputs,
    step_raw,
    state_write,
    state_read,
    log_rate,
    skip_gain,
    step_bias,
    grad_gated,
):
    x, g, dy = head_inputs[0], gate_inputs[0], grad_gated[0]
    raw = step_raw[0]
    rows, cols = x.shape
    heads = raw.shape[1]
    half = state_write.shape[2]
    wo, ro = state_write[0], state_read[0]
    wt, rt = swap(wo), swap(ro)
    rate, skip, bias = (v.reshape(1, heads) for v in (log_rate, skip_gain, step_bias))
    keys = [wo, wt, ro, rt]
    payload = ((cols + 16, STATE), BF16)
    big = ((rows, cols), BF16)
    thin = ((rows, heads), F32)
    up, down, ua, xb, al, be, wide, small = call(
        kernel_local,
        [payload, payload, big, big, thin, thin, ((8, cols), F32), ((8, heads), F32)],
        [x, g, dy, raw, bias, rate] + keys,
        [pltpu.VMEM((rows, cols), F32)] * 2,
    )
    got_a = cycle(up, "context", 1)
    got_b = cycle(down, "context", -1)
    got_c = cycle(got_a, "context", 1)
    got_d = cycle(got_b, "context", -1)
    gate, gate_f, inp, inp_f, dr, dw, p, q, skips = call(
        kernel_within,
        [big] * 4 + [((rows, STATE), F32)] * 2 + [thin] * 2 + [((8, heads), F32)],
        [x, g, dy, skip] + keys + [ua, xb, al, be, wide],
        [pltpu.VMEM((rows, cols), F32)] * 2 + [pltpu.VMEM((8, cols), F32)],
        us=6.0,
    )
    state, adjoint, grad_step, sums = call(
        kernel_steps,
        [((STATE, cols), BF16)] * 2 + [thin, ((8, heads), F32)],
        [got_a, got_b, got_c, got_d] + keys
        + [ua, xb, p, q, small, raw, bias, rate, skips],
    )
    sums = all_sum(all_sum(sums, "context"), "dp")
    grad_in, grad_gate, keep_w, keep_r, send = call(
        kernel_last,
        [big, big, ((rows, half), F32), ((rows, half), F32), ((rows, 2 * half), BF16)],
        [state, adjoint] + keys + [ua, xb, wide, gate, gate_f, inp, inp_f, dr, dw],
    )
    got = swap(send).astype(F32)
    return (
        grad_in[None],
        grad_gate[None],
        (keep_w + got[:, :half])[None],
        (keep_r + got[:, half:])[None],
        grad_step[None],
        sums[0],
        sums[1],
        sums[2],
    )


def solution(mesh):
    wide = P("dp", "context", "tensor")
    head = P("tensor")
    return jax.shard_map(
        body,
        mesh=mesh,
        in_specs=(wide,) * 5 + (head,) * 3 + (wide,),
        out_specs=(wide,) * 5 + (head,) * 3,
        check_vma=False,
    )
```

time: 147 us -> 50.1 us (0.34)
  the two profiles are of different devices: /device:TPU:224 before, /device:TPU:1 now
where the time goes in v1:
time: 50.1 us; the launch traced here: 49.8 us
  starting transfers between devices  18.7 us (37%)
  waiting for transfers between devices  11.8 us (24%)
  Pallas kernels  10.3 us (21%)
  local copies, waits for them, and re-layouts  8.17 us (16%)
  between operations  0.72 us (1%)
    ppermute x10, starting transfers between devices, cycle(): lax.ppermute(array, axis, [(i, (i + by) % count) for i in range(count)])  10.9 us
    ppermute x10, waiting for transfers between devices, cycle(): lax.ppermute(array, axis, [(i, (i + by) % count) for i in range(count)])  10.3 us
    pallas_call x4, Pallas kernels, call(): pl.pallas_call(kernel, out_shape=shapes, in_specs=[pl.BlockSpec(memory_sp...  10.3 us
    ppermute x3, starting transfers between devices, swap(): return lax.ppermute(array, 'tensor', [(i, i ^ 1) for i in range(count)])  7.79 us
    unnamed x22, local copies, waits for them, and re-layouts  7.65 us
    ppermute x3, waiting for transfers between devices, swap(): return lax.ppermute(array, 'tensor', [(i, i ^ 1) for i in range(count)])  1.48 us
  transfers between devices with their start and end apart: 13, of which 6 were waited for; matrix products, arithmetic and copies ran while one was open for 3% of the time, Pallas kernels for 13%

profile of v1, /device:TPU:1, one launch (start us, length us, event | category | flops | bytes accessed | tf_op | source)
XLA Modules:
  0.0 49.8 jit_solution(11105229659433137220)
XLA Ops:
  0.6 0.0 copy-start.6
  0.6 0.9 %copy.19 = bf16[1,256,64]{2,1,0:T(8,128)(2,1)S(1)} copy(bf16[1,256,64]{1,2,0:T(8,128)(2,1)} %param.13) | data formatting | bytes 65536 | tf_op args[4]
  1.5 0.0 copy-start.7
  1.5 3.3 %collective-permute-start.1 = (bf16[256,64]{1,0:T(8,128)(2,1)S(1)}, bf16[256,64]{1,0:T(8,128)(2,1)S(1)}, u32[]{:S(2)}, u32[]{:S(2)}) collective-permute-start(bf16[256,64]{1,0:T(8,128)(2,1)S(1)} %bitcast.25), channel_id=1, source_target_pairs={{0,1},{1,0},{2,3},{3,2},{4,5},{5,4},{6,7},{7,6},{8,9},{9,8},{10,11... | collective-permute-start | bytes 98312 | tf_op jit(solution)/shard_map/ppermute | solution.py:334
  4.9 0.0 copy-done.6
  4.9 0.1 copy.18
  5.0 0.1 collective-permute-start
  5.1 0.0 copy-done.7
  5.1 0.1 copy.17
  5.2 0.6 %collective-permute-done.1.rt_ref = bf16[256,64]{1,0:T(8,128)(2,1)S(1)} collective-permute-done((bf16[256,64]{1,0:T(8,128)(2,1)S(1)}, bf16[256,64]{1,0:T(8,128)(2,1)S(1)}, u32[]{:S(2)}, u32[]{:S(2)}) %collective-permute-start.1) | collective-permute-done | bytes 32800 | tf_op jit(solution)/shard_map/ppermute | solution.py:334
  5.8 0.6 %collective-permute-done.wt_ref = bf16[256,64]{1,0:T(8,128)(2,1)S(1)} collective-permute-done((bf16[256,64]{1,0:T(8,128)(2,1)S(1)}, bf16[256,64]{1,0:T(8,128)(2,1)S(1)}, u32[]{:S(2)}, u32[]{:S(2)}) %collective-permute-start) | collective-permute-done | bytes 32800 | tf_op jit(solution)/shard_map/ppermute | solution.py:334
  6.3 0.7 %copy-done.4 = f32[16]{0:T(128)S(1)} copy-done((f32[16]{0:T(128)S(1)}, f32[16]{0:T(128)}, u32[]{:S(2)}) %copy-start.4) | copy-done | bytes 88
  7.0 0.0 copy-done.5
  7.0 1.0 %copy-done = bf16[1,256,1024]{2,1,0:T(8,128)(2,1)S(1)} copy-done((bf16[1,256,1024]{2,1,0:T(8,128)(2,1)S(1)}, bf16[1,256,1024]{2,1,0:T(8,128)(2,1)}, u32[]{:S(2)}) %copy-start) | copy-done | bytes 524312
  8.0 1.0 %copy-done.1 = bf16[1,256,1024]{2,1,0:T(8,128)(2,1)S(1)} copy-done((bf16[1,256,1024]{2,1,0:T(8,128)(2,1)S(1)}, bf16[1,256,1024]{2,1,0:T(8,128)(2,1)}, u32[]{:S(2)}) %copy-start.1) | copy-done | bytes 524312
  9.1 1.0 %copy-done.2 = bf16[1,256,1024]{2,1,0:T(8,128)(2,1)S(1)} copy-done((bf16[1,256,1024]{2,1,0:T(8,128)(2,1)S(1)}, bf16[1,256,1024]{2,1,0:T(8,128)(2,1)}, u32[]{:S(2)}) %copy-start.2) | copy-done | bytes 524312
  10.1 1.4 %shard_map.152 = (bf16[1040,128]{1,0:T(8,128)(2,1)S(1)}, bf16[1040,128]{1,0:T(8,128)(2,1)S(1)}, bf16[256,1024]{1,0:T(8,128)(2,1)S(1)}, bf16[256,1024]{1,0:T(8,12...) custom-call(bf16[256,1024]{1,0:T(8,128)(2,1)S(1)} %bitcast.35, ...), custom_call_target="tpu_custom_call" | custom-call | flops 3000000000 | bytes 3000000 | tf_op jit(solution)/shard_map/pallas_call | solution.py:314
  11.6 0.1 collective-permute-start.2
  11.7 2.7 %collective-permute-start.3 = (bf16[1040,128]{1,0:T(8,128)(2,1)S(1)}, bf16[1040,128]{1,0:T(8,128)(2,1)S(1)}, u32[]{:S(2)}, u32[]{:S(2)}) collective-permute-start(bf16[1040,128]{1,0:T(8,128)(2,1)S(1)} %get-tuple-element.35), channel_id=1, source_target_pairs={{0,48},{16,0},{32,16},{48,32},{1,49},{17,1},{33,17},{49,33},{2,50}... | collective-permute-start | bytes 798728 | tf_op jit(solution)/shard_map/ppermute | solution.py:329
  14.3 6.4 %collective-permute-done.2.a_ref = bf16[1040,128]{1,0:T(8,128)(2,1)S(1)} collective-permute-done((bf16[1040,128]{1,0:T(8,128)(2,1)S(1)}, bf16[1040,128]{1,0:T(8,128)(2,1)S(1)}, u32[]{:S(2)}, u32[]{:S(2)}) %collective-permute-start.2) | collective-permute-done | bytes 266272 | tf_op jit(solution)/shard_map/ppermute | solution.py:329
  20.7 0.0 collective-permute-start.4
  20.7 0.0 collective-permute-done.3.b_ref
  20.7 2.7 %collective-permute-start.5 = (bf16[1040,128]{1,0:T(8,128)(2,1)S(1)}, bf16[1040,128]{1,0:T(8,128)(2,1)S(1)}, u32[]{:S(2)}, u32[]{:S(2)}) collective-permute-start(bf16[1040,128]{1,0:T(8,128)(2,1)S(1)} %collective-permute-done.3.b_ref), channel_id=1, source_target_pairs={{0,48},{16,0},{32,16},{48,32},{1,49},{17,1},{33,17},{49,33},{2,50}... | collective-permute-start | bytes 798728 | tf_op jit(solution)/shard_map/ppermute | solution.py:329
  23.4 0.7 %copy-done.3 = f32[16]{0:T(128)S(1)} copy-done((f32[16]{0:T(128)S(1)}, f32[16]{0:T(128)}, u32[]{:S(2)}) %copy-start.3) | copy-done | bytes 88
  24.0 4.0 %shard_map.153 = (bf16[256,1024]{1,0:T(8,128)(2,1)S(1)}, bf16[256,1024]{1,0:T(8,128)(2,1)S(1)}, bf16[256,1024]{1,0:T(8,128)(2,1)S(1)}, bf16[256,1024]{1,0:T(8,12...) custom-call(bf16[256,1024]{1,0:T(8,128)(2,1)S(1)} %bitcast.36, ...), custom_call_target="tpu_custom_call" | custom-call | flops 6000000000 | bytes 6000000 | tf_op jit(solution)/shard_map/pallas_call | solution.py:314
  28.0 0.8 %collective-permute-done.4.c_ref = bf16[1040,128]{1,0:T(8,128)(2,1)S(1)} collective-permute-done((bf16[1040,128]{1,0:T(8,128)(2,1)S(1)}, bf16[1040,128]{1,0:T(8,128)(2,1)S(1)}, u32[]{:S(2)}, u32[]{:S(2)}) %collective-permute-start.4) | collective-permute-done | bytes 266272 | tf_op jit(solution)/shard_map/ppermute | solution.py:329
  28.8 0.0 collective-permute-done.5.d_ref
  28.8 2.5 %shard_map.154 = (bf16[128,1024]{1,0:T(8,128)(2,1)S(1)}, bf16[128,1024]{1,0:T(8,128)(2,1)S(1)}, f32[256,16]{1,0:T(8,128)S(1)}, f32[8,16]{1,0:T(8,128)S(1)}) custom-call(bf16[1040,128]{1,0:T(8,128)(2,1)S(1)} %collective-permute-done.2.a_ref, bf16[1040,128]{1,0:T(8,128)(2,1)S(1)} %collective-permute-done.3.b_ref, ...), custom_call_target="tpu_custom_call" | custom-call | flops 3000000000 | bytes 3000000 | tf_op jit(solution)/shard_map/pallas_call | solution.py:314
  31.3 2.5 %collective-permute-start.9 = (f32[8,16]{1,0:T(8,128)S(1)}, f32[8,16]{1,0:T(8,128)S(1)}, u32[]{:S(2)}, u32[]{:S(2)}) collective-permute-start(f32[8,16]{1,0:T(8,128)S(1)} %get-tuple-element.59), channel_id=1, source_target_pairs={{0,48},{16,0},{32,16},{48,32},{1,49},{17,1},{33,17},{49,33},{2,50}... | collective-permute-start | bytes 1544 | tf_op jit(solution)/shard_map/ppermute | solution.py:329
  33.8 0.0 collective-permute-start.8
  33.8 0.9 %collective-permute-start.7 = (f32[8,16]{1,0:T(8,128)S(1)}, f32[8,16]{1,0:T(8,128)S(1)}, u32[]{:S(2)}, u32[]{:S(2)}) collective-permute-start(f32[8,16]{1,0:T(8,128)S(1)} %get-tuple-element.59), channel_id=1, source_target_pairs={{0,16},{16,32},{32,48},{48,0},{1,17},{17,33},{33,49},{49,1},{2,18}... | collective-permute-start | bytes 1544 | tf_op jit(solution)/shard_map/ppermute | solution.py:329
  34.7 0.0 collective-permute-done.9
  34.7 3.1 %collective-permute-done.8 = f32[8,16]{1,0:T(8,128)S(1)} collective-permute-done((f32[8,16]{1,0:T(8,128)S(1)}, f32[8,16]{1,0:T(8,128)S(1)}, u32[]{:S(2)}, u32[]{:S(2)}) %collective-permute-start.8) | collective-permute-done | bytes 544 | tf_op jit(solution)/shard_map/ppermute | solution.py:329
  37.8 0.0 collective-permute-done.7
  37.8 1.0 %collective-permute-start.12 = (f32[8,16]{1,0:T(8,128)S(1)}, f32[8,16]{1,0:T(8,128)S(1)}, u32[]{:S(2)}, u32[]{:S(2)}) collective-permute-start(f32[8,16]{1,0:T(8,128)S(1)} %add_add_fusion.1), channel_id=1, source_target_pairs={{0,192},{64,0},{128,64},{192,128},{1,193},{65,1},{129,65},{193,129... | collective-permute-start | bytes 1544 | tf_op jit(solution)/shard_map/ppermute | solution.py:329
  38.8 0.5 %collective-permute-start.11 = (f32[8,16]{1,0:T(8,128)S(1)}, f32[8,16]{1,0:T(8,128)S(1)}, u32[]{:S(2)}, u32[]{:S(2)}) collective-permute-start(f32[8,16]{1,0:T(8,128)S(1)} %add_add_fusion.1), channel_id=1, source_target_pairs={{0,128},{64,192},{128,0},{192,64},{1,129},{65,193},{129,1},{193,65... | collective-permute-start | bytes 1544 | tf_op jit(solution)/shard_map/ppermute | solution.py:329
  39.4 0.6 %collective-permute-start.10 = (f32[8,16]{1,0:T(8,128)S(1)}, f32[8,16]{1,0:T(8,128)S(1)}, u32[]{:S(2)}, u32[]{:S(2)}) collective-permute-start(f32[8,16]{1,0:T(8,128)S(1)} %add_add_fusion.1), channel_id=1, source_target_pairs={{0,64},{64,128},{128,192},{192,0},{1,65},{65,129},{129,193},{193,1... | collective-permute-start | bytes 1544 | tf_op jit(solution)/shard_map/ppermute | solution.py:329
  40.0 2.4 %shard_map.155 = (bf16[256,1024]{1,0:T(8,128)(2,1)}, bf16[256,1024]{1,0:T(8,128)(2,1)}, f32[256,64]{1,0:T(8,128)S(1)}, f32[256,64]{1,0:T(8,128)S(1)}, bf16[256,128]{1,0:T(8,128)(2,1)S(1)}) custom-call(bf16[128,1024]{1,0:T(8,128)(2,1)S(1)} %get-tuple-element.45.state_ref, bf16[128,1024]{1,0:T(8,128)(2,1)S(1)} %get-tuple-element.46.adjoint_ref, ...), custom_call_target="tpu_custom_call" | custom-call | flops 3000000000 | bytes 3000000 | tf_op jit(solution)/shard_map/pallas_call | solution.py:314
  42.3 0.7 %copy.22 = f32[1,256,16]{1,2,0:T(8,128)} copy(f32[1,256,16]{2,1,0:T(8,128)S(1)} %bitcast.22) | data formatting | bytes 32768
  43.0 4.4 %collective-permute-start.6 = (bf16[256,128]{1,0:T(8,128)(2,1)S(1)}, bf16[256,128]{1,0:T(8,128)(2,1)S(1)}, u32[]{:S(2)}, u32[]{:S(2)}) collective-permute-start(bf16[256,128]{1,0:T(8,128)(2,1)S(1)} %get-tuple-element.56), channel_id=1, source_target_pairs={{0,1},{1,0},{2,3},{3,2},{4,5},{5,4},{6,7},{7,6},{8,9},{9,8},{10,11... | collective-permute-start | bytes 196616 | tf_op jit(solution)/shard_map/ppermute | solution.py:334
  47.3 0.0 collective-permute-done.12
  47.4 0.0 collective-permute-done.11
  47.4 0.0 collective-permute-done.10
  47.4 0.5 %slice_bitcast_fusion = (f32[16]{0:T(128)}, f32[16]{0:T(128)}, f32[16]{0:T(128)}) fusion(f32[8,16]{1,0:T(8,128)S(1)} %add_add_fusion), kind=kLoop, calls=%fused_computation.6 | loop fusion | bytes 384 | tf_op jit(solution)/shard_map/squeeze | solution.py:403
  47.9 0.4 collective-permute-done.6
  48.3 0.1 fusion
  48.4 0.7 %copy.21 = f32[1,256,64]{1,2,0:T(8,128)} copy(f32[1,256,64]{2,1,0:T(8,128)S(1)} %get-tuple-element.68) | data formatting | bytes 131072
  49.1 0.7 %copy.20 = f32[1,256,64]{1,2,0:T(8,128)} copy(f32[1,256,64]{2,1,0:T(8,128)S(1)} %get-tuple-element.69) | data formatting | bytes 131072
  (9 shorter events, 0.0 us)
Async XLA Ops:
  0.6 4.2 %copy-start.6 = (bf16[1,256,64]{1,2,0:T(8,128)(2,1)S(1)}, bf16[1,256,64]{1,2,0:T(8,128)(2,1)}, u32[]{:S(2)}) copy-start(bf16[1,256,64]{1,2,0:T(8,128)(2,1)} %param.12) | copy-start | bytes 98308
  1.5 3.6 %copy-start.7 = (f32[1,256,16]{1,2,0:T(8,128)S(1)}, f32[1,256,16]{1,2,0:T(8,128)}, u32[]{:S(2)}) copy-start(f32[1,256,16]{1,2,0:T(8,128)} %param.11) | copy-start | bytes 49156
  1.5 4.2 %collective-permute-start.1 = (bf16[256,64]{1,0:T(8,128)(2,1)S(1)}, bf16[256,64]{1,0:T(8,128)(2,1)S(1)}, u32[]{:S(2)}, u32[]{:S(2)}) collective-permute-start(bf16[256,64]{1,0:T(8,128)(2,1)S(1)} %bitcast.25), channel_id=1, source_target_pairs={{0,1},{1,0},{2,3},{3,2},{4,5},{5,4},{6,7},{7,6},{8,9},{9,8},{10,11... | collective-permute-start | bytes 98312 | tf_op jit(solution)/shard_map/ppermute | solution.py:334
  5.0 1.3 %collective-permute-start = (bf16[256,64]{1,0:T(8,128)(2,1)S(1)}, bf16[256,64]{1,0:T(8,128)(2,1)S(1)}, u32[]{:S(2)}, u32[]{:S(2)}) collective-permute-start(bf16[256,64]{1,0:T(8,128)(2,1)S(1)} %bitcast.30), channel_id=1, source_target_pairs={{0,1},{1,0},{2,3},{3,2},{4,5},{5,4},{6,7},{7,6},{8,9},{9,8},{10,11... | collective-permute-start | bytes 98312 | tf_op jit(solution)/shard_map/ppermute | solution.py:334
  6.3 0.7 %copy-start.4 = (f32[16]{0:T(128)S(1)}, f32[16]{0:T(128)}, u32[]{:S(2)}) copy-start(f32[16]{0:T(128)} %param.16) | copy-start | bytes 196
  6.3 0.7 %copy-start.5 = (f32[16]{0:T(128)S(1)}, f32[16]{0:T(128)}, u32[]{:S(2)}) copy-start(f32[16]{0:T(128)} %param.14) | copy-start | bytes 196
  7.0 1.0 %copy-start = (bf16[1,256,1024]{2,1,0:T(8,128)(2,1)S(1)}, bf16[1,256,1024]{2,1,0:T(8,128)(2,1)}, u32[]{:S(2)}) copy-start(bf16[1,256,1024]{2,1,0:T(8,128)(2,1)} %param.9) | copy-start | bytes 1572868
  8.0 1.0 %copy-start.1 = (bf16[1,256,1024]{2,1,0:T(8,128)(2,1)S(1)}, bf16[1,256,1024]{2,1,0:T(8,128)(2,1)}, u32[]{:S(2)}) copy-start(bf16[1,256,1024]{2,1,0:T(8,128)(2,1)} %param.10) | copy-start | bytes 1572868
  9.1 1.0 %copy-start.2 = (bf16[1,256,1024]{2,1,0:T(8,128)(2,1)S(1)}, bf16[1,256,1024]{2,1,0:T(8,128)(2,1)}, u32[]{:S(2)}) copy-start(bf16[1,256,1024]{2,1,0:T(8,128)(2,1)} %param.17) | copy-start | bytes 1572868
  11.6 9.1 %collective-permute-start.2 = (bf16[1040,128]{1,0:T(8,128)(2,1)S(1)}, bf16[1040,128]{1,0:T(8,128)(2,1)S(1)}, u32[]{:S(2)}, u32[]{:S(2)}) collective-permute-start(bf16[1040,128]{1,0:T(8,128)(2,1)S(1)} %get-tuple-element.34), channel_id=1, source_target_pairs={{0,16},{16,32},{32,48},{48,0},{1,17},{17,33},{33,49},{49,1},{2,18}... | collective-permute-start | bytes 798728 | tf_op jit(solution)/shard_map/ppermute | solution.py:329
  11.7 9.0 %collective-permute-start.3 = (bf16[1040,128]{1,0:T(8,128)(2,1)S(1)}, bf16[1040,128]{1,0:T(8,128)(2,1)S(1)}, u32[]{:S(2)}, u32[]{:S(2)}) collective-permute-start(bf16[1040,128]{1,0:T(8,128)(2,1)S(1)} %get-tuple-element.35), channel_id=1, source_target_pairs={{0,48},{16,0},{32,16},{48,32},{1,49},{17,1},{33,17},{49,33},{2,50}... | collective-permute-start | bytes 798728 | tf_op jit(solution)/shard_map/ppermute | solution.py:329
  20.7 8.1 %collective-permute-start.4 = (bf16[1040,128]{1,0:T(8,128)(2,1)S(1)}, bf16[1040,128]{1,0:T(8,128)(2,1)S(1)}, u32[]{:S(2)}, u32[]{:S(2)}) collective-permute-start(bf16[1040,128]{1,0:T(8,128)(2,1)S(1)} %collective-permute-done.2.a_ref), channel_id=1, source_target_pairs={{0,16},{16,32},{32,48},{48,0},{1,17},{17,33},{33,49},{49,1},{2,18}... | collective-permute-start | bytes 798728 | tf_op jit(solution)/shard_map/ppermute | solution.py:329
  20.7 8.1 %collective-permute-start.5 = (bf16[1040,128]{1,0:T(8,128)(2,1)S(1)}, bf16[1040,128]{1,0:T(8,128)(2,1)S(1)}, u32[]{:S(2)}, u32[]{:S(2)}) collective-permute-start(bf16[1040,128]{1,0:T(8,128)(2,1)S(1)} %collective-permute-done.3.b_ref), channel_id=1, source_target_pairs={{0,48},{16,0},{32,16},{48,32},{1,49},{17,1},{33,17},{49,33},{2,50}... | collective-permute-start | bytes 798728 | tf_op jit(solution)/shard_map/ppermute | solution.py:329
  23.4 0.7 %copy-start.3 = (f32[16]{0:T(128)S(1)}, f32[16]{0:T(128)}, u32[]{:S(2)}) copy-start(f32[16]{0:T(128)} %param.15) | copy-start | bytes 196
  31.3 3.3 %collective-permute-start.9 = (f32[8,16]{1,0:T(8,128)S(1)}, f32[8,16]{1,0:T(8,128)S(1)}, u32[]{:S(2)}, u32[]{:S(2)}) collective-permute-start(f32[8,16]{1,0:T(8,128)S(1)} %get-tuple-element.59), channel_id=1, source_target_pairs={{0,48},{16,0},{32,16},{48,32},{1,49},{17,1},{33,17},{49,33},{2,50}... | collective-permute-start | bytes 1544 | tf_op jit(solution)/shard_map/ppermute | solution.py:329
  33.8 4.0 %collective-permute-start.8 = (f32[8,16]{1,0:T(8,128)S(1)}, f32[8,16]{1,0:T(8,128)S(1)}, u32[]{:S(2)}, u32[]{:S(2)}) collective-permute-start(f32[8,16]{1,0:T(8,128)S(1)} %get-tuple-element.59), channel_id=1, source_target_pairs={{0,32},{16,48},{32,0},{48,16},{1,33},{17,49},{33,1},{49,17},{2,34}... | collective-permute-start | bytes 1544 | tf_op jit(solution)/shard_map/ppermute | solution.py:329
  33.8 4.0 %collective-permute-start.7 = (f32[8,16]{1,0:T(8,128)S(1)}, f32[8,16]{1,0:T(8,128)S(1)}, u32[]{:S(2)}, u32[]{:S(2)}) collective-permute-start(f32[8,16]{1,0:T(8,128)S(1)} %get-tuple-element.59), channel_id=1, source_target_pairs={{0,16},{16,32},{32,48},{48,0},{1,17},{17,33},{33,49},{49,1},{2,18}... | collective-permute-start | bytes 1544 | tf_op jit(solution)/shard_map/ppermute | solution.py:329
  37.8 9.6 %collective-permute-start.12 = (f32[8,16]{1,0:T(8,128)S(1)}, f32[8,16]{1,0:T(8,128)S(1)}, u32[]{:S(2)}, u32[]{:S(2)}) collective-permute-start(f32[8,16]{1,0:T(8,128)S(1)} %add_add_fusion.1), channel_id=1, source_target_pairs={{0,192},{64,0},{128,64},{192,128},{1,193},{65,1},{129,65},{193,129... | collective-permute-start | bytes 1544 | tf_op jit(solution)/shard_map/ppermute | solution.py:329
  38.8 8.5 %collective-permute-start.11 = (f32[8,16]{1,0:T(8,128)S(1)}, f32[8,16]{1,0:T(8,128)S(1)}, u32[]{:S(2)}, u32[]{:S(2)}) collective-permute-start(f32[8,16]{1,0:T(8,128)S(1)} %add_add_fusion.1), channel_id=1, source_target_pairs={{0,128},{64,192},{128,0},{192,64},{1,129},{65,193},{129,1},{193,65... | collective-permute-start | bytes 1544 | tf_op jit(solution)/shard_map/ppermute | solution.py:329
  39.4 8.0 %collective-permute-start.10 = (f32[8,16]{1,0:T(8,128)S(1)}, f32[8,16]{1,0:T(8,128)S(1)}, u32[]{:S(2)}, u32[]{:S(2)}) collective-permute-start(f32[8,16]{1,0:T(8,128)S(1)} %add_add_fusion.1), channel_id=1, source_target_pairs={{0,64},{64,128},{128,192},{192,0},{1,65},{65,129},{129,193},{193,1... | collective-permute-start | bytes 1544 | tf_op jit(solution)/shard_map/ppermute | solution.py:329
  43.0 5.3 %collective-permute-start.6 = (bf16[256,128]{1,0:T(8,128)(2,1)S(1)}, bf16[256,128]{1,0:T(8,128)(2,1)S(1)}, u32[]{:S(2)}, u32[]{:S(2)}) collective-permute-start(bf16[256,128]{1,0:T(8,128)(2,1)S(1)} %get-tuple-element.56), channel_id=1, source_target_pairs={{0,1},{1,0},{2,3},{3,2},{4,5},{5,4},{6,7},{7,6},{8,9},{9,8},{10,11... | collective-permute-start | bytes 196616 | tf_op jit(solution)/shard_map/ppermute | solution.py:334

commit v2 on v1

v2 whole, which is shorter than its diff:
```python
import functools
import math

import jax
import jax.numpy as jnp
from jax import lax
from jax.experimental import pallas as pl
from jax.experimental.pallas import tpu as pltpu
from jax.sharding import PartitionSpec as P

HEAD_DIM = 64
STATE = 128
BLOCK = 128
LOG2E = math.log2(math.e)
F32 = jnp.float32
BF16 = jnp.bfloat16
TILE = 256


def dot(a, b, dims=((1,), (0,))):
    return lax.dot_general(a, b, (dims, ((), ())), preferred_element_type=F32)


def pieces(v, count):
    out = []
    for _ in range(count):
        part = v.astype(BF16)
        out.append(part)
        v = v - part.astype(F32)
    return out


def split_dot_left(exact, v, count):
    return sum(dot(exact, part) for part in pieces(v, count))


def split_dot_right(v, exact, count):
    return sum(dot(part, exact) for part in pieces(v, count))


def expander(heads, lo, size):
    head = lax.broadcasted_iota(jnp.int32, (heads, size), 0)
    column = lax.broadcasted_iota(jnp.int32, (heads, size), 1) + lo
    return ((column >= head * HEAD_DIM) & (column < (head + 1) * HEAD_DIM)).astype(BF16)


def selector(heads, lo, size):
    head = lax.broadcasted_iota(jnp.int32, (size, heads), 1)
    column = lax.broadcasted_iota(jnp.int32, (size, heads), 0) + lo
    return ((column >= head * HEAD_DIM) & (column < (head + 1) * HEAD_DIM)).astype(BF16)


def triangle(rows, lower):
    i = lax.broadcasted_iota(jnp.int32, (rows, rows), 0)
    j = lax.broadcasted_iota(jnp.int32, (rows, rows), 1)
    return ((i >= j) if lower else (i <= j)).astype(BF16)


def softplus(z):
    return jnp.maximum(z, 0.0) + jnp.log(1.0 + jnp.exp(-jnp.abs(z)))


def at_block(b):
    return pl.ds(b * BLOCK, BLOCK)


def kernel_scale(
    x_in, g_in, dy_in, raw_in, bias_in, rate_in, skip_in, w_in, r_in,
    x_ref, g_ref, dy_ref, w_ref, r_ref, skip_ref, qq_ref, z_ref, rate_ref, al_ref, be_ref,
    wide_ref, small_ref,
    raw_ref, bias_ref, al_e, be_e, sems,
):
    rows, cols = x_ref.shape
    heads = raw_ref.shape[0]
    blocks = rows // BLOCK
    thin = [
        (raw_in, raw_ref), (bias_in, bias_ref), (rate_in, rate_ref),
        (skip_in, skip_ref), (w_in, w_ref), (r_in, r_ref),
    ]
    copies = [pltpu.make_async_copy(s, d, sems.at[i]) for i, (s, d) in enumerate(thin)]
    large = []
    for b in range(blocks):
        large.append([
            pltpu.make_async_copy(s.at[at_block(b)], d.at[at_block(b)], sems.at[6 + 3 * b + i])
            for i, (s, d) in enumerate([(g_in, g_ref), (dy_in, dy_ref), (x_in, x_ref)])
        ])
    for copy in copies[:3] + large[0] + large[1] + copies[3:]:
        copy.start()
    for copy in copies[:3]:
        copy.wait()
    z = raw_ref[...].T + bias_ref[...]
    z_ref[...] = z
    step = softplus(z)
    log2_decay = step * (-LOG2E * jnp.exp(rate_ref[...]))
    run = split_dot_left(triangle(rows, True), log2_decay, 3)
    mid0 = run[BLOCK // 2 - 1 : BLOCK // 2]
    mid1 = run[BLOCK + BLOCK // 2 - 1 : BLOCK + BLOCK // 2]
    end = run[rows - 1 : rows]
    row = lax.broadcasted_iota(jnp.int32, (rows, heads), 0)
    rel = run - jnp.where(row < BLOCK, mid0, mid1)
    al = jnp.exp2(rel)
    be = jnp.exp2(-rel) * step
    al_ref[...] = al
    be_ref[...] = be
    small = jnp.exp2(
        jnp.concatenate([mid0, mid1, end - mid0, end - mid1, mid1 - mid0, end, end, end], axis=0)
    )
    small_ref[...] = small
    for lo in range(0, cols, TILE):
        wide = expander(heads, lo, TILE)
        here = pl.ds(lo, TILE)
        al_e[:, here] = split_dot_right(al, wide, 2)
        be_e[:, here] = split_dot_right(be, wide, 2)
        wide_ref[:, here] = split_dot_right(small, wide, 3)
    for b in range(blocks):
        for copy in large[b]:
            copy.wait()
        at = at_block(b)
        for lo in range(0, cols, BLOCK):
            here = pl.ds(lo, BLOCK)
            g = g_ref[at, here].astype(F32)
            u = dy_ref[at, here].astype(F32) * g / (1.0 + jnp.exp(-g))
            qq_ref[1, at, here] = (u * al_e[at, here]).astype(BF16)
            qq_ref[0, at, here] = (x_ref[at, here].astype(F32) * be_e[at, here]).astype(BF16)
    for copy in copies[3:]:
        copy.wait()


def kernel_states(
    w_ref, wt_ref, r_ref, rt_ref, qq_ref, wide_ref, small_ref, turned_ref, e_ref, f_ref
):
    cols = qq_ref.shape[2]
    blocks = qq_ref.shape[1] // BLOCK
    place = lax.axis_index("context")
    writes = jnp.concatenate([w_ref[...], wt_ref[...]], axis=0)
    reads = jnp.concatenate([r_ref[...], rt_ref[...]], axis=0)
    turned_ref[0] = writes
    turned_ref[1] = reads
    for lo in range(0, cols, BLOCK):
        here = pl.ds(lo, BLOCK)
        state = jnp.zeros((STATE, BLOCK), F32)
        adjoint = state
        for b in range(blocks):
            at = at_block(b)
            part = slice(b * BLOCK, (b + 1) * BLOCK)
            state += dot(writes[:, part], qq_ref[0, at, here]) * wide_ref[2 + b : 3 + b, here]
            adjoint += dot(reads[:, part], qq_ref[1, at, here]) * wide_ref[b : b + 1, here]
        e_ref[here, :] = jnp.where(place < 2, state, adjoint).astype(BF16)
        f_ref[here, :] = jnp.where(lax.rem(place, 2) == 0, state, adjoint).astype(BF16)
    heads = small_ref.shape[1]
    total = jnp.concatenate(
        [small_ref[5:6], jnp.zeros((1, STATE - heads), F32)], axis=1
    )
    parts = [part.astype(F32) for part in pieces(total, 3)]
    totals = jnp.concatenate(parts + [jnp.zeros((13, STATE), F32)], axis=0).astype(BF16)
    e_ref[pl.ds(cols, 16), :] = totals
    f_ref[pl.ds(cols, 16), :] = totals


def kernel_within(
    x_ref, g_ref, dy_ref, skip_ref, turned_ref, qq_ref, al_ref, be_ref, wide_ref,
    gate_ref, gate_f_ref, in_ref, in_f_ref, dr_ref, dw_ref, keys_ref, p_ref, q_ref, skip_out_ref,
    al_e, be_e, skip_e,
):
    rows, cols = x_ref.shape
    heads = skip_ref.shape[1]
    for lo in range(0, cols, TILE):
        wide = expander(heads, lo, TILE)
        here = pl.ds(lo, TILE)
        al_e[:, here] = split_dot_right(al_ref[...], wide, 2)
        be_e[:, here] = split_dot_right(be_ref[...], wide, 2)
        skip_e[:, here] = split_dot_right(jnp.broadcast_to(skip_ref[...], (8, heads)), wide, 3)
    nt = ((1,), (1,))
    wt = [turned_ref[0, :, at_block(b)] for b in range(2)]
    rt = [turned_ref[1, :, at_block(b)] for b in range(2)]
    w = [v.astype(F32).T.astype(BF16) for v in wt]
    r = [v.astype(F32).T.astype(BF16) for v in rt]
    for b in range(2):
        keys_ref[0, at_block(b), :] = w[b]
        keys_ref[1, at_block(b), :] = r[b]
    i = lax.broadcasted_iota(jnp.int32, (BLOCK, BLOCK), 0)
    j = lax.broadcasted_iota(jnp.int32, (BLOCK, BLOCK), 1)
    i00 = jnp.where(i >= j, dot(r[0], wt[0]), 0.0).astype(BF16)
    i11 = jnp.where(i >= j, dot(r[1], wt[1]), 0.0).astype(BF16)
    i10 = dot(r[1], wt[0]).astype(BF16)
    t00 = jnp.where(i <= j, dot(w[0], rt[0]), 0.0).astype(BF16)
    t11 = jnp.where(i <= j, dot(w[1], rt[1]), 0.0).astype(BF16)
    t10 = dot(w[0], rt[1]).astype(BF16)
    m00 = jnp.zeros((BLOCK, BLOCK), F32)
    m11 = m00
    m10 = m00
    p = [jnp.zeros((BLOCK, heads), F32)] * 2
    q = [jnp.zeros((BLOCK, heads), F32)] * 2
    skips = jnp.zeros((8, heads), F32)
    for lo in range(0, cols, BLOCK):
        here = pl.ds(lo, BLOCK)
        sel = selector(heads, lo, BLOCK)
        link = wide_ref[4:5, here]
        xb = [qq_ref[0, at_block(b), here] for b in range(2)]
        ua = [qq_ref[1, at_block(b), here] for b in range(2)]
        m00 += dot(ua[0], xb[0], nt)
        m11 += dot(ua[1], xb[1], nt)
        m10 += dot(ua[1], (xb[0].astype(F32) * link).astype(BF16), nt)
        v = [dot(i00, xb[0]), dot(i11, xb[1]) + link * dot(i10, xb[0])]
        z = [dot(t00, ua[0]) + link * dot(t10, ua[1]), dot(t11, ua[1])]
        skip = skip_e[0:1, here]
        for b in range(2):
            at = at_block(b)
            p[b] += split_dot_right(ua[b].astype(F32) * v[b], sel, 2)
            q[b] += split_dot_right(xb[b].astype(F32) * z[b], sel, 2)
            g = g_ref[at, here].astype(F32)
            dy = dy_ref[at, here].astype(F32)
            x = x_ref[at, here].astype(F32)
            sig = 1.0 / (1.0 + jnp.exp(-g))
            u = dy * g * sig
            up = dy * sig * (1.0 + g * (1.0 - sig))
            al = al_e[at, here]
            be = be_e[at, here]
            gate_ref[at, here] = (up * (al * v[b] + skip * x)).astype(BF16)
            gate_f_ref[at, here] = (up * al * wide_ref[b : b + 1, here]).astype(BF16)
            in_ref[at, here] = (be * z[b] + skip * u).astype(BF16)
            in_f_ref[at, here] = (be * wide_ref[2 + b : 3 + b, here]).astype(BF16)
            ux = jnp.sum((u * x).reshape(BLOCK // 8, 8, BLOCK), axis=0)
            skips += split_dot_right(ux, sel, 3)
    for b in range(2):
        p_ref[at_block(b), :] = p[b]
        q_ref[at_block(b), :] = q[b]
    skip_out_ref[...] = skips
    m00 = jnp.where(i >= j, m00, 0.0).astype(BF16)
    m11 = jnp.where(i >= j, m11, 0.0).astype(BF16)
    m10 = m10.astype(BF16)
    dr_ref[:, at_block(0)] = dot(wt[0], m00, nt)
    dr_ref[:, at_block(1)] = dot(wt[0], m10, nt) + dot(wt[1], m11, nt)
    dw_ref[:, at_block(0)] = dot(rt[0], m00) + dot(rt[1], m10)
    dw_ref[:, at_block(1)] = dot(rt[1], m11)


def kernel_after(first_ref, token_ref, out_ref):
    del first_ref, token_ref, out_ref


def head_sums(buffer_ref, key, weight_ref, index, heads):
    cols = weight_ref.shape[2]
    out = jnp.zeros((key.shape[0], heads), F32)
    for lo in range(0, cols, BLOCK):
        here = pl.ds(lo, BLOCK)
        product = weight_ref[index, :, here].astype(F32) * dot(key, buffer_ref[here, :])
        out += split_dot_right(product, selector(heads, lo, BLOCK), 2)
    return out


def pair_sums(one_ref, two_ref, cols, heads):
    out = jnp.zeros((8, heads), F32)
    for lo in range(0, cols, BLOCK):
        here = pl.ds(lo, BLOCK)
        product = one_ref[here, :].astype(F32) * two_ref[here, :].astype(F32)
        product = jnp.sum(product.reshape(STATE // 8, 8, BLOCK), axis=0)
        out += split_dot_right(product, selector(heads, lo, BLOCK), 2)
    return out


def kernel_early(e_ref, f_ref, keys_ref, qq_ref, small_ref, pe_ref, pf_ref, cross_ref):
    cols = qq_ref.shape[2]
    heads = small_ref.shape[1]
    place = lax.axis_index("context")
    mine = (place >= 2).astype(jnp.int32)
    side = lax.rem(place, 2)
    pe_ref[...] = head_sums(e_ref, keys_ref[mine], qq_ref, mine, heads)
    pf_ref[...] = head_sums(f_ref, keys_ref[side], qq_ref, side, heads)
    cross_ref[...] = pair_sums(e_ref, f_ref, cols, heads)


def total_of(ref, cols, heads):
    parts = ref[pl.ds(cols, 16), :].astype(F32)
    return (parts[0:1] + parts[1:2] + parts[2:3])[:, :heads]


def kernel_steps(
    h_ref, e_ref, f_ref, keys_ref, qq_ref, pe_ref, pf_ref, cross_ref, p_ref, q_ref,
    small_ref, z_ref, rate_ref, skips_ref,
    step_ref, sums_ref,
):
    rows, cols = qq_ref.shape[1:]
    heads = small_ref.shape[1]
    place = lax.axis_index("context")
    mine = (place >= 2).astype(jnp.int32)
    inner = (place == 1) | (place == 2)
    te, tf, th = (total_of(ref, cols, heads) for ref in (e_ref, f_ref, h_ref))
    ph = head_sums(h_ref, keys_ref[mine], qq_ref, mine, heads)
    cross = cross_ref[...] + te * pair_sums(h_ref, f_ref, cols, heads)
    cross = jnp.where(inner, jnp.sum(cross, axis=0, keepdims=True), 0.0)
    pe = pe_ref[...]
    pf = pf_ref[...]
    px = jnp.where(inner, pe + te * ph, pf + tf * (ph + th * pe))
    py = jnp.where(inner, pf, 0.0)
    row = lax.broadcasted_iota(jnp.int32, (rows, heads), 0)
    p = jnp.where(mine == 1, px, py) * jnp.where(row < BLOCK, small_ref[0:1], small_ref[1:2])
    q = jnp.where(mine == 1, py, px) * jnp.where(row < BLOCK, small_ref[2:3], small_ref[3:4])
    ends = jnp.sum(q, axis=0, keepdims=True) + small_ref[5:6] * cross
    q = q + q_ref[...]
    flow = split_dot_left(triangle(rows, False), p + p_ref[...] - q, 3) + ends
    z = z_ref[...]
    step = softplus(z)
    rate = jnp.exp(rate_ref[...])
    grad = (q / step - rate * flow) / (1.0 + jnp.exp(-z))
    step_ref[...] = grad.T
    sum_rate = jnp.sum(flow * step, axis=0, keepdims=True) * -rate
    sum_bias = jnp.sum(grad, axis=0, keepdims=True)
    sum_skip = jnp.sum(skips_ref[...], axis=0, keepdims=True)
    index = lax.broadcasted_iota(jnp.int32, (8, heads), 0)
    sums_ref[...] = jnp.where(
        index == 0, sum_rate, jnp.where(index == 1, sum_skip, jnp.where(index == 2, sum_bias, 0.0))
    )


def kernel_last(
    e_ref, f_ref, h_ref, keys_ref, qq_ref, wide_ref,
    gate_ref, gate_f_ref, in_ref, in_f_ref, dr_ref, dw_ref, after_ref,
    grad_in_ref, grad_gate_ref, keep_ref, send_ref,
    coef_e,
):
    del after_ref
    rows, cols = qq_ref.shape[1:]
    half = STATE // 2
    heads = cols // HEAD_DIM
    nt = ((1,), (1,))
    place = lax.axis_index("context")
    inner = (place == 1) | (place == 2)
    te, tf, th = (total_of(ref, cols, heads) for ref in (e_ref, f_ref, h_ref))
    coef = jnp.concatenate(
        [jnp.where(inner, 1.0, tf * th), jnp.where(inner, te, tf)] + [jnp.zeros_like(te)] * 6,
        axis=0,
    )
    for lo in range(0, cols, TILE):
        coef_e[:, pl.ds(lo, TILE)] = split_dot_right(coef, expander(heads, lo, TILE), 3)
    dr = [dr_ref[:, at_block(b)] for b in range(2)]
    dw = [dw_ref[:, at_block(b)] for b in range(2)]
    for lo in range(0, cols, BLOCK):
        here = pl.ds(lo, BLOCK)
        got_f = f_ref[here, :].astype(F32)
        x = (
            e_ref[here, :].astype(F32) * coef_e[0:1, here]
            + h_ref[here, :].astype(F32) * coef_e[1:2, here]
            + jnp.where(inner, 0.0, got_f)
        )
        y = jnp.where(inner, got_f, 0.0)
        s = jnp.where(place >= 2, x, y)
        a = jnp.where(place >= 2, y, x)
        s_half = s.astype(BF16)
        a_half = a.astype(BF16)
        for b in range(2):
            at = at_block(b)
            scaled_s = (s * wide_ref[b : b + 1, here]).astype(BF16)
            scaled_a = (a * wide_ref[2 + b : 3 + b, here]).astype(BF16)
            dr[b] += dot(scaled_s, qq_ref[1, at, here], nt)
            dw[b] += dot(scaled_a, qq_ref[0, at, here], nt)
            v = dot(keys_ref[1, at, :], s_half)
            z = dot(keys_ref[0, at, :], a_half)
            grad_gate_ref[at, here] = (
                gate_ref[at, here].astype(F32) + gate_f_ref[at, here].astype(F32) * v
            ).astype(BF16)
            grad_in_ref[at, here] = (
                in_ref[at, here].astype(F32) + in_f_ref[at, here].astype(F32) * z
            ).astype(BF16)
    for b in range(2):
        keep_ref[pl.ds(0, half), at_block(b)] = dw[b][:half]
        keep_ref[pl.ds(half, half), at_block(b)] = dr[b][:half]
        send_ref[pl.ds(0, half), at_block(b)] = dw[b][half:].astype(BF16)
        send_ref[pl.ds(half, half), at_block(b)] = dr[b][half:].astype(BF16)


def kernel_add(a_ref, b_ref, c_ref, d_ref, after_ref, out_ref):
    del after_ref
    out_ref[...] = (a_ref[...] + b_ref[...]) + (c_ref[...] + d_ref[...])


def kernel_finish(
    keep_ref, got_ref, a_ref, b_ref, c_ref, d_ref, w_ref, r_ref, rate_ref, skip_ref, bias_ref
):
    half = w_ref.shape[0]
    w_ref[...] = keep_ref[pl.ds(0, half), :] + got_ref[pl.ds(0, half), :].astype(F32)
    r_ref[...] = keep_ref[pl.ds(half, half), :] + got_ref[pl.ds(half, half), :].astype(F32)
    sums = (a_ref[...] + b_ref[...]) + (c_ref[...] + d_ref[...])
    rate_ref[...] = sums[0:1]
    skip_ref[...] = sums[1:2]
    bias_ref[...] = sums[2:3]


V = pltpu.VMEM
ANY = pl.ANY


def call(kernel, outs, args, scratch=(), us=3.0, spaces=None, out_spaces=None, alias=None):
    spaces = spaces or [V] * len(args)
    out_spaces = out_spaces or [V] * len(outs)
    return pl.pallas_call(
        kernel,
        out_shape=[jax.ShapeDtypeStruct(s, d) for s, d in outs],
        in_specs=[pl.BlockSpec(memory_space=s) for s in spaces],
        out_specs=[pl.BlockSpec(memory_space=s) for s in out_spaces],
        scratch_shapes=list(scratch),
        input_output_aliases=alias or {},
        compiler_params=pltpu.CompilerParams(vmem_limit_bytes=36 * 1024 * 1024),
        cost_estimate=pl.CostEstimate(
            flops=int(us * 1e9), bytes_accessed=int(us * 1e6), transcendentals=0
        ),
    )(*args)


def exchange(array, axis, mask):
    count = lax.axis_size(axis)
    pairs = [(i, i ^ mask) for i in range(count) if i ^ mask < count]
    return lax.ppermute(array, axis, pairs)


def body(
    head_inputs,
    gate_inputs,
    step_raw,
    state_write,
    state_read,
    log_rate,
    skip_gain,
    step_bias,
    grad_gated,
):
    x, g, dy = head_inputs[0], gate_inputs[0], grad_gated[0]
    raw = step_raw[0].T
    heads, rows = raw.shape
    cols = x.shape[1]
    half = state_write.shape[2]
    w, r = state_write[0].T, state_read[0].T
    wt, rt = exchange(w, "tensor", 1), exchange(r, "tensor", 1)
    rate, skip, bias = (v.reshape(1, heads) for v in (log_rate, skip_gain, step_bias))
    payload = ((cols + 16, STATE), BF16)
    big = ((rows, cols), BF16)
    pair = ((2, rows, cols), BF16)
    thin = ((rows, heads), F32)
    tiny = ((8, heads), F32)
    one = ((1, heads), F32)
    key = ((half, rows), BF16)
    x, g, dy, w, r, skip, qq, z, rate, al, be, wide, small = call(
        kernel_scale,
        [big, big, big, key, key, one, pair, thin, one, thin, thin, ((8, cols), F32), tiny],
        [
            pltpu.with_memory_space_constraint(v, pltpu.HBM)
            for v in (x, g, dy, raw, bias, rate, skip, w, r)
        ],
        [V((heads, rows), F32), V((1, heads), F32), V((rows, cols), F32), V((rows, cols), F32),
         pltpu.SemaphoreType.DMA((12,))],
        spaces=[pltpu.HBM] * 9,
    )
    turned, send_e, send_f = call(
        kernel_states,
        [((2, STATE, rows), BF16), payload, payload],
        [w, wt, r, rt, qq, wide, small],
    )
    got_e = exchange(send_e, "context", 3)
    got_f = exchange(send_f, "context", 1)
    gate, gate_f, inp, inp_f, dr, dw, keys, p, q, skips = call(
        kernel_within,
        [big] * 4 + [((STATE, rows), F32)] * 2 + [((2, rows, STATE), BF16), thin, thin, tiny],
        [x, g, dy, skip, turned, qq, al, be, wide],
        [V((rows, cols), F32)] * 2 + [V((8, cols), F32)],
        us=4.0,
    )
    (got_e,) = call(
        kernel_after, [payload], [got_e, skips],
        spaces=[ANY, ANY], out_spaces=[ANY], alias={0: 0}, us=0.01,
    )
    got_h = exchange(got_e, "context", 1)
    pe, pf, cross = call(
        kernel_early, [thin, thin, tiny], [got_e, got_f, keys, qq, small], us=2.0
    )
    grad_step, sums = call(
        kernel_steps,
        [((heads, rows), F32), tiny],
        [got_h, got_e, got_f, keys, qq, pe, pf, cross, p, q, small, z, rate, skips],
        us=1.0,
    )
    others = [exchange(sums, "context", mask) for mask in (1, 2, 3)]
    grad_in, grad_gate, keep, send = call(
        kernel_last,
        [big, big, ((STATE, rows), F32), ((STATE, rows), BF16)],
        [got_e, got_f, got_h, keys, qq, wide, gate, gate_f, inp, inp_f, dr, dw, sums],
        [V((8, cols), F32)],
        us=2.0,
        spaces=[V] * 12 + [ANY],
    )
    (sums,) = call(kernel_add, [tiny], [sums] + others + [send], spaces=[V] * 4 + [ANY], us=0.1)
    got = exchange(send, "tensor", 1)
    others = [exchange(sums, "dp", mask) for mask in (1, 2, 3)]
    grad_w, grad_r, sum_rate, sum_skip, sum_bias = call(
        kernel_finish,
        [((half, rows), F32)] * 2 + [one] * 3,
        [keep, got, sums] + others,
        us=0.2,
    )
    return (
        grad_in[None],
        grad_gate[None],
        grad_w.T[None],
        grad_r.T[None],
        grad_step.T[None],
        sum_rate.reshape(heads),
        sum_skip.reshape(heads),
        sum_bias.reshape(heads),
    )


def solution(mesh):
    wide = P("dp", "context", "tensor")
    head = P("tensor")
    return jax.shard_map(
        body,
        mesh=mesh,
        in_specs=(wide,) * 5 + (head,) * 3 + (wide,),
        out_specs=(wide,) * 5 + (head,) * 3,
        check_vma=False,
    )
```

time: 50.1 us -> 42.9 us (0.86)
  the two profiles are of different devices: /device:TPU:1 before, /device:TPU:224 now
where the time goes in v2:
time: 42.9 us; the launch traced here: 42.7 us
  waiting for transfers between devices  16 us (37%)
  Pallas kernels  13.6 us (32%)
  starting transfers between devices  12.4 us (29%)
  between operations  0.7 us (2%)
    ppermute x12, waiting for transfers between devices, exchange(): return lax.ppermute(array, axis, pairs)  16 us
    pallas_call x9, Pallas kernels, call(): pl.pallas_call(kernel, out_shape=[jax.ShapeDtypeStruct(s, d) for s, d in...  13.6 us
    ppermute x12, starting transfers between devices, exchange(): return lax.ppermute(array, axis, pairs)  12.4 us
  transfers between devices with their start and end apart: 12, of which 7 were waited for; matrix products, arithmetic and copies ran while one was open for 0% of the time, Pallas kernels for 19%

profile of v2, /device:TPU:224, one launch (start us, length us, event | category | flops | bytes accessed | tf_op | source)
XLA Modules:
  0.0 42.7 jit_solution(2599437241057699075)
XLA Ops:
  0.6 0.1 collective-permute-start
  0.7 0.5 %collective-permute-start.1 = (bf16[64,256]{1,0:T(8,128)(2,1)}, bf16[64,256]{1,0:T(8,128)(2,1)S(1)}, u32[]{:S(2)}, u32[]{:S(2)}) collective-permute-start(bf16[64,256]{1,0:T(8,128)(2,1)} %bitcast.34), channel_id=1, source_target_pairs={{0,1},{1,0},{2,3},{3,2},{4,5},{5,4},{6,7},{7,6},{8,9},{9,8},{10,11... | collective-permute-start | bytes 98312 | tf_op jit(solution)/shard_map/ppermute | solution.py:413
  1.2 2.5 %shard_map.152 = (bf16[256,1024]{1,0:T(8,128)(2,1)S(1)}, bf16[256,1024]{1,0:T(8,128)(2,1)S(1)}, bf16[256,1024]{1,0:T(8,128)(2,1)S(1)}, bf16[64,256]{1,0:T(8,128)...) custom-call(bf16[256,1024]{1,0:T(8,128)(2,1)} %bitcast.29, ...), custom_call_target="tpu_custom_call" | custom-call | flops 3000000000 | bytes 3000000 | tf_op jit(solution)/shard_map/pallas_call | solution.py:396
  3.8 0.0 collective-permute-done.wt_ref
  3.8 0.0 collective-permute-done.1.rt_ref
  3.8 0.5 %shard_map.153 = (bf16[2,128,256]{2,1,0:T(8,128)(2,1)S(1)}, bf16[1040,128]{1,0:T(8,128)(2,1)S(1)}, bf16[1040,128]{1,0:T(8,128)(2,1)S(1)}) custom-call(bf16[64,256]{1,0:T(8,128)(2,1)S(1)} %get-tuple-element.48.w_ref, bf16[64,256]{1,0:T(8,128)(2,1)S(1)} %collective-permute-done.wt_ref, bf16[64,256]{1,0:T(8,128)(2,1)S(1)} %get-tuple-element.49.r_ref, ...), custom_call_target="tpu_custom_call" | custom-call | flops 3000000000 | bytes 3000000 | tf_op jit(solution)/shard_map/pallas_call | solution.py:396
  4.3 3.1 %collective-permute-start.2 = (bf16[1040,128]{1,0:T(8,128)(2,1)S(1)}, bf16[1040,128]{1,0:T(8,128)(2,1)S(1)}, u32[]{:S(2)}, u32[]{:S(2)}) collective-permute-start(bf16[1040,128]{1,0:T(8,128)(2,1)S(1)} %get-tuple-element.53), channel_id=1, source_target_pairs={{0,48},{16,32},{32,16},{48,0},{1,49},{17,33},{33,17},{49,1},{2,50}... | collective-permute-start | bytes 798728 | tf_op jit(solution)/shard_map/ppermute | solution.py:413
  7.4 0.1 collective-permute-start.3
  7.6 4.0 %shard_map.154 = (bf16[256,1024]{1,0:T(8,128)(2,1)S(1)}, bf16[256,1024]{1,0:T(8,128)(2,1)S(1)}, bf16[256,1024]{1,0:T(8,128)(2,1)S(1)}, bf16[256,1024]{1,0:T(8,12...) custom-call(bf16[256,1024]{1,0:T(8,128)(2,1)S(1)} %get-tuple-element, ...), custom_call_target="tpu_custom_call" | custom-call | flops 4000000000 | bytes 4000000 | tf_op jit(solution)/shard_map/pallas_call | solution.py:396
  11.5 2.6 %collective-permute-done.2.first_ref = bf16[1040,128]{1,0:T(8,128)(2,1)S(1)} collective-permute-done((bf16[1040,128]{1,0:T(8,128)(2,1)S(1)}, bf16[1040,128]{1,0:T(8,128)(2,1)S(1)}, u32[]{:S(2)}, u32[]{:S(2)}) %collective-permute-start.2) | collective-permute-done | bytes 266272 | tf_op jit(solution)/shard_map/ppermute | solution.py:413
  14.1 0.3 collective-permute-start.4
  14.4 1.1 %collective-permute-done.3.f_ref = bf16[1040,128]{1,0:T(8,128)(2,1)S(1)} collective-permute-done((bf16[1040,128]{1,0:T(8,128)(2,1)S(1)}, bf16[1040,128]{1,0:T(8,128)(2,1)S(1)}, u32[]{:S(2)}, u32[]{:S(2)}) %collective-permute-start.3) | collective-permute-done | bytes 266272 | tf_op jit(solution)/shard_map/ppermute | solution.py:413
  15.5 1.5 %shard_map.156 = (f32[256,16]{1,0:T(8,128)S(1)}, f32[256,16]{1,0:T(8,128)S(1)}, f32[8,16]{1,0:T(8,128)S(1)}) custom-call(bf16[1040,128]{1,0:T(8,128)(2,1)S(1)} %shard_map.155.e_ref, bf16[1040,128]{1,0:T(8,128)(2,1)S(1)} %collective-permute-done.3.f_ref, bf16[2,256,128]{2,1,0:T(8,128)(2,1)S(1)} %get-tuple-element.63.keys_ref, ...), custom_call_target="tpu_custom_call" | custom-call | flops 2000000000 | bytes 2000000 | tf_op jit(solution)/shard_map/pallas_call | solution.py:396
  17.1 4.7 %collective-permute-done.4.h_ref = bf16[1040,128]{1,0:T(8,128)(2,1)S(1)} collective-permute-done((bf16[1040,128]{1,0:T(8,128)(2,1)S(1)}, bf16[1040,128]{1,0:T(8,128)(2,1)S(1)}, u32[]{:S(2)}, u32[]{:S(2)}) %collective-permute-start.4) | collective-permute-done | bytes 266272 | tf_op jit(solution)/shard_map/ppermute | solution.py:413
  21.7 1.8 %shard_map.157 = (f32[16,256]{1,0:T(8,128)}, f32[8,16]{1,0:T(8,128)S(1)}) custom-call(bf16[1040,128]{1,0:T(8,128)(2,1)S(1)} %collective-permute-done.4.h_ref, bf16[1040,128]{1,0:T(8,128)(2,1)S(1)} %shard_map.155.e_ref, bf16[1040,128]{1,0:T(8,128)(2,1)S(1)} %collective-permute-done.3.f_ref, bf16[2,256,128]{2,1,0:T(8,128)(2,1)S(1)} %get-tuple-element.63.keys_ref, ...), custom_call_target="tpu_custom_call" | custom-call | flops 1000000000 | bytes 1000000 | tf_op jit(solution)/shard_map/pallas_call | solution.py:396
  23.5 2.5 %shard_map.158 = (bf16[256,1024]{1,0:T(8,128)(2,1)}, bf16[256,1024]{1,0:T(8,128)(2,1)}, f32[128,256]{1,0:T(8,128)S(1)}, bf16[128,256]{1,0:T(8,128)(2,1)S(1)}) custom-call(bf16[1040,128]{1,0:T(8,128)(2,1)S(1)} %shard_map.155.e_ref, bf16[1040,128]{1,0:T(8,128)(2,1)S(1)} %collective-permute-done.3.f_ref, bf16[1040,128]{1,0:T(8,128)(2,1)S(1)} %collective-permute-done.4.h_ref, ...), custom_call_target="tpu_custom_call" | custom-call | flops 2000000000 | bytes 2000000 | tf_op jit(solution)/shard_map/pallas_call | solution.py:396
  26.1 0.0 collective-permute-start.5
  26.1 2.9 %collective-permute-start.8 = (f32[8,16]{1,0:T(8,128)S(1)}, f32[8,16]{1,0:T(8,128)S(1)}, u32[]{:S(2)}, u32[]{:S(2)}) collective-permute-start(f32[8,16]{1,0:T(8,128)S(1)} %get-tuple-element.77.after_ref.a_ref), channel_id=1, source_target_pairs={{0,48},{16,32},{32,16},{48,0},{1,49},{17,33},{33,17},{49,1},{2,50}... | collective-permute-start | bytes 1544 | tf_op jit(solution)/shard_map/ppermute | solution.py:413
  29.0 0.0 collective-permute-start.7
  29.0 1.2 %collective-permute-start.6 = (f32[8,16]{1,0:T(8,128)S(1)}, f32[8,16]{1,0:T(8,128)S(1)}, u32[]{:S(2)}, u32[]{:S(2)}) collective-permute-start(f32[8,16]{1,0:T(8,128)S(1)} %get-tuple-element.77.after_ref.a_ref), channel_id=1, source_target_pairs={{0,16},{16,0},{32,48},{48,32},{1,17},{17,1},{33,49},{49,33},{2,18}... | collective-permute-start | bytes 1544 | tf_op jit(solution)/shard_map/ppermute | solution.py:413
  30.2 0.7 %collective-permute-done.8.d_ref = f32[8,16]{1,0:T(8,128)S(1)} collective-permute-done((f32[8,16]{1,0:T(8,128)S(1)}, f32[8,16]{1,0:T(8,128)S(1)}, u32[]{:S(2)}, u32[]{:S(2)}) %collective-permute-start.8) | collective-permute-done | bytes 544 | tf_op jit(solution)/shard_map/ppermute | solution.py:413
  30.9 3.2 %collective-permute-done.7.c_ref = f32[8,16]{1,0:T(8,128)S(1)} collective-permute-done((f32[8,16]{1,0:T(8,128)S(1)}, f32[8,16]{1,0:T(8,128)S(1)}, u32[]{:S(2)}, u32[]{:S(2)}) %collective-permute-start.7) | collective-permute-done | bytes 544 | tf_op jit(solution)/shard_map/ppermute | solution.py:413
  34.1 0.0 collective-permute-done.6.b_ref
  34.1 2.8 %collective-permute-start.11 = (f32[8,16]{1,0:T(8,128)S(1)}, f32[8,16]{1,0:T(8,128)S(1)}, u32[]{:S(2)}, u32[]{:S(2)}) collective-permute-start(f32[8,16]{1,0:T(8,128)S(1)} %shard_map.159.a_ref), channel_id=1, source_target_pairs={{0,192},{64,128},{128,64},{192,0},{1,193},{65,129},{129,65},{193,1... | collective-permute-start | bytes 1544 | tf_op jit(solution)/shard_map/ppermute | solution.py:413
  36.9 0.8 %collective-permute-start.10 = (f32[8,16]{1,0:T(8,128)S(1)}, f32[8,16]{1,0:T(8,128)S(1)}, u32[]{:S(2)}, u32[]{:S(2)}) collective-permute-start(f32[8,16]{1,0:T(8,128)S(1)} %shard_map.159.a_ref), channel_id=1, source_target_pairs={{0,128},{64,192},{128,0},{192,64},{1,129},{65,193},{129,1},{193,65... | collective-permute-start | bytes 1544 | tf_op jit(solution)/shard_map/ppermute | solution.py:413
  37.7 0.5 %collective-permute-start.9 = (f32[8,16]{1,0:T(8,128)S(1)}, f32[8,16]{1,0:T(8,128)S(1)}, u32[]{:S(2)}, u32[]{:S(2)}) collective-permute-start(f32[8,16]{1,0:T(8,128)S(1)} %shard_map.159.a_ref), channel_id=1, source_target_pairs={{0,64},{64,0},{128,192},{192,128},{1,65},{65,1},{129,193},{193,129... | collective-permute-start | bytes 1544 | tf_op jit(solution)/shard_map/ppermute | solution.py:413
  38.3 0.7 %collective-permute-done.11.d_ref = f32[8,16]{1,0:T(8,128)S(1)} collective-permute-done((f32[8,16]{1,0:T(8,128)S(1)}, f32[8,16]{1,0:T(8,128)S(1)}, u32[]{:S(2)}, u32[]{:S(2)}) %collective-permute-start.11) | collective-permute-done | bytes 544 | tf_op jit(solution)/shard_map/ppermute | solution.py:413
  39.0 3.0 %collective-permute-done.10.c_ref = f32[8,16]{1,0:T(8,128)S(1)} collective-permute-done((f32[8,16]{1,0:T(8,128)S(1)}, f32[8,16]{1,0:T(8,128)S(1)}, u32[]{:S(2)}, u32[]{:S(2)}) %collective-permute-start.10) | collective-permute-done | bytes 544 | tf_op jit(solution)/shard_map/ppermute | solution.py:413
  42.0 0.0 collective-permute-done.9.b_ref
  42.0 0.0 collective-permute-done.5.got_ref
  42.0 0.7 %shard_map.160 = (f32[64,256]{1,0:T(8,128)}, f32[64,256]{1,0:T(8,128)}, f32[1,16]{1,0:T(1,128)}, f32[1,16]{1,0:T(1,128)}, f32[1,16]{1,0:T(1,128)}) custom-call(f32[128,256]{1,0:T(8,128)S(1)} %get-tuple-element.80.keep_ref, bf16[128,256]{1,0:T(8,128)(2,1)S(1)} %collective-permute-done.5.got_ref, f32[8,16]{1,0:T(8,128)S(1)} %shard_map.159.a_ref, ...), custom_call_target="tpu_custom_call" | custom-call | flops 200000000 | bytes 200000 | tf_op jit(solution)/shard_map/pallas_call | solution.py:396
  (2 shorter events, 0.0 us)
Async XLA Ops:
  0.6 3.1 %collective-permute-start = (bf16[64,256]{1,0:T(8,128)(2,1)}, bf16[64,256]{1,0:T(8,128)(2,1)S(1)}, u32[]{:S(2)}, u32[]{:S(2)}) collective-permute-start(bf16[64,256]{1,0:T(8,128)(2,1)} %bitcast.32), channel_id=1, source_target_pairs={{0,1},{1,0},{2,3},{3,2},{4,5},{5,4},{6,7},{7,6},{8,9},{9,8},{10,11... | collective-permute-start | bytes 98312 | tf_op jit(solution)/shard_map/ppermute | solution.py:413
  0.7 3.1 %collective-permute-start.1 = (bf16[64,256]{1,0:T(8,128)(2,1)}, bf16[64,256]{1,0:T(8,128)(2,1)S(1)}, u32[]{:S(2)}, u32[]{:S(2)}) collective-permute-start(bf16[64,256]{1,0:T(8,128)(2,1)} %bitcast.34), channel_id=1, source_target_pairs={{0,1},{1,0},{2,3},{3,2},{4,5},{5,4},{6,7},{7,6},{8,9},{9,8},{10,11... | collective-permute-start | bytes 98312 | tf_op jit(solution)/shard_map/ppermute | solution.py:413
  4.3 9.8 %collective-permute-start.2 = (bf16[1040,128]{1,0:T(8,128)(2,1)S(1)}, bf16[1040,128]{1,0:T(8,128)(2,1)S(1)}, u32[]{:S(2)}, u32[]{:S(2)}) collective-permute-start(bf16[1040,128]{1,0:T(8,128)(2,1)S(1)} %get-tuple-element.53), channel_id=1, source_target_pairs={{0,48},{16,32},{32,16},{48,0},{1,49},{17,33},{33,17},{49,1},{2,50}... | collective-permute-start | bytes 798728 | tf_op jit(solution)/shard_map/ppermute | solution.py:413
  7.4 8.1 %collective-permute-start.3 = (bf16[1040,128]{1,0:T(8,128)(2,1)S(1)}, bf16[1040,128]{1,0:T(8,128)(2,1)S(1)}, u32[]{:S(2)}, u32[]{:S(2)}) collective-permute-start(bf16[1040,128]{1,0:T(8,128)(2,1)S(1)} %get-tuple-element.62), channel_id=1, source_target_pairs={{0,16},{16,0},{32,48},{48,32},{1,17},{17,1},{33,49},{49,33},{2,18}... | collective-permute-start | bytes 798728 | tf_op jit(solution)/shard_map/ppermute | solution.py:413
  14.1 7.6 %collective-permute-start.4 = (bf16[1040,128]{1,0:T(8,128)(2,1)S(1)}, bf16[1040,128]{1,0:T(8,128)(2,1)S(1)}, u32[]{:S(2)}, u32[]{:S(2)}) collective-permute-start(bf16[1040,128]{1,0:T(8,128)(2,1)S(1)} %shard_map.155.e_ref), channel_id=1, source_target_pairs={{0,16},{16,0},{32,48},{48,32},{1,17},{17,1},{33,49},{49,33},{2,18}... | collective-permute-start | bytes 798728 | tf_op jit(solution)/shard_map/ppermute | solution.py:413
  26.1 16.0 %collective-permute-start.5 = (bf16[128,256]{1,0:T(8,128)(2,1)S(1)}, bf16[128,256]{1,0:T(8,128)(2,1)S(1)}, u32[]{:S(2)}, u32[]{:S(2)}) collective-permute-start(bf16[128,256]{1,0:T(8,128)(2,1)S(1)} %get-tuple-element.81.after_ref), channel_id=1, source_target_pairs={{0,1},{1,0},{2,3},{3,2},{4,5},{5,4},{6,7},{7,6},{8,9},{9,8},{10,11... | collective-permute-start | bytes 196616 | tf_op jit(solution)/shard_map/ppermute | solution.py:413
  26.1 4.8 %collective-permute-start.8 = (f32[8,16]{1,0:T(8,128)S(1)}, f32[8,16]{1,0:T(8,128)S(1)}, u32[]{:S(2)}, u32[]{:S(2)}) collective-permute-start(f32[8,16]{1,0:T(8,128)S(1)} %get-tuple-element.77.after_ref.a_ref), channel_id=1, source_target_pairs={{0,48},{16,32},{32,16},{48,0},{1,49},{17,33},{33,17},{49,1},{2,50}... | collective-permute-start | bytes 1544 | tf_op jit(solution)/shard_map/ppermute | solution.py:413
  29.0 5.1 %collective-permute-start.7 = (f32[8,16]{1,0:T(8,128)S(1)}, f32[8,16]{1,0:T(8,128)S(1)}, u32[]{:S(2)}, u32[]{:S(2)}) collective-permute-start(f32[8,16]{1,0:T(8,128)S(1)} %get-tuple-element.77.after_ref.a_ref), channel_id=1, source_target_pairs={{0,32},{16,48},{32,0},{48,16},{1,33},{17,49},{33,1},{49,17},{2,34}... | collective-permute-start | bytes 1544 | tf_op jit(solution)/shard_map/ppermute | solution.py:413
  29.0 5.1 %collective-permute-start.6 = (f32[8,16]{1,0:T(8,128)S(1)}, f32[8,16]{1,0:T(8,128)S(1)}, u32[]{:S(2)}, u32[]{:S(2)}) collective-permute-start(f32[8,16]{1,0:T(8,128)S(1)} %get-tuple-element.77.after_ref.a_ref), channel_id=1, source_target_pairs={{0,16},{16,0},{32,48},{48,32},{1,17},{17,1},{33,49},{49,33},{2,18}... | collective-permute-start | bytes 1544 | tf_op jit(solution)/shard_map/ppermute | solution.py:413
  34.1 4.9 %collective-permute-start.11 = (f32[8,16]{1,0:T(8,128)S(1)}, f32[8,16]{1,0:T(8,128)S(1)}, u32[]{:S(2)}, u32[]{:S(2)}) collective-permute-start(f32[8,16]{1,0:T(8,128)S(1)} %shard_map.159.a_ref), channel_id=1, source_target_pairs={{0,192},{64,128},{128,64},{192,0},{1,193},{65,129},{129,65},{193,1... | collective-permute-start | bytes 1544 | tf_op jit(solution)/shard_map/ppermute | solution.py:413
  36.9 5.1 %collective-permute-start.10 = (f32[8,16]{1,0:T(8,128)S(1)}, f32[8,16]{1,0:T(8,128)S(1)}, u32[]{:S(2)}, u32[]{:S(2)}) collective-permute-start(f32[8,16]{1,0:T(8,128)S(1)} %shard_map.159.a_ref), channel_id=1, source_target_pairs={{0,128},{64,192},{128,0},{192,64},{1,129},{65,193},{129,1},{193,65... | collective-permute-start | bytes 1544 | tf_op jit(solution)/shard_map/ppermute | solution.py:413
  37.7 4.3 %collective-permute-start.9 = (f32[8,16]{1,0:T(8,128)S(1)}, f32[8,16]{1,0:T(8,128)S(1)}, u32[]{:S(2)}, u32[]{:S(2)}) collective-permute-start(f32[8,16]{1,0:T(8,128)S(1)} %shard_map.159.a_ref), channel_id=1, source_target_pairs={{0,64},{64,0},{128,192},{192,128},{1,65},{65,1},{129,193},{193,129... | collective-permute-start | bytes 1544 | tf_op jit(solution)/shard_map/ppermute | solution.py:413

commit v3 on v2

--- a/solution.py
+++ b/solution.py
@@ -369,8 +369,7 @@
         send_ref[pl.ds(half, half), at_block(b)] = dr[b][half:].astype(BF16)
 
 
-def kernel_add(a_ref, b_ref, c_ref, d_ref, after_ref, out_ref):
-    del after_ref
+def kernel_add(a_ref, b_ref, c_ref, d_ref, out_ref):
     out_ref[...] = (a_ref[...] + b_ref[...]) + (c_ref[...] + d_ref[...])
 
 
@@ -482,12 +481,12 @@
     grad_in, grad_gate, keep, send = call(
         kernel_last,
         [big, big, ((STATE, rows), F32), ((STATE, rows), BF16)],
-        [got_e, got_f, got_h, keys, qq, wide, gate, gate_f, inp, inp_f, dr, dw, sums],
+        [got_e, got_f, got_h, keys, qq, wide, gate, gate_f, inp, inp_f, dr, dw, others[-1]],
         [V((8, cols), F32)],
         us=2.0,
         spaces=[V] * 12 + [ANY],
     )
-    (sums,) = call(kernel_add, [tiny], [sums] + others + [send], spaces=[V] * 4 + [ANY], us=0.1)
+    (sums,) = call(kernel_add, [tiny], [sums] + others, us=0.1)
     got = exchange(send, "tensor", 1)
     others = [exchange(sums, "dp", mask) for mask in (1, 2, 3)]
     grad_w, grad_r, sum_rate, sum_skip, sum_bias = call(

time: 42.9 us -> 45.4 us (1.058)
  starting transfers between devices: 12.4 us -> 14.9 us
    ppermute x12, starting transfers between devices: 12.4 us -> 14.9 us  [exchange(): return lax.ppermute(array, axis, pairs)]
  transfers between devices with their start and end apart: 12 -> 12, of which waited for: 7 -> 8; matrix products, arithmetic and copies ran while one was open for 0% -> 0% of each run, Pallas kernels for 19% -> 18%
where the time goes in v3:
time: 45.4 us; the launch traced here: 44.8 us
  waiting for transfers between devices  15.7 us (35%)
  starting transfers between devices  14.9 us (33%)
  Pallas kernels  13.6 us (30%)
  between operations  0.7 us (2%)
    ppermute x12, waiting for transfers between devices, exchange(): return lax.ppermute(array, axis, pairs)  15.7 us
    ppermute x12, starting transfers between devices, exchange(): return lax.ppermute(array, axis, pairs)  14.9 us
    pallas_call x9, Pallas kernels, call(): pl.pallas_call(kernel, out_shape=[jax.ShapeDtypeStruct(s, d) for s, d in...  13.6 us
  transfers between devices with their start and end apart: 12, of which 8 were waited for; matrix products, arithmetic and copies ran while one was open for 0% of the time, Pallas kernels for 18%

profile of v3, /device:TPU:224, one launch (start us, length us, event | category | flops | bytes accessed | tf_op | source)
XLA Modules:
  0.0 44.8 jit_solution(15181426223464254477)
XLA Ops:
  0.6 0.1 collective-permute-start
  0.7 0.5 %collective-permute-start.1 = (bf16[64,256]{1,0:T(8,128)(2,1)}, bf16[64,256]{1,0:T(8,128)(2,1)S(1)}, u32[]{:S(2)}, u32[]{:S(2)}) collective-permute-start(bf16[64,256]{1,0:T(8,128)(2,1)} %bitcast.34), channel_id=1, source_target_pairs={{0,1},{1,0},{2,3},{3,2},{4,5},{5,4},{6,7},{7,6},{8,9},{9,8},{10,11... | collective-permute-start | bytes 98312 | tf_op jit(solution)/shard_map/ppermute | solution.py:412
  1.2 2.5 %shard_map.152 = (bf16[256,1024]{1,0:T(8,128)(2,1)S(1)}, bf16[256,1024]{1,0:T(8,128)(2,1)S(1)}, bf16[256,1024]{1,0:T(8,128)(2,1)S(1)}, bf16[64,256]{1,0:T(8,128)...) custom-call(bf16[256,1024]{1,0:T(8,128)(2,1)} %bitcast.29, ...), custom_call_target="tpu_custom_call" | custom-call | flops 3000000000 | bytes 3000000 | tf_op jit(solution)/shard_map/pallas_call | solution.py:395
  3.8 0.0 collective-permute-done.wt_ref
  3.8 0.0 collective-permute-done.1.rt_ref
  3.8 0.5 %shard_map.153 = (bf16[2,128,256]{2,1,0:T(8,128)(2,1)S(1)}, bf16[1040,128]{1,0:T(8,128)(2,1)S(1)}, bf16[1040,128]{1,0:T(8,128)(2,1)S(1)}) custom-call(bf16[64,256]{1,0:T(8,128)(2,1)S(1)} %get-tuple-element.48.w_ref, bf16[64,256]{1,0:T(8,128)(2,1)S(1)} %collective-permute-done.wt_ref, bf16[64,256]{1,0:T(8,128)(2,1)S(1)} %get-tuple-element.49.r_ref, ...), custom_call_target="tpu_custom_call" | custom-call | flops 3000000000 | bytes 3000000 | tf_op jit(solution)/shard_map/pallas_call | solution.py:395
  4.3 3.1 %collective-permute-start.2 = (bf16[1040,128]{1,0:T(8,128)(2,1)S(1)}, bf16[1040,128]{1,0:T(8,128)(2,1)S(1)}, u32[]{:S(2)}, u32[]{:S(2)}) collective-permute-start(bf16[1040,128]{1,0:T(8,128)(2,1)S(1)} %get-tuple-element.53), channel_id=1, source_target_pairs={{0,48},{16,32},{32,16},{48,0},{1,49},{17,33},{33,17},{49,1},{2,50}... | collective-permute-start | bytes 798728 | tf_op jit(solution)/shard_map/ppermute | solution.py:412
  7.4 0.1 collective-permute-start.3
  7.6 4.0 %shard_map.154 = (bf16[256,1024]{1,0:T(8,128)(2,1)S(1)}, bf16[256,1024]{1,0:T(8,128)(2,1)S(1)}, bf16[256,1024]{1,0:T(8,128)(2,1)S(1)}, bf16[256,1024]{1,0:T(8,12...) custom-call(bf16[256,1024]{1,0:T(8,128)(2,1)S(1)} %get-tuple-element, ...), custom_call_target="tpu_custom_call" | custom-call | flops 4000000000 | bytes 4000000 | tf_op jit(solution)/shard_map/pallas_call | solution.py:395
  11.5 2.6 %collective-permute-done.2.first_ref = bf16[1040,128]{1,0:T(8,128)(2,1)S(1)} collective-permute-done((bf16[1040,128]{1,0:T(8,128)(2,1)S(1)}, bf16[1040,128]{1,0:T(8,128)(2,1)S(1)}, u32[]{:S(2)}, u32[]{:S(2)}) %collective-permute-start.2) | collective-permute-done | bytes 266272 | tf_op jit(solution)/shard_map/ppermute | solution.py:412
  14.1 0.3 collective-permute-start.4
  14.4 1.1 %collective-permute-done.3.f_ref = bf16[1040,128]{1,0:T(8,128)(2,1)S(1)} collective-permute-done((bf16[1040,128]{1,0:T(8,128)(2,1)S(1)}, bf16[1040,128]{1,0:T(8,128)(2,1)S(1)}, u32[]{:S(2)}, u32[]{:S(2)}) %collective-permute-start.3) | collective-permute-done | bytes 266272 | tf_op jit(solution)/shard_map/ppermute | solution.py:412
  15.5 1.5 %shard_map.156 = (f32[256,16]{1,0:T(8,128)S(1)}, f32[256,16]{1,0:T(8,128)S(1)}, f32[8,16]{1,0:T(8,128)S(1)}) custom-call(bf16[1040,128]{1,0:T(8,128)(2,1)S(1)} %shard_map.155.e_ref, bf16[1040,128]{1,0:T(8,128)(2,1)S(1)} %collective-permute-done.3.f_ref, bf16[2,256,128]{2,1,0:T(8,128)(2,1)S(1)} %get-tuple-element.63.keys_ref, ...), custom_call_target="tpu_custom_call" | custom-call | flops 2000000000 | bytes 2000000 | tf_op jit(solution)/shard_map/pallas_call | solution.py:395
  17.1 4.7 %collective-permute-done.4.h_ref = bf16[1040,128]{1,0:T(8,128)(2,1)S(1)} collective-permute-done((bf16[1040,128]{1,0:T(8,128)(2,1)S(1)}, bf16[1040,128]{1,0:T(8,128)(2,1)S(1)}, u32[]{:S(2)}, u32[]{:S(2)}) %collective-permute-start.4) | collective-permute-done | bytes 266272 | tf_op jit(solution)/shard_map/ppermute | solution.py:412
  21.7 1.8 %shard_map.157 = (f32[16,256]{1,0:T(8,128)}, f32[8,16]{1,0:T(8,128)S(1)}) custom-call(bf16[1040,128]{1,0:T(8,128)(2,1)S(1)} %collective-permute-done.4.h_ref, bf16[1040,128]{1,0:T(8,128)(2,1)S(1)} %shard_map.155.e_ref, bf16[1040,128]{1,0:T(8,128)(2,1)S(1)} %collective-permute-done.3.f_ref, bf16[2,256,128]{2,1,0:T(8,128)(2,1)S(1)} %get-tuple-element.63.keys_ref, ...), custom_call_target="tpu_custom_call" | custom-call | flops 1000000000 | bytes 1000000 | tf_op jit(solution)/shard_map/pallas_call | solution.py:395
  23.5 2.9 %collective-permute-start.5 = (f32[8,16]{1,0:T(8,128)S(1)}, f32[8,16]{1,0:T(8,128)S(1)}, u32[]{:S(2)}, u32[]{:S(2)}) collective-permute-start(f32[8,16]{1,0:T(8,128)S(1)} %get-tuple-element.77.a_ref), channel_id=1, source_target_pairs={{0,48},{16,32},{32,16},{48,0},{1,49},{17,33},{33,17},{49,1},{2,50}... | collective-permute-start | bytes 1544 | tf_op jit(solution)/shard_map/ppermute | solution.py:412
  26.4 1.9 %collective-permute-done.5.after_ref.d_ref = f32[8,16]{1,0:T(8,128)S(1)} collective-permute-done((f32[8,16]{1,0:T(8,128)S(1)}, f32[8,16]{1,0:T(8,128)S(1)}, u32[]{:S(2)}, u32[]{:S(2)}) %collective-permute-start.5) | collective-permute-done | bytes 544 | tf_op jit(solution)/shard_map/ppermute | solution.py:412
  28.3 2.5 %shard_map.158 = (bf16[256,1024]{1,0:T(8,128)(2,1)}, bf16[256,1024]{1,0:T(8,128)(2,1)}, f32[128,256]{1,0:T(8,128)S(1)}, bf16[128,256]{1,0:T(8,128)(2,1)S(1)}) custom-call(bf16[1040,128]{1,0:T(8,128)(2,1)S(1)} %shard_map.155.e_ref, bf16[1040,128]{1,0:T(8,128)(2,1)S(1)} %collective-permute-done.3.f_ref, bf16[1040,128]{1,0:T(8,128)(2,1)S(1)} %collective-permute-done.4.h_ref, ...), custom_call_target="tpu_custom_call" | custom-call | flops 2000000000 | bytes 2000000 | tf_op jit(solution)/shard_map/pallas_call | solution.py:395
  30.9 0.0 collective-permute-start.6
  30.9 1.4 %collective-permute-start.8 = (f32[8,16]{1,0:T(8,128)S(1)}, f32[8,16]{1,0:T(8,128)S(1)}, u32[]{:S(2)}, u32[]{:S(2)}) collective-permute-start(f32[8,16]{1,0:T(8,128)S(1)} %get-tuple-element.77.a_ref), channel_id=1, source_target_pairs={{0,32},{16,48},{32,0},{48,16},{1,33},{17,49},{33,1},{49,17},{2,34}... | collective-permute-start | bytes 1544 | tf_op jit(solution)/shard_map/ppermute | solution.py:412
  32.3 2.4 %collective-permute-start.7 = (f32[8,16]{1,0:T(8,128)S(1)}, f32[8,16]{1,0:T(8,128)S(1)}, u32[]{:S(2)}, u32[]{:S(2)}) collective-permute-start(f32[8,16]{1,0:T(8,128)S(1)} %get-tuple-element.77.a_ref), channel_id=1, source_target_pairs={{0,16},{16,0},{32,48},{48,32},{1,17},{17,1},{33,49},{49,33},{2,18}... | collective-permute-start | bytes 1544 | tf_op jit(solution)/shard_map/ppermute | solution.py:412
  34.6 1.4 %collective-permute-done.8.c_ref = f32[8,16]{1,0:T(8,128)S(1)} collective-permute-done((f32[8,16]{1,0:T(8,128)S(1)}, f32[8,16]{1,0:T(8,128)S(1)}, u32[]{:S(2)}, u32[]{:S(2)}) %collective-permute-start.8) | collective-permute-done | bytes 544 | tf_op jit(solution)/shard_map/ppermute | solution.py:412
  36.0 0.3 collective-permute-done.7.b_ref
  36.3 2.7 %collective-permute-start.11 = (f32[8,16]{1,0:T(8,128)S(1)}, f32[8,16]{1,0:T(8,128)S(1)}, u32[]{:S(2)}, u32[]{:S(2)}) collective-permute-start(f32[8,16]{1,0:T(8,128)S(1)} %shard_map.159.a_ref), channel_id=1, source_target_pairs={{0,192},{64,128},{128,64},{192,0},{1,193},{65,129},{129,65},{193,1... | collective-permute-start | bytes 1544 | tf_op jit(solution)/shard_map/ppermute | solution.py:412
  39.0 0.8 %collective-permute-start.10 = (f32[8,16]{1,0:T(8,128)S(1)}, f32[8,16]{1,0:T(8,128)S(1)}, u32[]{:S(2)}, u32[]{:S(2)}) collective-permute-start(f32[8,16]{1,0:T(8,128)S(1)} %shard_map.159.a_ref), channel_id=1, source_target_pairs={{0,128},{64,192},{128,0},{192,64},{1,129},{65,193},{129,1},{193,65... | collective-permute-start | bytes 1544 | tf_op jit(solution)/shard_map/ppermute | solution.py:412
  39.8 0.5 %collective-permute-start.9 = (f32[8,16]{1,0:T(8,128)S(1)}, f32[8,16]{1,0:T(8,128)S(1)}, u32[]{:S(2)}, u32[]{:S(2)}) collective-permute-start(f32[8,16]{1,0:T(8,128)S(1)} %shard_map.159.a_ref), channel_id=1, source_target_pairs={{0,64},{64,0},{128,192},{192,128},{1,65},{65,1},{129,193},{193,129... | collective-permute-start | bytes 1544 | tf_op jit(solution)/shard_map/ppermute | solution.py:412
  40.4 0.7 %collective-permute-done.11.d_ref = f32[8,16]{1,0:T(8,128)S(1)} collective-permute-done((f32[8,16]{1,0:T(8,128)S(1)}, f32[8,16]{1,0:T(8,128)S(1)}, u32[]{:S(2)}, u32[]{:S(2)}) %collective-permute-start.11) | collective-permute-done | bytes 544 | tf_op jit(solution)/shard_map/ppermute | solution.py:412
  41.1 3.0 %collective-permute-done.10.c_ref = f32[8,16]{1,0:T(8,128)S(1)} collective-permute-done((f32[8,16]{1,0:T(8,128)S(1)}, f32[8,16]{1,0:T(8,128)S(1)}, u32[]{:S(2)}, u32[]{:S(2)}) %collective-permute-start.10) | collective-permute-done | bytes 544 | tf_op jit(solution)/shard_map/ppermute | solution.py:412
  44.1 0.0 collective-permute-done.9.b_ref
  44.1 0.0 collective-permute-done.6.got_ref
  44.1 0.7 %shard_map.160 = (f32[64,256]{1,0:T(8,128)}, f32[64,256]{1,0:T(8,128)}, f32[1,16]{1,0:T(1,128)}, f32[1,16]{1,0:T(1,128)}, f32[1,16]{1,0:T(1,128)}) custom-call(f32[128,256]{1,0:T(8,128)S(1)} %get-tuple-element.80.keep_ref, bf16[128,256]{1,0:T(8,128)(2,1)S(1)} %collective-permute-done.6.got_ref, f32[8,16]{1,0:T(8,128)S(1)} %shard_map.159.a_ref, ...), custom_call_target="tpu_custom_call" | custom-call | flops 200000000 | bytes 200000 | tf_op jit(solution)/shard_map/pallas_call | solution.py:395
  (2 shorter events, 0.0 us)
Async XLA Ops:
  0.6 3.1 %collective-permute-start = (bf16[64,256]{1,0:T(8,128)(2,1)}, bf16[64,256]{1,0:T(8,128)(2,1)S(1)}, u32[]{:S(2)}, u32[]{:S(2)}) collective-permute-start(bf16[64,256]{1,0:T(8,128)(2,1)} %bitcast.32), channel_id=1, source_target_pairs={{0,1},{1,0},{2,3},{3,2},{4,5},{5,4},{6,7},{7,6},{8,9},{9,8},{10,11... | collective-permute-start | bytes 98312 | tf_op jit(solution)/shard_map/ppermute | solution.py:412
  0.7 3.1 %collective-permute-start.1 = (bf16[64,256]{1,0:T(8,128)(2,1)}, bf16[64,256]{1,0:T(8,128)(2,1)S(1)}, u32[]{:S(2)}, u32[]{:S(2)}) collective-permute-start(bf16[64,256]{1,0:T(8,128)(2,1)} %bitcast.34), channel_id=1, source_target_pairs={{0,1},{1,0},{2,3},{3,2},{4,5},{5,4},{6,7},{7,6},{8,9},{9,8},{10,11... | collective-permute-start | bytes 98312 | tf_op jit(solution)/shard_map/ppermute | solution.py:412
  4.3 9.8 %collective-permute-start.2 = (bf16[1040,128]{1,0:T(8,128)(2,1)S(1)}, bf16[1040,128]{1,0:T(8,128)(2,1)S(1)}, u32[]{:S(2)}, u32[]{:S(2)}) collective-permute-start(bf16[1040,128]{1,0:T(8,128)(2,1)S(1)} %get-tuple-element.53), channel_id=1, source_target_pairs={{0,48},{16,32},{32,16},{48,0},{1,49},{17,33},{33,17},{49,1},{2,50}... | collective-permute-start | bytes 798728 | tf_op jit(solution)/shard_map/ppermute | solution.py:412
  7.4 8.1 %collective-permute-start.3 = (bf16[1040,128]{1,0:T(8,128)(2,1)S(1)}, bf16[1040,128]{1,0:T(8,128)(2,1)S(1)}, u32[]{:S(2)}, u32[]{:S(2)}) collective-permute-start(bf16[1040,128]{1,0:T(8,128)(2,1)S(1)} %get-tuple-element.62), channel_id=1, source_target_pairs={{0,16},{16,0},{32,48},{48,32},{1,17},{17,1},{33,49},{49,33},{2,18}... | collective-permute-start | bytes 798728 | tf_op jit(solution)/shard_map/ppermute | solution.py:412
  14.1 7.6 %collective-permute-start.4 = (bf16[1040,128]{1,0:T(8,128)(2,1)S(1)}, bf16[1040,128]{1,0:T(8,128)(2,1)S(1)}, u32[]{:S(2)}, u32[]{:S(2)}) collective-permute-start(bf16[1040,128]{1,0:T(8,128)(2,1)S(1)} %shard_map.155.e_ref), channel_id=1, source_target_pairs={{0,16},{16,0},{32,48},{48,32},{1,17},{17,1},{33,49},{49,33},{2,18}... | collective-permute-start | bytes 798728 | tf_op jit(solution)/shard_map/ppermute | solution.py:412
  23.5 4.8 %collective-permute-start.5 = (f32[8,16]{1,0:T(8,128)S(1)}, f32[8,16]{1,0:T(8,128)S(1)}, u32[]{:S(2)}, u32[]{:S(2)}) collective-permute-start(f32[8,16]{1,0:T(8,128)S(1)} %get-tuple-element.77.a_ref), channel_id=1, source_target_pairs={{0,48},{16,32},{32,16},{48,0},{1,49},{17,33},{33,17},{49,1},{2,50}... | collective-permute-start | bytes 1544 | tf_op jit(solution)/shard_map/ppermute | solution.py:412
  30.9 13.3 %collective-permute-start.6 = (bf16[128,256]{1,0:T(8,128)(2,1)S(1)}, bf16[128,256]{1,0:T(8,128)(2,1)S(1)}, u32[]{:S(2)}, u32[]{:S(2)}) collective-permute-start(bf16[128,256]{1,0:T(8,128)(2,1)S(1)} %get-tuple-element.81), channel_id=1, source_target_pairs={{0,1},{1,0},{2,3},{3,2},{4,5},{5,4},{6,7},{7,6},{8,9},{9,8},{10,11... | collective-permute-start | bytes 196616 | tf_op jit(solution)/shard_map/ppermute | solution.py:412
  30.9 5.1 %collective-permute-start.8 = (f32[8,16]{1,0:T(8,128)S(1)}, f32[8,16]{1,0:T(8,128)S(1)}, u32[]{:S(2)}, u32[]{:S(2)}) collective-permute-start(f32[8,16]{1,0:T(8,128)S(1)} %get-tuple-element.77.a_ref), channel_id=1, source_target_pairs={{0,32},{16,48},{32,0},{48,16},{1,33},{17,49},{33,1},{49,17},{2,34}... | collective-permute-start | bytes 1544 | tf_op jit(solution)/shard_map/ppermute | solution.py:412
  32.3 4.0 %collective-permute-start.7 = (f32[8,16]{1,0:T(8,128)S(1)}, f32[8,16]{1,0:T(8,128)S(1)}, u32[]{:S(2)}, u32[]{:S(2)}) collective-permute-start(f32[8,16]{1,0:T(8,128)S(1)} %get-tuple-element.77.a_ref), channel_id=1, source_target_pairs={{0,16},{16,0},{32,48},{48,32},{1,17},{17,1},{33,49},{49,33},{2,18}... | collective-permute-start | bytes 1544 | tf_op jit(solution)/shard_map/ppermute | solution.py:412
  36.3 4.8 %collective-permute-start.11 = (f32[8,16]{1,0:T(8,128)S(1)}, f32[8,16]{1,0:T(8,128)S(1)}, u32[]{:S(2)}, u32[]{:S(2)}) collective-permute-start(f32[8,16]{1,0:T(8,128)S(1)} %shard_map.159.a_ref), channel_id=1, source_target_pairs={{0,192},{64,128},{128,64},{192,0},{1,193},{65,129},{129,65},{193,1... | collective-permute-start | bytes 1544 | tf_op jit(solution)/shard_map/ppermute | solution.py:412
  39.0 5.1 %collective-permute-start.10 = (f32[8,16]{1,0:T(8,128)S(1)}, f32[8,16]{1,0:T(8,128)S(1)}, u32[]{:S(2)}, u32[]{:S(2)}) collective-permute-start(f32[8,16]{1,0:T(8,128)S(1)} %shard_map.159.a_ref), channel_id=1, source_target_pairs={{0,128},{64,192},{128,0},{192,64},{1,129},{65,193},{129,1},{193,65... | collective-permute-start | bytes 1544 | tf_op jit(solution)/shard_map/ppermute | solution.py:412
  39.8 4.3 %collective-permute-start.9 = (f32[8,16]{1,0:T(8,128)S(1)}, f32[8,16]{1,0:T(8,128)S(1)}, u32[]{:S(2)}, u32[]{:S(2)}) collective-permute-start(f32[8,16]{1,0:T(8,128)S(1)} %shard_map.159.a_ref), channel_id=1, source_target_pairs={{0,64},{64,0},{128,192},{192,128},{1,65},{65,1},{129,193},{193,129... | collective-permute-start | bytes 1544 | tf_op jit(solution)/shard_map/ppermute | solution.py:412

commit v4 on v3

--- a/solution.py
+++ b/solution.py
@@ -60,6 +60,10 @@
     return jnp.maximum(z, 0.0) + jnp.log(1.0 + jnp.exp(-jnp.abs(z)))
 
 
+def logistic(v):
+    return 0.5 + 0.5 * jnp.tanh(0.5 * v)
+
+
 def at_block(b):
     return pl.ds(b * BLOCK, BLOCK)
 
@@ -68,7 +72,7 @@
     x_in, g_in, dy_in, raw_in, bias_in, rate_in, skip_in, w_in, r_in,
     x_ref, g_ref, dy_ref, w_ref, r_ref, skip_ref, qq_ref, z_ref, rate_ref, al_ref, be_ref,
     wide_ref, small_ref,
-    raw_ref, bias_ref, al_e, be_e, sems,
+    raw_ref, bias_ref, sems,
 ):
     rows, cols = x_ref.shape
     heads = raw_ref.shape[0]
@@ -98,6 +102,8 @@
     end = run[rows - 1 : rows]
     row = lax.broadcasted_iota(jnp.int32, (rows, heads), 0)
     rel = run - jnp.where(row < BLOCK, mid0, mid1)
+    for copy in large[0]:
+        copy.wait()
     al = jnp.exp2(rel)
     be = jnp.exp2(-rel) * step
     al_ref[...] = al
@@ -106,22 +112,27 @@
         jnp.concatenate([mid0, mid1, end - mid0, end - mid1, mid1 - mid0, end, end, end], axis=0)
     )
     small_ref[...] = small
+    small_parts = pieces(small, 3)
+    al_parts = pieces(al, 2)
+    be_parts = pieces(be, 2)
     for lo in range(0, cols, TILE):
         wide = expander(heads, lo, TILE)
-        here = pl.ds(lo, TILE)
-        al_e[:, here] = split_dot_right(al, wide, 2)
-        be_e[:, here] = split_dot_right(be, wide, 2)
-        wide_ref[:, here] = split_dot_right(small, wide, 3)
+        wide_ref[:, pl.ds(lo, TILE)] = sum(dot(part, wide) for part in small_parts)
     for b in range(blocks):
-        for copy in large[b]:
-            copy.wait()
+        if b:
+            for copy in large[b]:
+                copy.wait()
         at = at_block(b)
-        for lo in range(0, cols, BLOCK):
-            here = pl.ds(lo, BLOCK)
+        part = slice(b * BLOCK, (b + 1) * BLOCK)
+        for lo in range(0, cols, TILE):
+            here = pl.ds(lo, TILE)
+            wide = expander(heads, lo, TILE)
+            al_tile = sum(dot(v[part], wide) for v in al_parts)
+            be_tile = sum(dot(v[part], wide) for v in be_parts)
             g = g_ref[at, here].astype(F32)
-            u = dy_ref[at, here].astype(F32) * g / (1.0 + jnp.exp(-g))
-            qq_ref[1, at, here] = (u * al_e[at, here]).astype(BF16)
-            qq_ref[0, at, here] = (x_ref[at, here].astype(F32) * be_e[at, here]).astype(BF16)
+            u = dy_ref[at, here].astype(F32) * g * logistic(g)
+            qq_ref[1, at, here] = (u * al_tile).astype(BF16)
+            qq_ref[0, at, here] = (x_ref[at, here].astype(F32) * be_tile).astype(BF16)
     for copy in copies[3:]:
         copy.wait()
 
@@ -211,7 +222,7 @@
             g = g_ref[at, here].astype(F32)
             dy = dy_ref[at, here].astype(F32)
             x = x_ref[at, here].astype(F32)
-            sig = 1.0 / (1.0 + jnp.exp(-g))
+            sig = logistic(g)
             u = dy * g * sig
             up = dy * sig * (1.0 + g * (1.0 - sig))
             al = al_e[at, here]
@@ -241,12 +252,17 @@
 
 def head_sums(buffer_ref, key, weight_ref, index, heads):
     cols = weight_ref.shape[2]
-    out = jnp.zeros((key.shape[0], heads), F32)
-    for lo in range(0, cols, BLOCK):
-        here = pl.ds(lo, BLOCK)
-        product = weight_ref[index, :, here].astype(F32) * dot(key, buffer_ref[here, :])
-        out += split_dot_right(product, selector(heads, lo, BLOCK), 2)
-    return out
+    parts, select = [], []
+    for lo in range(0, cols, TILE):
+        tile = jnp.concatenate(
+            [buffer_ref[pl.ds(lo + k, BLOCK), :] for k in range(0, TILE, BLOCK)], axis=1
+        )
+        product = weight_ref[index, :, pl.ds(lo, TILE)].astype(F32) * dot(key, tile)
+        sel = selector(heads, lo, TILE)
+        for part in pieces(product, 2):
+            parts.append(part)
+            select.append(sel)
+    return dot(jnp.concatenate(parts, axis=1), jnp.concatenate(select, axis=0))
 
 
 def pair_sums(one_ref, two_ref, cols, heads):
@@ -313,14 +329,13 @@
     )
 
 
-def kernel_last(
-    e_ref, f_ref, h_ref, keys_ref, qq_ref, wide_ref,
-    gate_ref, gate_f_ref, in_ref, in_f_ref, dr_ref, dw_ref, after_ref,
-    grad_in_ref, grad_gate_ref, keep_ref, send_ref,
+def kernel_keys(
+    e_ref, f_ref, h_ref, qq_ref, wide_ref, dr_ref, dw_ref, after_ref,
+    keep_ref, send_ref, both_ref,
     coef_e,
 ):
     del after_ref
-    rows, cols = qq_ref.shape[1:]
+    cols = qq_ref.shape[2]
     half = STATE // 2
     heads = cols // HEAD_DIM
     nt = ((1,), (1,))
@@ -346,27 +361,39 @@
         y = jnp.where(inner, got_f, 0.0)
         s = jnp.where(place >= 2, x, y)
         a = jnp.where(place >= 2, y, x)
-        s_half = s.astype(BF16)
-        a_half = a.astype(BF16)
+        both_ref[0, :, here] = a.astype(BF16)
+        both_ref[1, :, here] = s.astype(BF16)
         for b in range(2):
             at = at_block(b)
             scaled_s = (s * wide_ref[b : b + 1, here]).astype(BF16)
             scaled_a = (a * wide_ref[2 + b : 3 + b, here]).astype(BF16)
             dr[b] += dot(scaled_s, qq_ref[1, at, here], nt)
             dw[b] += dot(scaled_a, qq_ref[0, at, here], nt)
-            v = dot(keys_ref[1, at, :], s_half)
-            z = dot(keys_ref[0, at, :], a_half)
+    for b in range(2):
+        keep_ref[pl.ds(0, half), at_block(b)] = dw[b][:half]
+        keep_ref[pl.ds(half, half), at_block(b)] = dr[b][:half]
+        send_ref[pl.ds(0, half), at_block(b)] = dw[b][half:].astype(BF16)
+        send_ref[pl.ds(half, half), at_block(b)] = dr[b][half:].astype(BF16)
+
+
+def kernel_outer(
+    both_ref, keys_ref, gate_ref, gate_f_ref, in_ref, in_f_ref, step_ref,
+    grad_in_ref, grad_gate_ref, grad_step_ref,
+):
+    grad_step_ref[...] = step_ref[...]
+    rows, cols = gate_ref.shape
+    for lo in range(0, cols, BLOCK):
+        here = pl.ds(lo, BLOCK)
+        for b in range(2):
+            at = at_block(b)
+            v = dot(keys_ref[1, at, :], both_ref[1, :, here])
+            z = dot(keys_ref[0, at, :], both_ref[0, :, here])
             grad_gate_ref[at, here] = (
                 gate_ref[at, here].astype(F32) + gate_f_ref[at, here].astype(F32) * v
             ).astype(BF16)
             grad_in_ref[at, here] = (
                 in_ref[at, here].astype(F32) + in_f_ref[at, here].astype(F32) * z
             ).astype(BF16)
-    for b in range(2):
-        keep_ref[pl.ds(0, half), at_block(b)] = dw[b][:half]
-        keep_ref[pl.ds(half, half), at_block(b)] = dr[b][:half]
-        send_ref[pl.ds(0, half), at_block(b)] = dw[b][half:].astype(BF16)
-        send_ref[pl.ds(half, half), at_block(b)] = dr[b][half:].astype(BF16)
 
 
 def kernel_add(a_ref, b_ref, c_ref, d_ref, out_ref):
@@ -445,8 +472,7 @@
             pltpu.with_memory_space_constraint(v, pltpu.HBM)
             for v in (x, g, dy, raw, bias, rate, skip, w, r)
         ],
-        [V((heads, rows), F32), V((1, heads), F32), V((rows, cols), F32), V((rows, cols), F32),
-         pltpu.SemaphoreType.DMA((12,))],
+        [V((heads, rows), F32), V((1, heads), F32), pltpu.SemaphoreType.DMA((12,))],
         spaces=[pltpu.HBM] * 9,
     )
     turned, send_e, send_f = call(
@@ -478,13 +504,17 @@
         us=1.0,
     )
     others = [exchange(sums, "context", mask) for mask in (1, 2, 3)]
-    grad_in, grad_gate, keep, send = call(
-        kernel_last,
-        [big, big, ((STATE, rows), F32), ((STATE, rows), BF16)],
-        [got_e, got_f, got_h, keys, qq, wide, gate, gate_f, inp, inp_f, dr, dw, others[-1]],
+    keep, send, ends = call(
+        kernel_keys,
+        [((STATE, rows), F32), ((STATE, rows), BF16), ((2, STATE, cols), BF16)],
+        [got_e, got_f, got_h, qq, wide, dr, dw, sums],
         [V((8, cols), F32)],
-        us=2.0,
-        spaces=[V] * 12 + [ANY],
+        us=1.0,
+        spaces=[V] * 7 + [ANY],
+    )
+    grad_in, grad_gate, grad_step = call(
+        kernel_outer, [big, big, ((heads, rows), F32)],
+        [ends, keys, gate, gate_f, inp, inp_f, grad_step], us=2.0,
     )
     (sums,) = call(kernel_add, [tiny], [sums] + others, us=0.1)
     got = exchange(send, "tensor", 1)

time: 45.4 us -> 39.4 us (0.87)
  starting transfers between devices: 14.9 us -> 12.6 us
  waiting for transfers between devices: 15.7 us -> 13.5 us
  Pallas kernels: 13.6 us -> 12.4 us
    ppermute x12, starting transfers between devices: 14.9 us -> 12.6 us  [exchange(): return lax.ppermute(array, axis, pairs)]
    ppermute x12, waiting for transfers between devices: 15.7 us -> 13.5 us  [exchange(): return lax.ppermute(array, axis, pairs)]
    pallas_call x9 -> x10, Pallas kernels: 13.6 us -> 12.4 us  [call(): pl.pallas_call(kernel, out_shape=[jax.ShapeDtypeStruct(s, d) for s, d in...]
  transfers between devices with their start and end apart: 12 -> 12, of which waited for: 8 -> 5; matrix products, arithmetic and copies ran while one was open for 0% -> 0% of each run, Pallas kernels for 18% -> 26%
where the time goes in v4:
time: 39.4 us; the launch traced here: 39.2 us
  waiting for transfers between devices  13.5 us (34%)
  starting transfers between devices  12.6 us (32%)
  Pallas kernels  12.4 us (31%)
  between operations  0.72 us (2%)
    ppermute x12, waiting for transfers between devices, exchange(): return lax.ppermute(array, axis, pairs)  13.5 us
    ppermute x12, starting transfers between devices, exchange(): return lax.ppermute(array, axis, pairs)  12.6 us
    pallas_call x10, Pallas kernels, call(): pl.pallas_call(kernel, out_shape=[jax.ShapeDtypeStruct(s, d) for s, d in...  12.4 us
  transfers between devices with their start and end apart: 12, of which 5 were waited for; matrix products, arithmetic and copies ran while one was open for 0% of the time, Pallas kernels for 26%

profile of v4, /device:TPU:224, one launch (start us, length us, event | category | flops | bytes accessed | tf_op | source)
XLA Modules:
  0.0 39.2 jit_solution(16643635313191814369)
XLA Ops:
  0.6 0.1 collective-permute-start
  0.7 0.5 %collective-permute-start.1 = (bf16[64,256]{1,0:T(8,128)(2,1)}, bf16[64,256]{1,0:T(8,128)(2,1)S(1)}, u32[]{:S(2)}, u32[]{:S(2)}) collective-permute-start(bf16[64,256]{1,0:T(8,128)(2,1)} %bitcast.34), channel_id=1, source_target_pairs={{0,1},{1,0},{2,3},{3,2},{4,5},{5,4},{6,7},{7,6},{8,9},{9,8},{10,11... | collective-permute-start | bytes 98312 | tf_op jit(solution)/shard_map/ppermute | solution.py:439
  1.2 2.2 %shard_map.152 = (bf16[256,1024]{1,0:T(8,128)(2,1)S(1)}, bf16[256,1024]{1,0:T(8,128)(2,1)S(1)}, bf16[256,1024]{1,0:T(8,128)(2,1)S(1)}, bf16[64,256]{1,0:T(8,128)...) custom-call(bf16[256,1024]{1,0:T(8,128)(2,1)} %bitcast.29, ...), custom_call_target="tpu_custom_call" | custom-call | flops 3000000000 | bytes 3000000 | tf_op jit(solution)/shard_map/pallas_call | solution.py:422
  3.4 0.0 collective-permute-done.wt_ref
  3.4 0.0 collective-permute-done.1.rt_ref
  3.4 0.5 %shard_map.153 = (bf16[2,128,256]{2,1,0:T(8,128)(2,1)S(1)}, bf16[1040,128]{1,0:T(8,128)(2,1)S(1)}, bf16[1040,128]{1,0:T(8,128)(2,1)S(1)}) custom-call(bf16[64,256]{1,0:T(8,128)(2,1)S(1)} %get-tuple-element.50.w_ref, bf16[64,256]{1,0:T(8,128)(2,1)S(1)} %collective-permute-done.wt_ref, bf16[64,256]{1,0:T(8,128)(2,1)S(1)} %get-tuple-element.51.r_ref, ...), custom_call_target="tpu_custom_call" | custom-call | flops 3000000000 | bytes 3000000 | tf_op jit(solution)/shard_map/pallas_call | solution.py:422
  4.0 3.1 %collective-permute-start.2 = (bf16[1040,128]{1,0:T(8,128)(2,1)S(1)}, bf16[1040,128]{1,0:T(8,128)(2,1)S(1)}, u32[]{:S(2)}, u32[]{:S(2)}) collective-permute-start(bf16[1040,128]{1,0:T(8,128)(2,1)S(1)} %get-tuple-element.55), channel_id=1, source_target_pairs={{0,48},{16,32},{32,16},{48,0},{1,49},{17,33},{33,17},{49,1},{2,50}... | collective-permute-start | bytes 798728 | tf_op jit(solution)/shard_map/ppermute | solution.py:439
  7.1 0.1 collective-permute-start.3
  7.2 3.9 %shard_map.154 = (bf16[256,1024]{1,0:T(8,128)(2,1)S(1)}, bf16[256,1024]{1,0:T(8,128)(2,1)S(1)}, bf16[256,1024]{1,0:T(8,128)(2,1)S(1)}, bf16[256,1024]{1,0:T(8,12...) custom-call(bf16[256,1024]{1,0:T(8,128)(2,1)S(1)} %get-tuple-element, ...), custom_call_target="tpu_custom_call" | custom-call | flops 4000000000 | bytes 4000000 | tf_op jit(solution)/shard_map/pallas_call | solution.py:422
  11.1 2.6 %collective-permute-done.2.first_ref = bf16[1040,128]{1,0:T(8,128)(2,1)S(1)} collective-permute-done((bf16[1040,128]{1,0:T(8,128)(2,1)S(1)}, bf16[1040,128]{1,0:T(8,128)(2,1)S(1)}, u32[]{:S(2)}, u32[]{:S(2)}) %collective-permute-start.2) | collective-permute-done | bytes 266272 | tf_op jit(solution)/shard_map/ppermute | solution.py:439
  13.7 0.3 collective-permute-start.4
  14.0 1.2 %collective-permute-done.3.f_ref = bf16[1040,128]{1,0:T(8,128)(2,1)S(1)} collective-permute-done((bf16[1040,128]{1,0:T(8,128)(2,1)S(1)}, bf16[1040,128]{1,0:T(8,128)(2,1)S(1)}, u32[]{:S(2)}, u32[]{:S(2)}) %collective-permute-start.3) | collective-permute-done | bytes 266272 | tf_op jit(solution)/shard_map/ppermute | solution.py:439
  15.2 1.3 %shard_map.156 = (f32[256,16]{1,0:T(8,128)S(1)}, f32[256,16]{1,0:T(8,128)S(1)}, f32[8,16]{1,0:T(8,128)S(1)}) custom-call(bf16[1040,128]{1,0:T(8,128)(2,1)S(1)} %shard_map.155.e_ref, bf16[1040,128]{1,0:T(8,128)(2,1)S(1)} %collective-permute-done.3.f_ref, bf16[2,256,128]{2,1,0:T(8,128)(2,1)S(1)} %get-tuple-element.67.keys_ref, ...), custom_call_target="tpu_custom_call" | custom-call | flops 2000000000 | bytes 2000000 | tf_op jit(solution)/shard_map/pallas_call | solution.py:422
  16.5 4.9 %collective-permute-done.4.h_ref = bf16[1040,128]{1,0:T(8,128)(2,1)S(1)} collective-permute-done((bf16[1040,128]{1,0:T(8,128)(2,1)S(1)}, bf16[1040,128]{1,0:T(8,128)(2,1)S(1)}, u32[]{:S(2)}, u32[]{:S(2)}) %collective-permute-start.4) | collective-permute-done | bytes 266272 | tf_op jit(solution)/shard_map/ppermute | solution.py:439
  21.4 1.1 %shard_map.157 = (f32[16,256]{1,0:T(8,128)S(1)}, f32[8,16]{1,0:T(8,128)S(1)}) custom-call(bf16[1040,128]{1,0:T(8,128)(2,1)S(1)} %collective-permute-done.4.h_ref, bf16[1040,128]{1,0:T(8,128)(2,1)S(1)} %shard_map.155.e_ref, bf16[1040,128]{1,0:T(8,128)(2,1)S(1)} %collective-permute-done.3.f_ref, bf16[2,256,128]{2,1,0:T(8,128)(2,1)S(1)} %get-tuple-element.67.keys_ref, ...), custom_call_target="tpu_custom_call" | custom-call | flops 1000000000 | bytes 1000000 | tf_op jit(solution)/shard_map/pallas_call | solution.py:422
  22.5 2.9 %collective-permute-start.8 = (f32[8,16]{1,0:T(8,128)S(1)}, f32[8,16]{1,0:T(8,128)S(1)}, u32[]{:S(2)}, u32[]{:S(2)}) collective-permute-start(f32[8,16]{1,0:T(8,128)S(1)} %get-tuple-element.75.after_ref.a_ref), channel_id=1, source_target_pairs={{0,48},{16,32},{32,16},{48,0},{1,49},{17,33},{33,17},{49,1},{2,50}... | collective-permute-start | bytes 1544 | tf_op jit(solution)/shard_map/ppermute | solution.py:439
  25.4 0.0 collective-permute-start.7
  25.4 1.2 %collective-permute-start.6 = (f32[8,16]{1,0:T(8,128)S(1)}, f32[8,16]{1,0:T(8,128)S(1)}, u32[]{:S(2)}, u32[]{:S(2)}) collective-permute-start(f32[8,16]{1,0:T(8,128)S(1)} %get-tuple-element.75.after_ref.a_ref), channel_id=1, source_target_pairs={{0,16},{16,0},{32,48},{48,32},{1,17},{17,1},{33,49},{49,33},{2,18}... | collective-permute-start | bytes 1544 | tf_op jit(solution)/shard_map/ppermute | solution.py:439
  26.6 1.0 %shard_map.158 = (f32[128,256]{1,0:T(8,128)S(1)}, bf16[128,256]{1,0:T(8,128)(2,1)S(1)}, bf16[2,128,1024]{2,1,0:T(8,128)(2,1)S(1)}) custom-call(bf16[1040,128]{1,0:T(8,128)(2,1)S(1)} %shard_map.155.e_ref, bf16[1040,128]{1,0:T(8,128)(2,1)S(1)} %collective-permute-done.3.f_ref, bf16[1040,128]{1,0:T(8,128)(2,1)S(1)} %collective-permute-done.4.h_ref, ...), custom_call_target="tpu_custom_call" | custom-call | flops 1000000000 | bytes 1000000 | tf_op jit(solution)/shard_map/pallas_call | solution.py:422
  27.7 0.1 collective-permute-start.5
  27.8 0.0 collective-permute-done.8.d_ref
  27.8 2.7 %collective-permute-done.7.c_ref = f32[8,16]{1,0:T(8,128)S(1)} collective-permute-done((f32[8,16]{1,0:T(8,128)S(1)}, f32[8,16]{1,0:T(8,128)S(1)}, u32[]{:S(2)}, u32[]{:S(2)}) %collective-permute-start.7) | collective-permute-done | bytes 544 | tf_op jit(solution)/shard_map/ppermute | solution.py:439
  30.5 0.0 collective-permute-done.6.b_ref
  30.5 2.9 %collective-permute-start.11 = (f32[8,16]{1,0:T(8,128)S(1)}, f32[8,16]{1,0:T(8,128)S(1)}, u32[]{:S(2)}, u32[]{:S(2)}) collective-permute-start(f32[8,16]{1,0:T(8,128)S(1)} %shard_map.160.a_ref), channel_id=1, source_target_pairs={{0,192},{64,128},{128,64},{192,0},{1,193},{65,129},{129,65},{193,1... | collective-permute-start | bytes 1544 | tf_op jit(solution)/shard_map/ppermute | solution.py:439
  33.4 0.8 %collective-permute-start.10 = (f32[8,16]{1,0:T(8,128)S(1)}, f32[8,16]{1,0:T(8,128)S(1)}, u32[]{:S(2)}, u32[]{:S(2)}) collective-permute-start(f32[8,16]{1,0:T(8,128)S(1)} %shard_map.160.a_ref), channel_id=1, source_target_pairs={{0,128},{64,192},{128,0},{192,64},{1,129},{65,193},{129,1},{193,65... | collective-permute-start | bytes 1544 | tf_op jit(solution)/shard_map/ppermute | solution.py:439
  34.2 0.5 %collective-permute-start.9 = (f32[8,16]{1,0:T(8,128)S(1)}, f32[8,16]{1,0:T(8,128)S(1)}, u32[]{:S(2)}, u32[]{:S(2)}) collective-permute-start(f32[8,16]{1,0:T(8,128)S(1)} %shard_map.160.a_ref), channel_id=1, source_target_pairs={{0,64},{64,0},{128,192},{192,128},{1,65},{65,1},{129,193},{193,129... | collective-permute-start | bytes 1544 | tf_op jit(solution)/shard_map/ppermute | solution.py:439
  34.7 1.7 %shard_map.159 = (bf16[256,1024]{1,0:T(8,128)(2,1)}, bf16[256,1024]{1,0:T(8,128)(2,1)}, f32[16,256]{1,0:T(8,128)}) custom-call(bf16[2,128,1024]{2,1,0:T(8,128)(2,1)S(1)} %get-tuple-element.76.both_ref, bf16[2,256,128]{2,1,0:T(8,128)(2,1)S(1)} %get-tuple-element.67.keys_ref, bf16[256,1024]{1,0:T(8,128)(2,1)S(1)} %get-tuple-element.77.gate_ref, ...), custom_call_target="tpu_custom_call" | custom-call | flops 2000000000 | bytes 2000000 | tf_op jit(solution)/shard_map/pallas_call | solution.py:422
  36.4 0.0 collective-permute-done.11.d_ref
  36.4 2.1 %collective-permute-done.10.c_ref = f32[8,16]{1,0:T(8,128)S(1)} collective-permute-done((f32[8,16]{1,0:T(8,128)S(1)}, f32[8,16]{1,0:T(8,128)S(1)}, u32[]{:S(2)}, u32[]{:S(2)}) %collective-permute-start.10) | collective-permute-done | bytes 544 | tf_op jit(solution)/shard_map/ppermute | solution.py:439
  38.5 0.0 collective-permute-done.9.b_ref
  38.5 0.0 collective-permute-done.5.got_ref
  38.5 0.7 %shard_map.161 = (f32[64,256]{1,0:T(8,128)}, f32[64,256]{1,0:T(8,128)}, f32[1,16]{1,0:T(1,128)}, f32[1,16]{1,0:T(1,128)}, f32[1,16]{1,0:T(1,128)}) custom-call(f32[128,256]{1,0:T(8,128)S(1)} %get-tuple-element.84.keep_ref, bf16[128,256]{1,0:T(8,128)(2,1)S(1)} %collective-permute-done.5.got_ref, f32[8,16]{1,0:T(8,128)S(1)} %shard_map.160.a_ref, ...), custom_call_target="tpu_custom_call" | custom-call | flops 200000000 | bytes 200000 | tf_op jit(solution)/shard_map/pallas_call | solution.py:422
  (2 shorter events, 0.0 us)
Async XLA Ops:
  0.6 2.8 %collective-permute-start = (bf16[64,256]{1,0:T(8,128)(2,1)}, bf16[64,256]{1,0:T(8,128)(2,1)S(1)}, u32[]{:S(2)}, u32[]{:S(2)}) collective-permute-start(bf16[64,256]{1,0:T(8,128)(2,1)} %bitcast.32), channel_id=1, source_target_pairs={{0,1},{1,0},{2,3},{3,2},{4,5},{5,4},{6,7},{7,6},{8,9},{9,8},{10,11... | collective-permute-start | bytes 98312 | tf_op jit(solution)/shard_map/ppermute | solution.py:439
  0.7 2.7 %collective-permute-start.1 = (bf16[64,256]{1,0:T(8,128)(2,1)}, bf16[64,256]{1,0:T(8,128)(2,1)S(1)}, u32[]{:S(2)}, u32[]{:S(2)}) collective-permute-start(bf16[64,256]{1,0:T(8,128)(2,1)} %bitcast.34), channel_id=1, source_target_pairs={{0,1},{1,0},{2,3},{3,2},{4,5},{5,4},{6,7},{7,6},{8,9},{9,8},{10,11... | collective-permute-start | bytes 98312 | tf_op jit(solution)/shard_map/ppermute | solution.py:439
  4.0 9.8 %collective-permute-start.2 = (bf16[1040,128]{1,0:T(8,128)(2,1)S(1)}, bf16[1040,128]{1,0:T(8,128)(2,1)S(1)}, u32[]{:S(2)}, u32[]{:S(2)}) collective-permute-start(bf16[1040,128]{1,0:T(8,128)(2,1)S(1)} %get-tuple-element.55), channel_id=1, source_target_pairs={{0,48},{16,32},{32,16},{48,0},{1,49},{17,33},{33,17},{49,1},{2,50}... | collective-permute-start | bytes 798728 | tf_op jit(solution)/shard_map/ppermute | solution.py:439
  7.1 8.1 %collective-permute-start.3 = (bf16[1040,128]{1,0:T(8,128)(2,1)S(1)}, bf16[1040,128]{1,0:T(8,128)(2,1)S(1)}, u32[]{:S(2)}, u32[]{:S(2)}) collective-permute-start(bf16[1040,128]{1,0:T(8,128)(2,1)S(1)} %get-tuple-element.64), channel_id=1, source_target_pairs={{0,16},{16,0},{32,48},{48,32},{1,17},{17,1},{33,49},{49,33},{2,18}... | collective-permute-start | bytes 798728 | tf_op jit(solution)/shard_map/ppermute | solution.py:439
  13.7 7.6 %collective-permute-start.4 = (bf16[1040,128]{1,0:T(8,128)(2,1)S(1)}, bf16[1040,128]{1,0:T(8,128)(2,1)S(1)}, u32[]{:S(2)}, u32[]{:S(2)}) collective-permute-start(bf16[1040,128]{1,0:T(8,128)(2,1)S(1)} %shard_map.155.e_ref), channel_id=1, source_target_pairs={{0,16},{16,0},{32,48},{48,32},{1,17},{17,1},{33,49},{49,33},{2,18}... | collective-permute-start | bytes 798728 | tf_op jit(solution)/shard_map/ppermute | solution.py:439
  22.5 5.3 %collective-permute-start.8 = (f32[8,16]{1,0:T(8,128)S(1)}, f32[8,16]{1,0:T(8,128)S(1)}, u32[]{:S(2)}, u32[]{:S(2)}) collective-permute-start(f32[8,16]{1,0:T(8,128)S(1)} %get-tuple-element.75.after_ref.a_ref), channel_id=1, source_target_pairs={{0,48},{16,32},{32,16},{48,0},{1,49},{17,33},{33,17},{49,1},{2,50}... | collective-permute-start | bytes 1544 | tf_op jit(solution)/shard_map/ppermute | solution.py:439
  25.4 5.1 %collective-permute-start.7 = (f32[8,16]{1,0:T(8,128)S(1)}, f32[8,16]{1,0:T(8,128)S(1)}, u32[]{:S(2)}, u32[]{:S(2)}) collective-permute-start(f32[8,16]{1,0:T(8,128)S(1)} %get-tuple-element.75.after_ref.a_ref), channel_id=1, source_target_pairs={{0,32},{16,48},{32,0},{48,16},{1,33},{17,49},{33,1},{49,17},{2,34}... | collective-permute-start | bytes 1544 | tf_op jit(solution)/shard_map/ppermute | solution.py:439
  25.4 5.1 %collective-permute-start.6 = (f32[8,16]{1,0:T(8,128)S(1)}, f32[8,16]{1,0:T(8,128)S(1)}, u32[]{:S(2)}, u32[]{:S(2)}) collective-permute-start(f32[8,16]{1,0:T(8,128)S(1)} %get-tuple-element.75.after_ref.a_ref), channel_id=1, source_target_pairs={{0,16},{16,0},{32,48},{48,32},{1,17},{17,1},{33,49},{49,33},{2,18}... | collective-permute-start | bytes 1544 | tf_op jit(solution)/shard_map/ppermute | solution.py:439
  27.7 10.8 %collective-permute-start.5 = (bf16[128,256]{1,0:T(8,128)(2,1)S(1)}, bf16[128,256]{1,0:T(8,128)(2,1)S(1)}, u32[]{:S(2)}, u32[]{:S(2)}) collective-permute-start(bf16[128,256]{1,0:T(8,128)(2,1)S(1)} %get-tuple-element.85), channel_id=1, source_target_pairs={{0,1},{1,0},{2,3},{3,2},{4,5},{5,4},{6,7},{7,6},{8,9},{9,8},{10,11... | collective-permute-start | bytes 196616 | tf_op jit(solution)/shard_map/ppermute | solution.py:439
  30.5 5.9 %collective-permute-start.11 = (f32[8,16]{1,0:T(8,128)S(1)}, f32[8,16]{1,0:T(8,128)S(1)}, u32[]{:S(2)}, u32[]{:S(2)}) collective-permute-start(f32[8,16]{1,0:T(8,128)S(1)} %shard_map.160.a_ref), channel_id=1, source_target_pairs={{0,192},{64,128},{128,64},{192,0},{1,193},{65,129},{129,65},{193,1... | collective-permute-start | bytes 1544 | tf_op jit(solution)/shard_map/ppermute | solution.py:439
  33.4 5.1 %collective-permute-start.10 = (f32[8,16]{1,0:T(8,128)S(1)}, f32[8,16]{1,0:T(8,128)S(1)}, u32[]{:S(2)}, u32[]{:S(2)}) collective-permute-start(f32[8,16]{1,0:T(8,128)S(1)} %shard_map.160.a_ref), channel_id=1, source_target_pairs={{0,128},{64,192},{128,0},{192,64},{1,129},{65,193},{129,1},{193,65... | collective-permute-start | bytes 1544 | tf_op jit(solution)/shard_map/ppermute | solution.py:439
  34.2 4.3 %collective-permute-start.9 = (f32[8,16]{1,0:T(8,128)S(1)}, f32[8,16]{1,0:T(8,128)S(1)}, u32[]{:S(2)}, u32[]{:S(2)}) collective-permute-start(f32[8,16]{1,0:T(8,128)S(1)} %shard_map.160.a_ref), channel_id=1, source_target_pairs={{0,64},{64,0},{128,192},{192,128},{1,65},{65,1},{129,193},{193,129... | collective-permute-start | bytes 1544 | tf_op jit(solution)/shard_map/ppermute | solution.py:439

commit v5 on v4

--- a/solution.py
+++ b/solution.py
@@ -169,8 +169,10 @@
 
 
 def kernel_within(
-    x_ref, g_ref, dy_ref, skip_ref, turned_ref, qq_ref, al_ref, be_ref, wide_ref,
-    gate_ref, gate_f_ref, in_ref, in_f_ref, dr_ref, dw_ref, keys_ref, p_ref, q_ref, skip_out_ref,
+    x_ref, g_ref, dy_ref, skip_ref, turned_ref, qq_ref, al_ref, be_ref, wide_ref, z_ref, rate_ref,
+    small_ref,
+    gate_ref, gate_f_ref, in_ref, in_f_ref, dr_ref, dw_ref, keys_ref, p_ref, q_ref, probe_ref,
+    local_ref,
     al_e, be_e, skip_e,
 ):
     rows, cols = x_ref.shape
@@ -233,10 +235,46 @@
             in_f_ref[at, here] = (be * wide_ref[2 + b : 3 + b, here]).astype(BF16)
             ux = jnp.sum((u * x).reshape(BLOCK // 8, 8, BLOCK), axis=0)
             skips += split_dot_right(ux, sel, 3)
-    for b in range(2):
-        p_ref[at_block(b), :] = p[b]
-        q_ref[at_block(b), :] = q[b]
-    skip_out_ref[...] = skips
+    z = z_ref[...]
+    rate = jnp.exp(rate_ref[...])
+    step = softplus(z)
+    slope = 1.0 / (1.0 + jnp.exp(-z))
+    lower = triangle(rows, True)
+    decayed = split_dot_left(lower, -rate * step, 3)
+    climbed = rate * split_dot_left(lower, slope, 3)
+    direct = slope / step
+    decay_end = decayed[rows - 1 : rows]
+    climb_end = climbed[rows - 1 : rows]
+    weights = [
+        [decay_end - decayed, direct + climbed - climb_end],
+        [decayed, -climbed],
+    ]
+    for side in range(2):
+        turned = [wt, rt][side]
+        for n in range(2):
+            parts = pieces(weights[side][n], 2)
+            for lo in range(0, cols, TILE):
+                here = pl.ds(lo, TILE)
+                wide = expander(heads, lo, TILE)
+                total = jnp.zeros((STATE, TILE), F32)
+                for b in range(2):
+                    part = slice(b * BLOCK, (b + 1) * BLOCK)
+                    weight = sum(dot(v[part], wide) for v in parts)
+                    scaled = qq_ref[side, at_block(b), here].astype(F32) * weight
+                    row = (2 if side == 0 else 0) + b
+                    total += dot(turned[b], scaled.astype(BF16)) * wide_ref[row : row + 1, here]
+                probe_ref[side, n, :, here] = total
+    p = jnp.concatenate(p, axis=0)
+    q = jnp.concatenate(q, axis=0)
+    p_ref[...] = p
+    q_ref[...] = q
+    local = [
+        jnp.sum(v, axis=0, keepdims=True)
+        for v in (decayed * (p - q), skips, direct * q - climbed * (p - q))
+    ]
+    kept = small_ref[5:6]
+    local += [decay_end * kept, -climb_end * kept] + [jnp.zeros_like(kept)] * 3
+    local_ref[...] = jnp.concatenate(local, axis=0)
     m00 = jnp.where(i >= j, m00, 0.0).astype(BF16)
     m11 = jnp.where(i >= j, m11, 0.0).astype(BF16)
     m10 = m10.astype(BF16)
@@ -246,110 +284,35 @@
     dw_ref[:, at_block(1)] = dot(rt[1], m11)
 
 
-def kernel_after(first_ref, token_ref, out_ref):
-    del first_ref, token_ref, out_ref
-
-
-def head_sums(buffer_ref, key, weight_ref, index, heads):
-    cols = weight_ref.shape[2]
-    parts, select = [], []
-    for lo in range(0, cols, TILE):
-        tile = jnp.concatenate(
-            [buffer_ref[pl.ds(lo + k, BLOCK), :] for k in range(0, TILE, BLOCK)], axis=1
-        )
-        product = weight_ref[index, :, pl.ds(lo, TILE)].astype(F32) * dot(key, tile)
-        sel = selector(heads, lo, TILE)
-        for part in pieces(product, 2):
-            parts.append(part)
-            select.append(sel)
-    return dot(jnp.concatenate(parts, axis=1), jnp.concatenate(select, axis=0))
-
-
-def pair_sums(one_ref, two_ref, cols, heads):
-    out = jnp.zeros((8, heads), F32)
-    for lo in range(0, cols, BLOCK):
-        here = pl.ds(lo, BLOCK)
-        product = one_ref[here, :].astype(F32) * two_ref[here, :].astype(F32)
-        product = jnp.sum(product.reshape(STATE // 8, 8, BLOCK), axis=0)
-        out += split_dot_right(product, selector(heads, lo, BLOCK), 2)
-    return out
-
-
-def kernel_early(e_ref, f_ref, keys_ref, qq_ref, small_ref, pe_ref, pf_ref, cross_ref):
-    cols = qq_ref.shape[2]
-    heads = small_ref.shape[1]
-    place = lax.axis_index("context")
-    mine = (place >= 2).astype(jnp.int32)
-    side = lax.rem(place, 2)
-    pe_ref[...] = head_sums(e_ref, keys_ref[mine], qq_ref, mine, heads)
-    pf_ref[...] = head_sums(f_ref, keys_ref[side], qq_ref, side, heads)
-    cross_ref[...] = pair_sums(e_ref, f_ref, cols, heads)
-
-
 def total_of(ref, cols, heads):
     parts = ref[pl.ds(cols, 16), :].astype(F32)
     return (parts[0:1] + parts[1:2] + parts[2:3])[:, :heads]
 
 
-def kernel_steps(
-    h_ref, e_ref, f_ref, keys_ref, qq_ref, pe_ref, pf_ref, cross_ref, p_ref, q_ref,
-    small_ref, z_ref, rate_ref, skips_ref,
-    step_ref, sums_ref,
-):
-    rows, cols = qq_ref.shape[1:]
-    heads = small_ref.shape[1]
-    place = lax.axis_index("context")
-    mine = (place >= 2).astype(jnp.int32)
-    inner = (place == 1) | (place == 2)
-    te, tf, th = (total_of(ref, cols, heads) for ref in (e_ref, f_ref, h_ref))
-    ph = head_sums(h_ref, keys_ref[mine], qq_ref, mine, heads)
-    cross = cross_ref[...] + te * pair_sums(h_ref, f_ref, cols, heads)
-    cross = jnp.where(inner, jnp.sum(cross, axis=0, keepdims=True), 0.0)
-    pe = pe_ref[...]
-    pf = pf_ref[...]
-    px = jnp.where(inner, pe + te * ph, pf + tf * (ph + th * pe))
-    py = jnp.where(inner, pf, 0.0)
-    row = lax.broadcasted_iota(jnp.int32, (rows, heads), 0)
-    p = jnp.where(mine == 1, px, py) * jnp.where(row < BLOCK, small_ref[0:1], small_ref[1:2])
-    q = jnp.where(mine == 1, py, px) * jnp.where(row < BLOCK, small_ref[2:3], small_ref[3:4])
-    ends = jnp.sum(q, axis=0, keepdims=True) + small_ref[5:6] * cross
-    q = q + q_ref[...]
-    flow = split_dot_left(triangle(rows, False), p + p_ref[...] - q, 3) + ends
-    z = z_ref[...]
-    step = softplus(z)
-    rate = jnp.exp(rate_ref[...])
-    grad = (q / step - rate * flow) / (1.0 + jnp.exp(-z))
-    step_ref[...] = grad.T
-    sum_rate = jnp.sum(flow * step, axis=0, keepdims=True) * -rate
-    sum_bias = jnp.sum(grad, axis=0, keepdims=True)
-    sum_skip = jnp.sum(skips_ref[...], axis=0, keepdims=True)
-    index = lax.broadcasted_iota(jnp.int32, (8, heads), 0)
-    sums_ref[...] = jnp.where(
-        index == 0, sum_rate, jnp.where(index == 1, sum_skip, jnp.where(index == 2, sum_bias, 0.0))
-    )
-
-
-def kernel_keys(
-    e_ref, f_ref, h_ref, qq_ref, wide_ref, dr_ref, dw_ref, after_ref,
-    keep_ref, send_ref, both_ref,
+def kernel_sums(
+    e_ref, f_ref, h_ref, probe_ref, local_ref,
+    sums_ref, both_ref, cross_ref,
     coef_e,
 ):
-    del after_ref
-    cols = qq_ref.shape[2]
-    half = STATE // 2
-    heads = cols // HEAD_DIM
-    nt = ((1,), (1,))
+    cols = both_ref.shape[2]
+    heads = local_ref.shape[1]
     place = lax.axis_index("context")
     inner = (place == 1) | (place == 2)
+    mine = (place >= 2).astype(jnp.int32)
     te, tf, th = (total_of(ref, cols, heads) for ref in (e_ref, f_ref, h_ref))
     coef = jnp.concatenate(
         [jnp.where(inner, 1.0, tf * th), jnp.where(inner, te, tf)] + [jnp.zeros_like(te)] * 6,
         axis=0,
     )
+    coef_parts = pieces(coef, 3)
     for lo in range(0, cols, TILE):
-        coef_e[:, pl.ds(lo, TILE)] = split_dot_right(coef, expander(heads, lo, TILE), 3)
-    dr = [dr_ref[:, at_block(b)] for b in range(2)]
-    dw = [dw_ref[:, at_block(b)] for b in range(2)]
+        wide = expander(heads, lo, TILE)
+        coef_e[:, pl.ds(lo, TILE)] = sum(dot(part, wide) for part in coef_parts)
+
+    def folded(v):
+        return jnp.sum(v.reshape(STATE // 8, 8, BLOCK), axis=0)
+
+    rows, select = [], []
     for lo in range(0, cols, BLOCK):
         here = pl.ds(lo, BLOCK)
         got_f = f_ref[here, :].astype(F32)
@@ -359,33 +322,70 @@
             + jnp.where(inner, 0.0, got_f)
         )
         y = jnp.where(inner, got_f, 0.0)
-        s = jnp.where(place >= 2, x, y)
-        a = jnp.where(place >= 2, y, x)
-        both_ref[0, :, here] = a.astype(BF16)
-        both_ref[1, :, here] = s.astype(BF16)
-        for b in range(2):
-            at = at_block(b)
-            scaled_s = (s * wide_ref[b : b + 1, here]).astype(BF16)
-            scaled_a = (a * wide_ref[2 + b : 3 + b, here]).astype(BF16)
-            dr[b] += dot(scaled_s, qq_ref[1, at, here], nt)
-            dw[b] += dot(scaled_a, qq_ref[0, at, here], nt)
+        both_ref[mine, :, here] = x.astype(BF16)
+        both_ref[1 - mine, :, here] = y.astype(BF16)
+        products = [
+            folded(x * probe_ref[mine, n, :, here] + y * probe_ref[1 - mine, n, :, here])
+            for n in range(2)
+        ] + [folded(x * y), jnp.zeros((8, BLOCK), F32)]
+        for part in pieces(jnp.concatenate(products, axis=0), 2):
+            rows.append(part)
+            select.append(selector(heads, lo, BLOCK))
+    out = dot(jnp.concatenate(rows, axis=1), jnp.concatenate(select, axis=0))
+    rate, bias, cross = (
+        jnp.sum(out[8 * n : 8 * n + 8], axis=0, keepdims=True) for n in range(3)
+    )
+    local = local_ref[...]
+    rate = rate + local[0:1] + local[3:4] * cross
+    bias = bias + local[2:3] + local[4:5] * cross
+    index = lax.broadcasted_iota(jnp.int32, (8, heads), 0)
+    sums_ref[...] = jnp.where(
+        index == 0, rate, jnp.where(index == 1, local[1:2], jnp.where(index == 2, bias, 0.0))
+    )
+    cross_ref[...] = jnp.broadcast_to(cross, (8, heads))
+
+
+def kernel_keys(both_ref, qq_ref, wide_ref, dr_ref, dw_ref, keep_ref, send_ref):
+    cols = qq_ref.shape[2]
+    half = STATE // 2
+    nt = ((1,), (1,))
     for b in range(2):
-        keep_ref[pl.ds(0, half), at_block(b)] = dw[b][:half]
-        keep_ref[pl.ds(half, half), at_block(b)] = dr[b][:half]
-        send_ref[pl.ds(0, half), at_block(b)] = dw[b][half:].astype(BF16)
-        send_ref[pl.ds(half, half), at_block(b)] = dr[b][half:].astype(BF16)
+        at = at_block(b)
+        dr = dr_ref[:, at]
+        dw = dw_ref[:, at]
+        for lo in range(0, cols, TILE):
+            here = pl.ds(lo, TILE)
+            s = (both_ref[1, :, here].astype(F32) * wide_ref[b : b + 1, here]).astype(BF16)
+            a = (both_ref[0, :, here].astype(F32) * wide_ref[2 + b : 3 + b, here]).astype(BF16)
+            dr += dot(s, qq_ref[1, at, here], nt)
+            dw += dot(a, qq_ref[0, at, here], nt)
+        keep_ref[pl.ds(0, half), at] = dw[:half]
+        keep_ref[pl.ds(half, half), at] = dr[:half]
+        send_ref[pl.ds(0, half), at] = dw[half:].astype(BF16)
+        send_ref[pl.ds(half, half), at] = dr[half:].astype(BF16)
 
 
 def kernel_outer(
-    both_ref, keys_ref, gate_ref, gate_f_ref, in_ref, in_f_ref, step_ref,
-    grad_in_ref, grad_gate_ref, grad_step_ref,
-):
-    grad_step_ref[...] = step_ref[...]
+    both_ref, keys_ref, qq_ref, gate_ref, gate_f_ref, in_ref, in_f_ref,
+    cross_ref, p_ref, q_ref, small_ref, z_ref, rate_ref,
+    grad_in_out, grad_gate_out, grad_step_out,
+    grad_in_ref, grad_gate_ref, step_ref, sems,
+):
     rows, cols = gate_ref.shape
-    for lo in range(0, cols, BLOCK):
-        here = pl.ds(lo, BLOCK)
-        for b in range(2):
-            at = at_block(b)
+    heads = small_ref.shape[1]
+    copies = []
+
+    def leave(src, dst):
+        copies.append(pltpu.make_async_copy(src, dst, sems.at[len(copies)]))
+        copies[-1].start()
+
+    sums = []
+    for b in range(2):
+        at = at_block(b)
+        parts = [[], []]
+        select = []
+        for lo in range(0, cols, TILE):
+            here = pl.ds(lo, TILE)
             v = dot(keys_ref[1, at, :], both_ref[1, :, here])
             z = dot(keys_ref[0, at, :], both_ref[0, :, here])
             grad_gate_ref[at, here] = (
@@ -394,6 +394,27 @@
             grad_in_ref[at, here] = (
                 in_ref[at, here].astype(F32) + in_f_ref[at, here].astype(F32) * z
             ).astype(BF16)
+            for side, got in enumerate((z, v)):
+                parts[side] += pieces(qq_ref[side, at, here].astype(F32) * got, 2)
+            select += [selector(heads, lo, TILE)] * 2
+        leave(grad_gate_ref.at[at], grad_gate_out.at[at])
+        leave(grad_in_ref.at[at], grad_in_out.at[at])
+        select = jnp.concatenate(select, axis=0)
+        sums.append([
+            dot(jnp.concatenate(parts[side], axis=1), select)
+            * small_ref[(2 if side == 0 else 0) + b : (3 if side == 0 else 1) + b]
+            for side in range(2)
+        ])
+    q, p = (jnp.concatenate([sums[b][side] for b in range(2)], axis=0) for side in range(2))
+    ends = jnp.sum(q, axis=0, keepdims=True) + small_ref[5:6] * cross_ref[0:1]
+    q = q + q_ref[...]
+    flow = split_dot_left(triangle(rows, False), p + p_ref[...] - q, 3) + ends
+    z = z_ref[...]
+    grad = (q / softplus(z) - jnp.exp(rate_ref[...]) * flow) / (1.0 + jnp.exp(-z))
+    step_ref[...] = grad.T
+    leave(step_ref, grad_step_out)
+    for copy in copies:
+        copy.wait()
 
 
 def kernel_add(a_ref, b_ref, c_ref, d_ref, out_ref):
@@ -482,43 +503,34 @@
     )
     got_e = exchange(send_e, "context", 3)
     got_f = exchange(send_f, "context", 1)
-    gate, gate_f, inp, inp_f, dr, dw, keys, p, q, skips = call(
+    got_h = exchange(send_e, "context", 2)
+    state = ((2, STATE, cols), BF16)
+    gate, gate_f, inp, inp_f, dr, dw, keys, p, q, probe, local = call(
         kernel_within,
-        [big] * 4 + [((STATE, rows), F32)] * 2 + [((2, rows, STATE), BF16), thin, thin, tiny],
-        [x, g, dy, skip, turned, qq, al, be, wide],
+        [big] * 4 + [((STATE, rows), F32)] * 2
+        + [((2, rows, STATE), BF16), thin, thin, ((2, 2, STATE, cols), F32), tiny],
+        [x, g, dy, skip, turned, qq, al, be, wide, z, rate, small],
         [V((rows, cols), F32)] * 2 + [V((8, cols), F32)],
         us=4.0,
     )
-    (got_e,) = call(
-        kernel_after, [payload], [got_e, skips],
-        spaces=[ANY, ANY], out_spaces=[ANY], alias={0: 0}, us=0.01,
-    )
-    got_h = exchange(got_e, "context", 1)
-    pe, pf, cross = call(
-        kernel_early, [thin, thin, tiny], [got_e, got_f, keys, qq, small], us=2.0
-    )
-    grad_step, sums = call(
-        kernel_steps,
-        [((heads, rows), F32), tiny],
-        [got_h, got_e, got_f, keys, qq, pe, pf, cross, p, q, small, z, rate, skips],
-        us=1.0,
-    )
-    others = [exchange(sums, "context", mask) for mask in (1, 2, 3)]
-    keep, send, ends = call(
-        kernel_keys,
-        [((STATE, rows), F32), ((STATE, rows), BF16), ((2, STATE, cols), BF16)],
-        [got_e, got_f, got_h, qq, wide, dr, dw, sums],
-        [V((8, cols), F32)],
-        us=1.0,
-        spaces=[V] * 7 + [ANY],
+    sums, both, cross = call(
+        kernel_sums, [tiny, state, tiny], [got_e, got_f, got_h, probe, local],
+        [V((8, cols), F32)], us=0.5,
+    )
+    others = [exchange(sums, "context", mask) for mask in (3, 2, 1)]
+    keep, send = call(
+        kernel_keys, [((STATE, rows), F32), ((STATE, rows), BF16)],
+        [both, qq, wide, dr, dw], us=1.0,
     )
     grad_in, grad_gate, grad_step = call(
         kernel_outer, [big, big, ((heads, rows), F32)],
-        [ends, keys, gate, gate_f, inp, inp_f, grad_step], us=2.0,
+        [both, keys, qq, gate, gate_f, inp, inp_f, cross, p, q, small, z, rate],
+        [V((rows, cols), BF16)] * 2 + [V((heads, rows), F32), pltpu.SemaphoreType.DMA((5,))],
+        us=2.0, out_spaces=[pltpu.HBM] * 3,
     )
     (sums,) = call(kernel_add, [tiny], [sums] + others, us=0.1)
     got = exchange(send, "tensor", 1)
-    others = [exchange(sums, "dp", mask) for mask in (1, 2, 3)]
+    others = [exchange(sums, "dp", mask) for mask in (1, 3, 2)]
     grad_w, grad_r, sum_rate, sum_skip, sum_bias = call(
         kernel_finish,
         [((half, rows), F32)] * 2 + [one] * 3,

time: 39.4 us -> 38.1 us (0.967)
  waiting for transfers between devices: 13.5 us -> 5.42 us
  Pallas kernels: 12.4 us -> 18.4 us
  starting transfers between devices: 12.6 us -> 13.4 us
    ppermute x12, waiting for transfers between devices: 13.5 us -> 5.42 us  [exchange(): return lax.ppermute(array, axis, pairs)]
    pallas_call x10 -> x8, Pallas kernels: 12.4 us -> 18.4 us  [call(): pl.pallas_call(kernel, out_shape=[jax.ShapeDtypeStruct(s, d) for s, d in...]
    ppermute x12, starting transfers between devices: 12.6 us -> 13.4 us  [exchange(): return lax.ppermute(array, axis, pairs)]
  transfers between devices with their start and end apart: 12 -> 12, of which waited for: 5 -> 5; matrix products, arithmetic and copies ran while one was open for 0% -> 0% of each run, Pallas kernels for 26% -> 43%
where the time goes in v5:
time: 38.1 us; the launch traced here: 38 us
  Pallas kernels  18.4 us (48%)
  starting transfers between devices  13.4 us (35%)
  waiting for transfers between devices  5.42 us (14%)
  between operations  0.73 us (2%)
    pallas_call x8, Pallas kernels, call(): pl.pallas_call(kernel, out_shape=[jax.ShapeDtypeStruct(s, d) for s, d in...  18.4 us
    ppermute x12, starting transfers between devices, exchange(): return lax.ppermute(array, axis, pairs)  13.4 us
    ppermute x12, waiting for transfers between devices, exchange(): return lax.ppermute(array, axis, pairs)  5.42 us
  transfers between devices with their start and end apart: 12, of which 5 were waited for; matrix products, arithmetic and copies ran while one was open for 0% of the time, Pallas kernels for 43%

profile of v5, /device:TPU:224, one launch (start us, length us, event | category | flops | bytes accessed | tf_op | source)
XLA Modules:
  0.0 38.0 jit_solution(9153701699127371767)
XLA Ops:
  0.6 0.1 collective-permute-start
  0.7 0.5 %collective-permute-start.1 = (bf16[64,256]{1,0:T(8,128)(2,1)}, bf16[64,256]{1,0:T(8,128)(2,1)S(1)}, u32[]{:S(2)}, u32[]{:S(2)}) collective-permute-start(bf16[64,256]{1,0:T(8,128)(2,1)} %bitcast.34), channel_id=1, source_target_pairs={{0,1},{1,0},{2,3},{3,2},{4,5},{5,4},{6,7},{7,6},{8,9},{9,8},{10,11... | collective-permute-start | bytes 98312 | tf_op jit(solution)/shard_map/ppermute | solution.py:460
  1.2 2.2 %shard_map.152 = (bf16[256,1024]{1,0:T(8,128)(2,1)S(1)}, bf16[256,1024]{1,0:T(8,128)(2,1)S(1)}, bf16[256,1024]{1,0:T(8,128)(2,1)S(1)}, bf16[64,256]{1,0:T(8,128)...) custom-call(bf16[256,1024]{1,0:T(8,128)(2,1)} %bitcast.29, ...), custom_call_target="tpu_custom_call" | custom-call | flops 3000000000 | bytes 3000000 | tf_op jit(solution)/shard_map/pallas_call | solution.py:443
  3.4 0.0 collective-permute-done.wt_ref
  3.4 0.0 collective-permute-done.1.rt_ref
  3.4 0.5 %shard_map.153 = (bf16[2,128,256]{2,1,0:T(8,128)(2,1)S(1)}, bf16[1040,128]{1,0:T(8,128)(2,1)S(1)}, bf16[1040,128]{1,0:T(8,128)(2,1)S(1)}) custom-call(bf16[64,256]{1,0:T(8,128)(2,1)S(1)} %get-tuple-element.48.w_ref, bf16[64,256]{1,0:T(8,128)(2,1)S(1)} %collective-permute-done.wt_ref, bf16[64,256]{1,0:T(8,128)(2,1)S(1)} %get-tuple-element.49.r_ref, ...), custom_call_target="tpu_custom_call" | custom-call | flops 3000000000 | bytes 3000000 | tf_op jit(solution)/shard_map/pallas_call | solution.py:443
  4.0 3.1 %collective-permute-start.2 = (bf16[1040,128]{1,0:T(8,128)(2,1)S(1)}, bf16[1040,128]{1,0:T(8,128)(2,1)S(1)}, u32[]{:S(2)}, u32[]{:S(2)}) collective-permute-start(bf16[1040,128]{1,0:T(8,128)(2,1)S(1)} %get-tuple-element.53), channel_id=1, source_target_pairs={{0,48},{16,32},{32,16},{48,0},{1,49},{17,33},{33,17},{49,1},{2,50}... | collective-permute-start | bytes 798728 | tf_op jit(solution)/shard_map/ppermute | solution.py:460
  7.1 0.6 %collective-permute-start.4 = (bf16[1040,128]{1,0:T(8,128)(2,1)S(1)}, bf16[1040,128]{1,0:T(8,128)(2,1)S(1)}, u32[]{:S(2)}, u32[]{:S(2)}) collective-permute-start(bf16[1040,128]{1,0:T(8,128)(2,1)S(1)} %get-tuple-element.53), channel_id=1, source_target_pairs={{0,32},{16,48},{32,0},{48,16},{1,33},{17,49},{33,1},{49,17},{2,34}... | collective-permute-start | bytes 798728 | tf_op jit(solution)/shard_map/ppermute | solution.py:460
  7.7 0.4 %collective-permute-start.3 = (bf16[1040,128]{1,0:T(8,128)(2,1)S(1)}, bf16[1040,128]{1,0:T(8,128)(2,1)S(1)}, u32[]{:S(2)}, u32[]{:S(2)}) collective-permute-start(bf16[1040,128]{1,0:T(8,128)(2,1)S(1)} %get-tuple-element.54), channel_id=1, source_target_pairs={{0,16},{16,0},{32,48},{48,32},{1,17},{17,1},{33,49},{49,33},{2,18}... | collective-permute-start | bytes 798728 | tf_op jit(solution)/shard_map/ppermute | solution.py:460
  8.1 11.2 %shard_map.154 = (bf16[256,1024]{1,0:T(8,128)(2,1)S(1)}, bf16[256,1024]{1,0:T(8,128)(2,1)S(1)}, bf16[256,1024]{1,0:T(8,128)(2,1)S(1)}, bf16[256,1024]{1,0:T(8,12...) custom-call(bf16[256,1024]{1,0:T(8,128)(2,1)S(1)} %get-tuple-element, ...), custom_call_target="tpu_custom_call" | custom-call | flops 4000000000 | bytes 4000000 | tf_op jit(solution)/shard_map/pallas_call | solution.py:443
  19.3 0.1 collective-permute-done.2.e_ref
  19.4 0.0 collective-permute-done.4.h_ref
  19.4 0.7 %collective-permute-done.3.f_ref = bf16[1040,128]{1,0:T(8,128)(2,1)S(1)} collective-permute-done((bf16[1040,128]{1,0:T(8,128)(2,1)S(1)}, bf16[1040,128]{1,0:T(8,128)(2,1)S(1)}, u32[]{:S(2)}, u32[]{:S(2)}) %collective-permute-start.3) | collective-permute-done | bytes 266272 | tf_op jit(solution)/shard_map/ppermute | solution.py:460
  20.1 0.9 %shard_map.155 = (f32[8,16]{1,0:T(8,128)S(1)}, bf16[2,128,1024]{2,1,0:T(8,128)(2,1)S(1)}, f32[8,16]{1,0:T(8,128)S(1)}) custom-call(bf16[1040,128]{1,0:T(8,128)(2,1)S(1)} %collective-permute-done.2.e_ref, bf16[1040,128]{1,0:T(8,128)(2,1)S(1)} %collective-permute-done.3.f_ref, bf16[1040,128]{1,0:T(8,128)(2,1)S(1)} %collective-permute-done.4.h_ref, ...), custom_call_target="tpu_custom_call" | custom-call | flops 500000000 | bytes 500000 | tf_op jit(solution)/shard_map/pallas_call | solution.py:443
  21.1 3.1 %collective-permute-start.6 = (f32[8,16]{1,0:T(8,128)S(1)}, f32[8,16]{1,0:T(8,128)S(1)}, u32[]{:S(2)}, u32[]{:S(2)}) collective-permute-start(f32[8,16]{1,0:T(8,128)S(1)} %get-tuple-element.81.a_ref), channel_id=1, source_target_pairs={{0,48},{16,32},{32,16},{48,0},{1,49},{17,33},{33,17},{49,1},{2,50}... | collective-permute-start | bytes 1544 | tf_op jit(solution)/shard_map/ppermute | solution.py:460
  24.2 0.6 %collective-permute-start.7 = (f32[8,16]{1,0:T(8,128)S(1)}, f32[8,16]{1,0:T(8,128)S(1)}, u32[]{:S(2)}, u32[]{:S(2)}) collective-permute-start(f32[8,16]{1,0:T(8,128)S(1)} %get-tuple-element.81.a_ref), channel_id=1, source_target_pairs={{0,32},{16,48},{32,0},{48,16},{1,33},{17,49},{33,1},{49,17},{2,34}... | collective-permute-start | bytes 1544 | tf_op jit(solution)/shard_map/ppermute | solution.py:460
  24.8 0.6 %collective-permute-start.8 = (f32[8,16]{1,0:T(8,128)S(1)}, f32[8,16]{1,0:T(8,128)S(1)}, u32[]{:S(2)}, u32[]{:S(2)}) collective-permute-start(f32[8,16]{1,0:T(8,128)S(1)} %get-tuple-element.81.a_ref), channel_id=1, source_target_pairs={{0,16},{16,0},{32,48},{48,32},{1,17},{17,1},{33,49},{49,33},{2,18}... | collective-permute-start | bytes 1544 | tf_op jit(solution)/shard_map/ppermute | solution.py:460
  25.4 0.5 %shard_map.157 = (f32[128,256]{1,0:T(8,128)S(1)}, bf16[128,256]{1,0:T(8,128)(2,1)S(1)}) custom-call(bf16[2,128,1024]{2,1,0:T(8,128)(2,1)S(1)} %get-tuple-element.66.both_ref, bf16[2,256,1024]{2,1,0:T(8,128)(2,1)S(1)} %get-tuple-element.50.qq_ref, f32[8,1024]{1,0:T(8,128)S(1)} %get-tuple-element.51.wide_ref, f32[128,256]{1,0:T(8,128)S(1)} %get-tuple-element.77.dr_ref, ...), custom_call_target="tpu_custom_call" | custom-call | flops 1000000000 | bytes 1000000 | tf_op jit(solution)/shard_map/pallas_call | solution.py:443
  25.9 0.1 collective-permute-start.5
  26.0 0.2 collective-permute-done.6.b_ref
  26.2 3.2 %collective-permute-done.7.c_ref = f32[8,16]{1,0:T(8,128)S(1)} collective-permute-done((f32[8,16]{1,0:T(8,128)S(1)}, f32[8,16]{1,0:T(8,128)S(1)}, u32[]{:S(2)}, u32[]{:S(2)}) %collective-permute-start.7) | collective-permute-done | bytes 544 | tf_op jit(solution)/shard_map/ppermute | solution.py:460
  29.3 0.0 collective-permute-done.8.d_ref
  29.3 2.9 %collective-permute-start.10 = (f32[8,16]{1,0:T(8,128)S(1)}, f32[8,16]{1,0:T(8,128)S(1)}, u32[]{:S(2)}, u32[]{:S(2)}) collective-permute-start(f32[8,16]{1,0:T(8,128)S(1)} %shard_map.158.a_ref), channel_id=1, source_target_pairs={{0,192},{64,128},{128,64},{192,0},{1,193},{65,129},{129,65},{193,1... | collective-permute-start | bytes 1544 | tf_op jit(solution)/shard_map/ppermute | solution.py:460
  32.2 0.8 %collective-permute-start.11 = (f32[8,16]{1,0:T(8,128)S(1)}, f32[8,16]{1,0:T(8,128)S(1)}, u32[]{:S(2)}, u32[]{:S(2)}) collective-permute-start(f32[8,16]{1,0:T(8,128)S(1)} %shard_map.158.a_ref), channel_id=1, source_target_pairs={{0,128},{64,192},{128,0},{192,64},{1,129},{65,193},{129,1},{193,65... | collective-permute-start | bytes 1544 | tf_op jit(solution)/shard_map/ppermute | solution.py:460
  33.0 0.5 %collective-permute-start.9 = (f32[8,16]{1,0:T(8,128)S(1)}, f32[8,16]{1,0:T(8,128)S(1)}, u32[]{:S(2)}, u32[]{:S(2)}) collective-permute-start(f32[8,16]{1,0:T(8,128)S(1)} %shard_map.158.a_ref), channel_id=1, source_target_pairs={{0,64},{64,0},{128,192},{192,128},{1,65},{65,1},{129,193},{193,129... | collective-permute-start | bytes 1544 | tf_op jit(solution)/shard_map/ppermute | solution.py:460
  33.5 2.5 %shard_map.156 = (bf16[256,1024]{1,0:T(8,128)(2,1)}, bf16[256,1024]{1,0:T(8,128)(2,1)}, f32[16,256]{1,0:T(8,128)}) custom-call(bf16[2,128,1024]{2,1,0:T(8,128)(2,1)S(1)} %get-tuple-element.66.both_ref, bf16[2,256,128]{2,1,0:T(8,128)(2,1)S(1)} %get-tuple-element.67.keys_ref, bf16[2,256,1024]{2,1,0:T(8,128)(2,1)S(1)} %get-tuple-element.50.qq_ref, ...), custom_call_target="tpu_custom_call" | custom-call | flops 2000000000 | bytes 2000000 | tf_op jit(solution)/shard_map/pallas_call | solution.py:443
  36.0 0.0 collective-permute-done.10.c_ref
  36.0 1.3 %collective-permute-done.11.d_ref = f32[8,16]{1,0:T(8,128)S(1)} collective-permute-done((f32[8,16]{1,0:T(8,128)S(1)}, f32[8,16]{1,0:T(8,128)S(1)}, u32[]{:S(2)}, u32[]{:S(2)}) %collective-permute-start.11) | collective-permute-done | bytes 544 | tf_op jit(solution)/shard_map/ppermute | solution.py:460
  37.3 0.0 collective-permute-done.9.b_ref
  37.3 0.0 collective-permute-done.5.got_ref
  37.3 0.7 %shard_map.159 = (f32[64,256]{1,0:T(8,128)}, f32[64,256]{1,0:T(8,128)}, f32[1,16]{1,0:T(1,128)}, f32[1,16]{1,0:T(1,128)}, f32[1,16]{1,0:T(1,128)}) custom-call(f32[128,256]{1,0:T(8,128)S(1)} %get-tuple-element.79.keep_ref, bf16[128,256]{1,0:T(8,128)(2,1)S(1)} %collective-permute-done.5.got_ref, f32[8,16]{1,0:T(8,128)S(1)} %shard_map.158.a_ref, ...), custom_call_target="tpu_custom_call" | custom-call | flops 200000000 | bytes 200000 | tf_op jit(solution)/shard_map/pallas_call | solution.py:443
  (1 shorter events, 0.0 us)
Async XLA Ops:
  0.6 2.8 %collective-permute-start = (bf16[64,256]{1,0:T(8,128)(2,1)}, bf16[64,256]{1,0:T(8,128)(2,1)S(1)}, u32[]{:S(2)}, u32[]{:S(2)}) collective-permute-start(bf16[64,256]{1,0:T(8,128)(2,1)} %bitcast.32), channel_id=1, source_target_pairs={{0,1},{1,0},{2,3},{3,2},{4,5},{5,4},{6,7},{7,6},{8,9},{9,8},{10,11... | collective-permute-start | bytes 98312 | tf_op jit(solution)/shard_map/ppermute | solution.py:460
  0.7 2.7 %collective-permute-start.1 = (bf16[64,256]{1,0:T(8,128)(2,1)}, bf16[64,256]{1,0:T(8,128)(2,1)S(1)}, u32[]{:S(2)}, u32[]{:S(2)}) collective-permute-start(bf16[64,256]{1,0:T(8,128)(2,1)} %bitcast.34), channel_id=1, source_target_pairs={{0,1},{1,0},{2,3},{3,2},{4,5},{5,4},{6,7},{7,6},{8,9},{9,8},{10,11... | collective-permute-start | bytes 98312 | tf_op jit(solution)/shard_map/ppermute | solution.py:460
  4.0 15.5 %collective-permute-start.2 = (bf16[1040,128]{1,0:T(8,128)(2,1)S(1)}, bf16[1040,128]{1,0:T(8,128)(2,1)S(1)}, u32[]{:S(2)}, u32[]{:S(2)}) collective-permute-start(bf16[1040,128]{1,0:T(8,128)(2,1)S(1)} %get-tuple-element.53), channel_id=1, source_target_pairs={{0,48},{16,32},{32,16},{48,0},{1,49},{17,33},{33,17},{49,1},{2,50}... | collective-permute-start | bytes 798728 | tf_op jit(solution)/shard_map/ppermute | solution.py:460
  7.1 12.4 %collective-permute-start.4 = (bf16[1040,128]{1,0:T(8,128)(2,1)S(1)}, bf16[1040,128]{1,0:T(8,128)(2,1)S(1)}, u32[]{:S(2)}, u32[]{:S(2)}) collective-permute-start(bf16[1040,128]{1,0:T(8,128)(2,1)S(1)} %get-tuple-element.53), channel_id=1, source_target_pairs={{0,32},{16,48},{32,0},{48,16},{1,33},{17,49},{33,1},{49,17},{2,34}... | collective-permute-start | bytes 798728 | tf_op jit(solution)/shard_map/ppermute | solution.py:460
  7.7 12.4 %collective-permute-start.3 = (bf16[1040,128]{1,0:T(8,128)(2,1)S(1)}, bf16[1040,128]{1,0:T(8,128)(2,1)S(1)}, u32[]{:S(2)}, u32[]{:S(2)}) collective-permute-start(bf16[1040,128]{1,0:T(8,128)(2,1)S(1)} %get-tuple-element.54), channel_id=1, source_target_pairs={{0,16},{16,0},{32,48},{48,32},{1,17},{17,1},{33,49},{49,33},{2,18}... | collective-permute-start | bytes 798728 | tf_op jit(solution)/shard_map/ppermute | solution.py:460
  21.1 5.1 %collective-permute-start.6 = (f32[8,16]{1,0:T(8,128)S(1)}, f32[8,16]{1,0:T(8,128)S(1)}, u32[]{:S(2)}, u32[]{:S(2)}) collective-permute-start(f32[8,16]{1,0:T(8,128)S(1)} %get-tuple-element.81.a_ref), channel_id=1, source_target_pairs={{0,48},{16,32},{32,16},{48,0},{1,49},{17,33},{33,17},{49,1},{2,50}... | collective-permute-start | bytes 1544 | tf_op jit(solution)/shard_map/ppermute | solution.py:460
  24.2 5.1 %collective-permute-start.7 = (f32[8,16]{1,0:T(8,128)S(1)}, f32[8,16]{1,0:T(8,128)S(1)}, u32[]{:S(2)}, u32[]{:S(2)}) collective-permute-start(f32[8,16]{1,0:T(8,128)S(1)} %get-tuple-element.81.a_ref), channel_id=1, source_target_pairs={{0,32},{16,48},{32,0},{48,16},{1,33},{17,49},{33,1},{49,17},{2,34}... | collective-permute-start | bytes 1544 | tf_op jit(solution)/shard_map/ppermute | solution.py:460
  24.8 4.5 %collective-permute-start.8 = (f32[8,16]{1,0:T(8,128)S(1)}, f32[8,16]{1,0:T(8,128)S(1)}, u32[]{:S(2)}, u32[]{:S(2)}) collective-permute-start(f32[8,16]{1,0:T(8,128)S(1)} %get-tuple-element.81.a_ref), channel_id=1, source_target_pairs={{0,16},{16,0},{32,48},{48,32},{1,17},{17,1},{33,49},{49,33},{2,18}... | collective-permute-start | bytes 1544 | tf_op jit(solution)/shard_map/ppermute | solution.py:460
  25.9 11.4 %collective-permute-start.5 = (bf16[128,256]{1,0:T(8,128)(2,1)S(1)}, bf16[128,256]{1,0:T(8,128)(2,1)S(1)}, u32[]{:S(2)}, u32[]{:S(2)}) collective-permute-start(bf16[128,256]{1,0:T(8,128)(2,1)S(1)} %get-tuple-element.80), channel_id=1, source_target_pairs={{0,1},{1,0},{2,3},{3,2},{4,5},{5,4},{6,7},{7,6},{8,9},{9,8},{10,11... | collective-permute-start | bytes 196616 | tf_op jit(solution)/shard_map/ppermute | solution.py:460
  29.3 6.7 %collective-permute-start.10 = (f32[8,16]{1,0:T(8,128)S(1)}, f32[8,16]{1,0:T(8,128)S(1)}, u32[]{:S(2)}, u32[]{:S(2)}) collective-permute-start(f32[8,16]{1,0:T(8,128)S(1)} %shard_map.158.a_ref), channel_id=1, source_target_pairs={{0,192},{64,128},{128,64},{192,0},{1,193},{65,129},{129,65},{193,1... | collective-permute-start | bytes 1544 | tf_op jit(solution)/shard_map/ppermute | solution.py:460
  32.2 5.1 %collective-permute-start.11 = (f32[8,16]{1,0:T(8,128)S(1)}, f32[8,16]{1,0:T(8,128)S(1)}, u32[]{:S(2)}, u32[]{:S(2)}) collective-permute-start(f32[8,16]{1,0:T(8,128)S(1)} %shard_map.158.a_ref), channel_id=1, source_target_pairs={{0,128},{64,192},{128,0},{192,64},{1,129},{65,193},{129,1},{193,65... | collective-permute-start | bytes 1544 | tf_op jit(solution)/shard_map/ppermute | solution.py:460
  33.0 4.3 %collective-permute-start.9 = (f32[8,16]{1,0:T(8,128)S(1)}, f32[8,16]{1,0:T(8,128)S(1)}, u32[]{:S(2)}, u32[]{:S(2)}) collective-permute-start(f32[8,16]{1,0:T(8,128)S(1)} %shard_map.158.a_ref), channel_id=1, source_target_pairs={{0,64},{64,0},{128,192},{192,128},{1,65},{65,1},{129,193},{193,129... | collective-permute-start | bytes 1544 | tf_op jit(solution)/shard_map/ppermute | solution.py:460

commit v6 on v5

--- a/solution.py
+++ b/solution.py
@@ -138,7 +138,8 @@
 
 
 def kernel_states(
-    w_ref, wt_ref, r_ref, rt_ref, qq_ref, wide_ref, small_ref, turned_ref, e_ref, f_ref
+    w_ref, wt_ref, r_ref, rt_ref, qq_ref, wide_ref, small_ref,
+    turned_ref, up_ref, down_ref, h_ref,
 ):
     cols = qq_ref.shape[2]
     blocks = qq_ref.shape[1] // BLOCK
@@ -156,16 +157,19 @@
             part = slice(b * BLOCK, (b + 1) * BLOCK)
             state += dot(writes[:, part], qq_ref[0, at, here]) * wide_ref[2 + b : 3 + b, here]
             adjoint += dot(reads[:, part], qq_ref[1, at, here]) * wide_ref[b : b + 1, here]
-        e_ref[here, :] = jnp.where(place < 2, state, adjoint).astype(BF16)
-        f_ref[here, :] = jnp.where(lax.rem(place, 2) == 0, state, adjoint).astype(BF16)
+        state = state.astype(BF16)
+        adjoint = adjoint.astype(BF16)
+        up_ref[here, :] = jnp.where(place < 3, state, adjoint)
+        down_ref[here, :] = jnp.where(place < 1, state, adjoint)
+        h_ref[here, :] = jnp.where(place < 2, state, adjoint)
     heads = small_ref.shape[1]
     total = jnp.concatenate(
         [small_ref[5:6], jnp.zeros((1, STATE - heads), F32)], axis=1
     )
     parts = [part.astype(F32) for part in pieces(total, 3)]
     totals = jnp.concatenate(parts + [jnp.zeros((13, STATE), F32)], axis=0).astype(BF16)
-    e_ref[pl.ds(cols, 16), :] = totals
-    f_ref[pl.ds(cols, 16), :] = totals
+    for ref in (up_ref, down_ref, h_ref):
+        ref[pl.ds(cols, 16), :] = totals
 
 
 def kernel_within(
@@ -173,16 +177,29 @@
     small_ref,
     gate_ref, gate_f_ref, in_ref, in_f_ref, dr_ref, dw_ref, keys_ref, p_ref, q_ref, probe_ref,
     local_ref,
-    al_e, be_e, skip_e,
+    spread_ref,
 ):
     rows, cols = x_ref.shape
     heads = skip_ref.shape[1]
-    for lo in range(0, cols, TILE):
-        wide = expander(heads, lo, TILE)
-        here = pl.ds(lo, TILE)
-        al_e[:, here] = split_dot_right(al_ref[...], wide, 2)
-        be_e[:, here] = split_dot_right(be_ref[...], wide, 2)
-        skip_e[:, here] = split_dot_right(jnp.broadcast_to(skip_ref[...], (8, heads)), wide, 3)
+    z = z_ref[...]
+    rate = jnp.exp(rate_ref[...])
+    step = softplus(z)
+    slope = 1.0 / (1.0 + jnp.exp(-z))
+    lower = triangle(rows, True)
+    decayed = split_dot_left(lower, -rate * step, 3)
+    climbed = rate * split_dot_left(lower, slope, 3)
+    direct = slope / step
+    decay_end = decayed[rows - 1 : rows]
+    climb_end = climbed[rows - 1 : rows]
+    thin = jnp.concatenate(
+        [
+            al_ref[...], be_ref[...],
+            decay_end - decayed, direct + climbed - climb_end, decayed, -climbed,
+            jnp.broadcast_to(skip_ref[...], (8, heads)),
+        ],
+        axis=0,
+    )
+    thin = jnp.concatenate(pieces(thin, 2), axis=1)
     nt = ((1,), (1,))
     wt = [turned_ref[0, :, at_block(b)] for b in range(2)]
     rt = [turned_ref[1, :, at_block(b)] for b in range(2)]
@@ -202,12 +219,15 @@
     m00 = jnp.zeros((BLOCK, BLOCK), F32)
     m11 = m00
     m10 = m00
-    p = [jnp.zeros((BLOCK, heads), F32)] * 2
-    q = [jnp.zeros((BLOCK, heads), F32)] * 2
-    skips = jnp.zeros((8, heads), F32)
-    for lo in range(0, cols, BLOCK):
-        here = pl.ds(lo, BLOCK)
-        sel = selector(heads, lo, BLOCK)
+    p_parts, q_parts = [[], []], [[], []]
+    skip_parts, selects, skip_selects = [], [], []
+    for lo in range(0, cols, TILE):
+        here = pl.ds(lo, TILE)
+        wide = expander(heads, lo, TILE)
+        spread_ref[...] = dot(thin, jnp.concatenate([wide, wide], axis=0))
+        sel = selector(heads, lo, TILE)
+        selects += [sel] * 2
+        skip_selects += [sel] * 3
         link = wide_ref[4:5, here]
         xb = [qq_ref[0, at_block(b), here] for b in range(2)]
         ua = [qq_ref[1, at_block(b), here] for b in range(2)]
@@ -216,56 +236,44 @@
         m10 += dot(ua[1], (xb[0].astype(F32) * link).astype(BF16), nt)
         v = [dot(i00, xb[0]), dot(i11, xb[1]) + link * dot(i10, xb[0])]
         z = [dot(t00, ua[0]) + link * dot(t10, ua[1]), dot(t11, ua[1])]
-        skip = skip_e[0:1, here]
+        skip = spread_ref[6 * rows : 6 * rows + 1, :]
+        totals = [[0.0, 0.0], [0.0, 0.0]]
+        products = 0.0
         for b in range(2):
             at = at_block(b)
-            p[b] += split_dot_right(ua[b].astype(F32) * v[b], sel, 2)
-            q[b] += split_dot_right(xb[b].astype(F32) * z[b], sel, 2)
+            xf, uf = xb[b].astype(F32), ua[b].astype(F32)
+            p_parts[b] += pieces(uf * v[b], 2)
+            q_parts[b] += pieces(xf * z[b], 2)
             g = g_ref[at, here].astype(F32)
             dy = dy_ref[at, here].astype(F32)
             x = x_ref[at, here].astype(F32)
             sig = logistic(g)
             u = dy * g * sig
             up = dy * sig * (1.0 + g * (1.0 - sig))
-            al = al_e[at, here]
-            be = be_e[at, here]
+            al = spread_ref[pl.ds(b * BLOCK, BLOCK), :]
+            be = spread_ref[pl.ds(rows + b * BLOCK, BLOCK), :]
             gate_ref[at, here] = (up * (al * v[b] + skip * x)).astype(BF16)
             gate_f_ref[at, here] = (up * al * wide_ref[b : b + 1, here]).astype(BF16)
             in_ref[at, here] = (be * z[b] + skip * u).astype(BF16)
             in_f_ref[at, here] = (be * wide_ref[2 + b : 3 + b, here]).astype(BF16)
-            ux = jnp.sum((u * x).reshape(BLOCK // 8, 8, BLOCK), axis=0)
-            skips += split_dot_right(ux, sel, 3)
-    z = z_ref[...]
-    rate = jnp.exp(rate_ref[...])
-    step = softplus(z)
-    slope = 1.0 / (1.0 + jnp.exp(-z))
-    lower = triangle(rows, True)
-    decayed = split_dot_left(lower, -rate * step, 3)
-    climbed = rate * split_dot_left(lower, slope, 3)
-    direct = slope / step
-    decay_end = decayed[rows - 1 : rows]
-    climb_end = climbed[rows - 1 : rows]
-    weights = [
-        [decay_end - decayed, direct + climbed - climb_end],
-        [decayed, -climbed],
-    ]
-    for side in range(2):
-        turned = [wt, rt][side]
-        for n in range(2):
-            parts = pieces(weights[side][n], 2)
-            for lo in range(0, cols, TILE):
-                here = pl.ds(lo, TILE)
-                wide = expander(heads, lo, TILE)
-                total = jnp.zeros((STATE, TILE), F32)
-                for b in range(2):
-                    part = slice(b * BLOCK, (b + 1) * BLOCK)
-                    weight = sum(dot(v[part], wide) for v in parts)
-                    scaled = qq_ref[side, at_block(b), here].astype(F32) * weight
-                    row = (2 if side == 0 else 0) + b
-                    total += dot(turned[b], scaled.astype(BF16)) * wide_ref[row : row + 1, here]
-                probe_ref[side, n, :, here] = total
-    p = jnp.concatenate(p, axis=0)
-    q = jnp.concatenate(q, axis=0)
+            products += jnp.sum((u * x).reshape(BLOCK // 8, 8, TILE), axis=0)
+            for side, (turned, own) in enumerate(((wt[b], xf), (rt[b], uf))):
+                row = (2 if side == 0 else 0) + b
+                for n in range(2):
+                    weight = spread_ref[pl.ds((2 + 2 * side + n) * rows + b * BLOCK, BLOCK), :]
+                    totals[side][n] += (
+                        dot(turned, (own * weight).astype(BF16)) * wide_ref[row : row + 1, here]
+                    )
+        for side in range(2):
+            for n in range(2):
+                probe_ref[side, n, :, here] = totals[side][n]
+        skip_parts += pieces(products, 3)
+    selects = jnp.concatenate(selects, axis=0)
+    p, q = (
+        jnp.concatenate([dot(jnp.concatenate(v, axis=1), selects) for v in parts], axis=0)
+        for parts in (p_parts, q_parts)
+    )
+    skips = dot(jnp.concatenate(skip_parts, axis=1), jnp.concatenate(skip_selects, axis=0))
     p_ref[...] = p
     q_ref[...] = q
     local = [
@@ -290,7 +298,7 @@
 
 
 def kernel_sums(
-    e_ref, f_ref, h_ref, probe_ref, local_ref,
+    up_ref, down_ref, h_ref, probe_ref, local_ref,
     sums_ref, both_ref, cross_ref,
     coef_e,
 ):
@@ -299,7 +307,9 @@
     place = lax.axis_index("context")
     inner = (place == 1) | (place == 2)
     mine = (place >= 2).astype(jnp.int32)
-    te, tf, th = (total_of(ref, cols, heads) for ref in (e_ref, f_ref, h_ref))
+    even = lax.rem(place, 2) == 0
+    t_up, t_down, th = (total_of(ref, cols, heads) for ref in (up_ref, down_ref, h_ref))
+    te, tf = jnp.where(even, t_up, t_down), jnp.where(even, t_down, t_up)
     coef = jnp.concatenate(
         [jnp.where(inner, 1.0, tf * th), jnp.where(inner, te, tf)] + [jnp.zeros_like(te)] * 6,
         axis=0,
@@ -315,9 +325,10 @@
     rows, select = [], []
     for lo in range(0, cols, BLOCK):
         here = pl.ds(lo, BLOCK)
-        got_f = f_ref[here, :].astype(F32)
+        up, down = up_ref[here, :].astype(F32), down_ref[here, :].astype(F32)
+        got_f = jnp.where(even, down, up)
         x = (
-            e_ref[here, :].astype(F32) * coef_e[0:1, here]
+            jnp.where(even, up, down) * coef_e[0:1, here]
             + h_ref[here, :].astype(F32) * coef_e[1:2, here]
             + jnp.where(inner, 0.0, got_f)
         )
@@ -460,6 +471,11 @@
     return lax.ppermute(array, axis, pairs)
 
 
+def cycle(array, axis, by):
+    count = lax.axis_size(axis)
+    return lax.ppermute(array, axis, [(i, (i + by) % count) for i in range(count)])
+
+
 def body(
     head_inputs,
     gate_inputs,
@@ -496,28 +512,27 @@
         [V((heads, rows), F32), V((1, heads), F32), pltpu.SemaphoreType.DMA((12,))],
         spaces=[pltpu.HBM] * 9,
     )
-    turned, send_e, send_f = call(
+    turned, send_up, send_down, send_h = call(
         kernel_states,
-        [((2, STATE, rows), BF16), payload, payload],
+        [((2, STATE, rows), BF16), payload, payload, payload],
         [w, wt, r, rt, qq, wide, small],
     )
-    got_e = exchange(send_e, "context", 3)
-    got_f = exchange(send_f, "context", 1)
-    got_h = exchange(send_e, "context", 2)
+    got_up, got_down = cycle(send_up, "context", 1), cycle(send_down, "context", -1)
+    got_h = exchange(send_h, "context", 2)
     state = ((2, STATE, cols), BF16)
     gate, gate_f, inp, inp_f, dr, dw, keys, p, q, probe, local = call(
         kernel_within,
         [big] * 4 + [((STATE, rows), F32)] * 2
         + [((2, rows, STATE), BF16), thin, thin, ((2, 2, STATE, cols), F32), tiny],
         [x, g, dy, skip, turned, qq, al, be, wide, z, rate, small],
-        [V((rows, cols), F32)] * 2 + [V((8, cols), F32)],
+        [V((6 * rows + 8, TILE), F32)],
         us=4.0,
     )
     sums, both, cross = call(
-        kernel_sums, [tiny, state, tiny], [got_e, got_f, got_h, probe, local],
+        kernel_sums, [tiny, state, tiny], [got_up, got_down, got_h, probe, local],
         [V((8, cols), F32)], us=0.5,
     )
-    others = [exchange(sums, "context", mask) for mask in (3, 2, 1)]
+    others = [exchange(sums, "context", mask) for mask in (1, 2, 3)]
     keep, send = call(
         kernel_keys, [((STATE, rows), F32), ((STATE, rows), BF16)],
         [both, qq, wide, dr, dw], us=1.0,
@@ -530,7 +545,7 @@
     )
     (sums,) = call(kernel_add, [tiny], [sums] + others, us=0.1)
     got = exchange(send, "tensor", 1)
-    others = [exchange(sums, "dp", mask) for mask in (1, 3, 2)]
+    others = [exchange(sums, "dp", mask) for mask in (1, 2, 3)]
     grad_w, grad_r, sum_rate, sum_skip, sum_bias = call(
         kernel_finish,
         [((half, rows), F32)] * 2 + [one] * 3,

time: 38.1 us -> 37.5 us (0.984)
  Pallas kernels: 18.4 us -> 11.7 us
  waiting for transfers between devices: 5.42 us -> 10.3 us
  starting transfers between devices: 13.4 us -> 14.5 us
    pallas_call x8, Pallas kernels: 18.4 us -> 11.7 us  [call(): pl.pallas_call(kernel, out_shape=[jax.ShapeDtypeStruct(s, d) for s, d in...]
    ppermute x0 -> x2, waiting for transfers between devices: none -> 5.15 us  [cycle(): lax.ppermute(array, axis, [(i, (i + by) % count) for i in range(count)])]
    ppermute x0 -> x2, starting transfers between devices: none -> 3.31 us  [cycle(): lax.ppermute(array, axis, [(i, (i + by) % count) for i in range(count)])]
    ppermute x12 -> x10, starting transfers between devices: 13.4 us -> 11.2 us  [exchange(): return lax.ppermute(array, axis, pairs)]
    ppermute x12 -> x10, waiting for transfers between devices: 5.42 us -> 5.2 us  [exchange(): return lax.ppermute(array, axis, pairs)]
  transfers between devices with their start and end apart: 12 -> 12, of which waited for: 5 -> 5; matrix products, arithmetic and copies ran while one was open for 0% -> 0% of each run, Pallas kernels for 43% -> 26%
where the time goes in v6:
time: 37.5 us; the launch traced here: 37.3 us
  starting transfers between devices  14.5 us (39%)
  Pallas kernels  11.7 us (31%)
  waiting for transfers between devices  10.3 us (27%)
  between operations  0.73 us (2%)
    pallas_call x8, Pallas kernels, call(): pl.pallas_call(kernel, out_shape=[jax.ShapeDtypeStruct(s, d) for s, d in...  11.7 us
    ppermute x10, starting transfers between devices, exchange(): return lax.ppermute(array, axis, pairs)  11.2 us
    ppermute x10, waiting for transfers between devices, exchange(): return lax.ppermute(array, axis, pairs)  5.2 us
    ppermute x2, waiting for transfers between devices, cycle(): lax.ppermute(array, axis, [(i, (i + by) % count) for i in range(count)])  5.15 us
    ppermute x2, starting transfers between devices, cycle(): lax.ppermute(array, axis, [(i, (i + by) % count) for i in range(count)])  3.31 us
  transfers between devices with their start and end apart: 12, of which 5 were waited for; matrix products, arithmetic and copies ran while one was open for 0% of the time, Pallas kernels for 26%

profile of v6, /device:TPU:224, one launch (start us, length us, event | category | flops | bytes accessed | tf_op | source)
XLA Modules:
  0.0 37.3 jit_solution(6695943102955951603)
XLA Ops:
  0.6 0.1 collective-permute-start
  0.7 0.5 %collective-permute-start.1 = (bf16[64,256]{1,0:T(8,128)(2,1)}, bf16[64,256]{1,0:T(8,128)(2,1)S(1)}, u32[]{:S(2)}, u32[]{:S(2)}) collective-permute-start(bf16[64,256]{1,0:T(8,128)(2,1)} %bitcast.34), channel_id=1, source_target_pairs={{0,1},{1,0},{2,3},{3,2},{4,5},{5,4},{6,7},{7,6},{8,9},{9,8},{10,11... | collective-permute-start | bytes 98312 | tf_op jit(solution)/shard_map/ppermute | solution.py:471
  1.2 2.2 %shard_map.152 = (bf16[256,1024]{1,0:T(8,128)(2,1)S(1)}, bf16[256,1024]{1,0:T(8,128)(2,1)S(1)}, bf16[256,1024]{1,0:T(8,128)(2,1)S(1)}, bf16[64,256]{1,0:T(8,128)...) custom-call(bf16[256,1024]{1,0:T(8,128)(2,1)} %bitcast.29, ...), custom_call_target="tpu_custom_call" | custom-call | flops 3000000000 | bytes 3000000 | tf_op jit(solution)/shard_map/pallas_call | solution.py:454
  3.4 0.0 collective-permute-done.wt_ref
  3.4 0.0 collective-permute-done.1.rt_ref
  3.4 0.6 %shard_map.153 = (bf16[2,128,256]{2,1,0:T(8,128)(2,1)S(1)}, bf16[1040,128]{1,0:T(8,128)(2,1)S(1)}, bf16[1040,128]{1,0:T(8,128)(2,1)S(1)}, bf16[1040,128]{1,0:T(8,128)(2,1)S(1)}) custom-call(bf16[64,256]{1,0:T(8,128)(2,1)S(1)} %get-tuple-element.49.w_ref, bf16[64,256]{1,0:T(8,128)(2,1)S(1)} %collective-permute-done.wt_ref, ...), custom_call_target="tpu_custom_call" | custom-call | flops 3000000000 | bytes 3000000 | tf_op jit(solution)/shard_map/pallas_call | solution.py:454
  4.0 1.7 %collective-permute-start.2 = (bf16[1040,128]{1,0:T(8,128)(2,1)S(1)}, bf16[1040,128]{1,0:T(8,128)(2,1)S(1)}, u32[]{:S(2)}, u32[]{:S(2)}) collective-permute-start(bf16[1040,128]{1,0:T(8,128)(2,1)S(1)} %get-tuple-element.54), channel_id=1, source_target_pairs={{0,16},{16,32},{32,48},{48,0},{1,17},{17,33},{33,49},{49,1},{2,18}... | collective-permute-start | bytes 798728 | tf_op jit(solution)/shard_map/ppermute | solution.py:476
  5.7 1.7 %collective-permute-start.3 = (bf16[1040,128]{1,0:T(8,128)(2,1)S(1)}, bf16[1040,128]{1,0:T(8,128)(2,1)S(1)}, u32[]{:S(2)}, u32[]{:S(2)}) collective-permute-start(bf16[1040,128]{1,0:T(8,128)(2,1)S(1)} %get-tuple-element.55), channel_id=1, source_target_pairs={{0,48},{16,0},{32,16},{48,32},{1,49},{17,1},{33,17},{49,33},{2,50}... | collective-permute-start | bytes 798728 | tf_op jit(solution)/shard_map/ppermute | solution.py:476
  7.3 2.0 %collective-permute-start.4 = (bf16[1040,128]{1,0:T(8,128)(2,1)S(1)}, bf16[1040,128]{1,0:T(8,128)(2,1)S(1)}, u32[]{:S(2)}, u32[]{:S(2)}) collective-permute-start(bf16[1040,128]{1,0:T(8,128)(2,1)S(1)} %get-tuple-element.56), channel_id=1, source_target_pairs={{0,32},{16,48},{32,0},{48,16},{1,33},{17,49},{33,1},{49,17},{2,34}... | collective-permute-start | bytes 798728 | tf_op jit(solution)/shard_map/ppermute | solution.py:471
  9.3 4.4 %shard_map.154 = (bf16[256,1024]{1,0:T(8,128)(2,1)S(1)}, bf16[256,1024]{1,0:T(8,128)(2,1)S(1)}, bf16[256,1024]{1,0:T(8,128)(2,1)S(1)}, bf16[256,1024]{1,0:T(8,12...) custom-call(bf16[256,1024]{1,0:T(8,128)(2,1)S(1)} %get-tuple-element, ...), custom_call_target="tpu_custom_call" | custom-call | flops 4000000000 | bytes 4000000 | tf_op jit(solution)/shard_map/pallas_call | solution.py:454
  13.7 0.1 collective-permute-done.2.up_ref
  13.8 5.1 %collective-permute-done.3.down_ref = bf16[1040,128]{1,0:T(8,128)(2,1)S(1)} collective-permute-done((bf16[1040,128]{1,0:T(8,128)(2,1)S(1)}, bf16[1040,128]{1,0:T(8,128)(2,1)S(1)}, u32[]{:S(2)}, u32[]{:S(2)}) %collective-permute-start.3) | collective-permute-done | bytes 266272 | tf_op jit(solution)/shard_map/ppermute | solution.py:476
  18.8 1.8 %collective-permute-done.4.h_ref = bf16[1040,128]{1,0:T(8,128)(2,1)S(1)} collective-permute-done((bf16[1040,128]{1,0:T(8,128)(2,1)S(1)}, bf16[1040,128]{1,0:T(8,128)(2,1)S(1)}, u32[]{:S(2)}, u32[]{:S(2)}) %collective-permute-start.4) | collective-permute-done | bytes 266272 | tf_op jit(solution)/shard_map/ppermute | solution.py:471
  20.6 1.0 %shard_map.155 = (f32[8,16]{1,0:T(8,128)S(1)}, bf16[2,128,1024]{2,1,0:T(8,128)(2,1)S(1)}, f32[8,16]{1,0:T(8,128)S(1)}) custom-call(bf16[1040,128]{1,0:T(8,128)(2,1)S(1)} %collective-permute-done.2.up_ref, bf16[1040,128]{1,0:T(8,128)(2,1)S(1)} %collective-permute-done.3.down_ref, bf16[1040,128]{1,0:T(8,128)(2,1)S(1)} %collective-permute-done.4.h_ref, ...), custom_call_target="tpu_custom_call" | custom-call | flops 500000000 | bytes 500000 | tf_op jit(solution)/shard_map/pallas_call | solution.py:454
  21.6 2.0 %collective-permute-start.8 = (f32[8,16]{1,0:T(8,128)S(1)}, f32[8,16]{1,0:T(8,128)S(1)}, u32[]{:S(2)}, u32[]{:S(2)}) collective-permute-start(f32[8,16]{1,0:T(8,128)S(1)} %get-tuple-element.83.a_ref), channel_id=1, source_target_pairs={{0,48},{16,32},{32,16},{48,0},{1,49},{17,33},{33,17},{49,1},{2,50}... | collective-permute-start | bytes 1544 | tf_op jit(solution)/shard_map/ppermute | solution.py:471
  23.5 1.3 %collective-permute-start.7 = (f32[8,16]{1,0:T(8,128)S(1)}, f32[8,16]{1,0:T(8,128)S(1)}, u32[]{:S(2)}, u32[]{:S(2)}) collective-permute-start(f32[8,16]{1,0:T(8,128)S(1)} %get-tuple-element.83.a_ref), channel_id=1, source_target_pairs={{0,32},{16,48},{32,0},{48,16},{1,33},{17,49},{33,1},{49,17},{2,34}... | collective-permute-start | bytes 1544 | tf_op jit(solution)/shard_map/ppermute | solution.py:471
  24.9 0.9 %collective-permute-start.6 = (f32[8,16]{1,0:T(8,128)S(1)}, f32[8,16]{1,0:T(8,128)S(1)}, u32[]{:S(2)}, u32[]{:S(2)}) collective-permute-start(f32[8,16]{1,0:T(8,128)S(1)} %get-tuple-element.83.a_ref), channel_id=1, source_target_pairs={{0,16},{16,0},{32,48},{48,32},{1,17},{17,1},{33,49},{49,33},{2,18}... | collective-permute-start | bytes 1544 | tf_op jit(solution)/shard_map/ppermute | solution.py:471
  25.8 0.5 %shard_map.157 = (f32[128,256]{1,0:T(8,128)S(1)}, bf16[128,256]{1,0:T(8,128)(2,1)S(1)}) custom-call(bf16[2,128,1024]{2,1,0:T(8,128)(2,1)S(1)} %get-tuple-element.68.both_ref, bf16[2,256,1024]{2,1,0:T(8,128)(2,1)S(1)} %get-tuple-element.51.qq_ref, f32[8,1024]{1,0:T(8,128)S(1)} %get-tuple-element.52.wide_ref, f32[128,256]{1,0:T(8,128)S(1)} %get-tuple-element.79.dr_ref, ...), custom_call_target="tpu_custom_call" | custom-call | flops 1000000000 | bytes 1000000 | tf_op jit(solution)/shard_map/pallas_call | solution.py:454
  26.3 0.3 collective-permute-start.5
  26.6 0.0 collective-permute-done.8.d_ref
  26.6 2.1 %collective-permute-done.7.c_ref = f32[8,16]{1,0:T(8,128)S(1)} collective-permute-done((f32[8,16]{1,0:T(8,128)S(1)}, f32[8,16]{1,0:T(8,128)S(1)}, u32[]{:S(2)}, u32[]{:S(2)}) %collective-permute-start.7) | collective-permute-done | bytes 544 | tf_op jit(solution)/shard_map/ppermute | solution.py:471
  28.7 0.0 collective-permute-done.6.b_ref
  28.7 2.9 %collective-permute-start.11 = (f32[8,16]{1,0:T(8,128)S(1)}, f32[8,16]{1,0:T(8,128)S(1)}, u32[]{:S(2)}, u32[]{:S(2)}) collective-permute-start(f32[8,16]{1,0:T(8,128)S(1)} %shard_map.158.a_ref), channel_id=1, source_target_pairs={{0,192},{64,128},{128,64},{192,0},{1,193},{65,129},{129,65},{193,1... | collective-permute-start | bytes 1544 | tf_op jit(solution)/shard_map/ppermute | solution.py:471
  31.5 0.8 %collective-permute-start.10 = (f32[8,16]{1,0:T(8,128)S(1)}, f32[8,16]{1,0:T(8,128)S(1)}, u32[]{:S(2)}, u32[]{:S(2)}) collective-permute-start(f32[8,16]{1,0:T(8,128)S(1)} %shard_map.158.a_ref), channel_id=1, source_target_pairs={{0,128},{64,192},{128,0},{192,64},{1,129},{65,193},{129,1},{193,65... | collective-permute-start | bytes 1544 | tf_op jit(solution)/shard_map/ppermute | solution.py:471
  32.3 0.5 %collective-permute-start.9 = (f32[8,16]{1,0:T(8,128)S(1)}, f32[8,16]{1,0:T(8,128)S(1)}, u32[]{:S(2)}, u32[]{:S(2)}) collective-permute-start(f32[8,16]{1,0:T(8,128)S(1)} %shard_map.158.a_ref), channel_id=1, source_target_pairs={{0,64},{64,0},{128,192},{192,128},{1,65},{65,1},{129,193},{193,129... | collective-permute-start | bytes 1544 | tf_op jit(solution)/shard_map/ppermute | solution.py:471
  32.9 2.5 %shard_map.156 = (bf16[256,1024]{1,0:T(8,128)(2,1)}, bf16[256,1024]{1,0:T(8,128)(2,1)}, f32[16,256]{1,0:T(8,128)}) custom-call(bf16[2,128,1024]{2,1,0:T(8,128)(2,1)S(1)} %get-tuple-element.68.both_ref, bf16[2,256,128]{2,1,0:T(8,128)(2,1)S(1)} %get-tuple-element.69.keys_ref, bf16[2,256,1024]{2,1,0:T(8,128)(2,1)S(1)} %get-tuple-element.51.qq_ref, ...), custom_call_target="tpu_custom_call" | custom-call | flops 2000000000 | bytes 2000000 | tf_op jit(solution)/shard_map/pallas_call | solution.py:454
  35.3 0.0 collective-permute-done.11.d_ref
  35.4 1.3 %collective-permute-done.10.c_ref = f32[8,16]{1,0:T(8,128)S(1)} collective-permute-done((f32[8,16]{1,0:T(8,128)S(1)}, f32[8,16]{1,0:T(8,128)S(1)}, u32[]{:S(2)}, u32[]{:S(2)}) %collective-permute-start.10) | collective-permute-done | bytes 544 | tf_op jit(solution)/shard_map/ppermute | solution.py:471
  36.6 0.0 collective-permute-done.9.b_ref
  36.6 0.0 collective-permute-done.5.got_ref
  36.6 0.7 %shard_map.159 = (f32[64,256]{1,0:T(8,128)}, f32[64,256]{1,0:T(8,128)}, f32[1,16]{1,0:T(1,128)}, f32[1,16]{1,0:T(1,128)}, f32[1,16]{1,0:T(1,128)}) custom-call(f32[128,256]{1,0:T(8,128)S(1)} %get-tuple-element.81.keep_ref, bf16[128,256]{1,0:T(8,128)(2,1)S(1)} %collective-permute-done.5.got_ref, f32[8,16]{1,0:T(8,128)S(1)} %shard_map.158.a_ref, ...), custom_call_target="tpu_custom_call" | custom-call | flops 200000000 | bytes 200000 | tf_op jit(solution)/shard_map/pallas_call | solution.py:454
  (1 shorter events, 0.0 us)
Async XLA Ops:
  0.6 2.8 %collective-permute-start = (bf16[64,256]{1,0:T(8,128)(2,1)}, bf16[64,256]{1,0:T(8,128)(2,1)S(1)}, u32[]{:S(2)}, u32[]{:S(2)}) collective-permute-start(bf16[64,256]{1,0:T(8,128)(2,1)} %bitcast.32), channel_id=1, source_target_pairs={{0,1},{1,0},{2,3},{3,2},{4,5},{5,4},{6,7},{7,6},{8,9},{9,8},{10,11... | collective-permute-start | bytes 98312 | tf_op jit(solution)/shard_map/ppermute | solution.py:471
  0.7 2.7 %collective-permute-start.1 = (bf16[64,256]{1,0:T(8,128)(2,1)}, bf16[64,256]{1,0:T(8,128)(2,1)S(1)}, u32[]{:S(2)}, u32[]{:S(2)}) collective-permute-start(bf16[64,256]{1,0:T(8,128)(2,1)} %bitcast.34), channel_id=1, source_target_pairs={{0,1},{1,0},{2,3},{3,2},{4,5},{5,4},{6,7},{7,6},{8,9},{9,8},{10,11... | collective-permute-start | bytes 98312 | tf_op jit(solution)/shard_map/ppermute | solution.py:471
  4.0 9.8 %collective-permute-start.2 = (bf16[1040,128]{1,0:T(8,128)(2,1)S(1)}, bf16[1040,128]{1,0:T(8,128)(2,1)S(1)}, u32[]{:S(2)}, u32[]{:S(2)}) collective-permute-start(bf16[1040,128]{1,0:T(8,128)(2,1)S(1)} %get-tuple-element.54), channel_id=1, source_target_pairs={{0,16},{16,32},{32,48},{48,0},{1,17},{17,33},{33,49},{49,1},{2,18}... | collective-permute-start | bytes 798728 | tf_op jit(solution)/shard_map/ppermute | solution.py:476
  5.7 13.2 %collective-permute-start.3 = (bf16[1040,128]{1,0:T(8,128)(2,1)S(1)}, bf16[1040,128]{1,0:T(8,128)(2,1)S(1)}, u32[]{:S(2)}, u32[]{:S(2)}) collective-permute-start(bf16[1040,128]{1,0:T(8,128)(2,1)S(1)} %get-tuple-element.55), channel_id=1, source_target_pairs={{0,48},{16,0},{32,16},{48,32},{1,49},{17,1},{33,17},{49,33},{2,50}... | collective-permute-start | bytes 798728 | tf_op jit(solution)/shard_map/ppermute | solution.py:476
  7.3 13.3 %collective-permute-start.4 = (bf16[1040,128]{1,0:T(8,128)(2,1)S(1)}, bf16[1040,128]{1,0:T(8,128)(2,1)S(1)}, u32[]{:S(2)}, u32[]{:S(2)}) collective-permute-start(bf16[1040,128]{1,0:T(8,128)(2,1)S(1)} %get-tuple-element.56), channel_id=1, source_target_pairs={{0,32},{16,48},{32,0},{48,16},{1,33},{17,49},{33,1},{49,17},{2,34}... | collective-permute-start | bytes 798728 | tf_op jit(solution)/shard_map/ppermute | solution.py:471
  21.6 5.0 %collective-permute-start.8 = (f32[8,16]{1,0:T(8,128)S(1)}, f32[8,16]{1,0:T(8,128)S(1)}, u32[]{:S(2)}, u32[]{:S(2)}) collective-permute-start(f32[8,16]{1,0:T(8,128)S(1)} %get-tuple-element.83.a_ref), channel_id=1, source_target_pairs={{0,48},{16,32},{32,16},{48,0},{1,49},{17,33},{33,17},{49,1},{2,50}... | collective-permute-start | bytes 1544 | tf_op jit(solution)/shard_map/ppermute | solution.py:471
  23.5 5.1 %collective-permute-start.7 = (f32[8,16]{1,0:T(8,128)S(1)}, f32[8,16]{1,0:T(8,128)S(1)}, u32[]{:S(2)}, u32[]{:S(2)}) collective-permute-start(f32[8,16]{1,0:T(8,128)S(1)} %get-tuple-element.83.a_ref), channel_id=1, source_target_pairs={{0,32},{16,48},{32,0},{48,16},{1,33},{17,49},{33,1},{49,17},{2,34}... | collective-permute-start | bytes 1544 | tf_op jit(solution)/shard_map/ppermute | solution.py:471
  24.9 3.8 %collective-permute-start.6 = (f32[8,16]{1,0:T(8,128)S(1)}, f32[8,16]{1,0:T(8,128)S(1)}, u32[]{:S(2)}, u32[]{:S(2)}) collective-permute-start(f32[8,16]{1,0:T(8,128)S(1)} %get-tuple-element.83.a_ref), channel_id=1, source_target_pairs={{0,16},{16,0},{32,48},{48,32},{1,17},{17,1},{33,49},{49,33},{2,18}... | collective-permute-start | bytes 1544 | tf_op jit(solution)/shard_map/ppermute | solution.py:471
  26.3 10.4 %collective-permute-start.5 = (bf16[128,256]{1,0:T(8,128)(2,1)S(1)}, bf16[128,256]{1,0:T(8,128)(2,1)S(1)}, u32[]{:S(2)}, u32[]{:S(2)}) collective-permute-start(bf16[128,256]{1,0:T(8,128)(2,1)S(1)} %get-tuple-element.82), channel_id=1, source_target_pairs={{0,1},{1,0},{2,3},{3,2},{4,5},{5,4},{6,7},{7,6},{8,9},{9,8},{10,11... | collective-permute-start | bytes 196616 | tf_op jit(solution)/shard_map/ppermute | solution.py:471
  28.7 6.7 %collective-permute-start.11 = (f32[8,16]{1,0:T(8,128)S(1)}, f32[8,16]{1,0:T(8,128)S(1)}, u32[]{:S(2)}, u32[]{:S(2)}) collective-permute-start(f32[8,16]{1,0:T(8,128)S(1)} %shard_map.158.a_ref), channel_id=1, source_target_pairs={{0,192},{64,128},{128,64},{192,0},{1,193},{65,129},{129,65},{193,1... | collective-permute-start | bytes 1544 | tf_op jit(solution)/shard_map/ppermute | solution.py:471
  31.5 5.1 %collective-permute-start.10 = (f32[8,16]{1,0:T(8,128)S(1)}, f32[8,16]{1,0:T(8,128)S(1)}, u32[]{:S(2)}, u32[]{:S(2)}) collective-permute-start(f32[8,16]{1,0:T(8,128)S(1)} %shard_map.158.a_ref), channel_id=1, source_target_pairs={{0,128},{64,192},{128,0},{192,64},{1,129},{65,193},{129,1},{193,65... | collective-permute-start | bytes 1544 | tf_op jit(solution)/shard_map/ppermute | solution.py:471
  32.3 4.3 %collective-permute-start.9 = (f32[8,16]{1,0:T(8,128)S(1)}, f32[8,16]{1,0:T(8,128)S(1)}, u32[]{:S(2)}, u32[]{:S(2)}) collective-permute-start(f32[8,16]{1,0:T(8,128)S(1)} %shard_map.158.a_ref), channel_id=1, source_target_pairs={{0,64},{64,0},{128,192},{192,128},{1,65},{65,1},{129,193},{193,129... | collective-permute-start | bytes 1544 | tf_op jit(solution)/shard_map/ppermute | solution.py:471

commit v7 on v6

--- a/solution.py
+++ b/solution.py
@@ -113,8 +113,13 @@
     )
     small_ref[...] = small
     small_parts = pieces(small, 3)
-    al_parts = pieces(al, 2)
-    be_parts = pieces(be, 2)
+    halves = [
+        jnp.concatenate(
+            pieces(jnp.concatenate([v[b * BLOCK : (b + 1) * BLOCK] for v in (al, be)], axis=0), 2),
+            axis=1,
+        )
+        for b in range(blocks)
+    ]
     for lo in range(0, cols, TILE):
         wide = expander(heads, lo, TILE)
         wide_ref[:, pl.ds(lo, TILE)] = sum(dot(part, wide) for part in small_parts)
@@ -123,12 +128,11 @@
             for copy in large[b]:
                 copy.wait()
         at = at_block(b)
-        part = slice(b * BLOCK, (b + 1) * BLOCK)
         for lo in range(0, cols, TILE):
             here = pl.ds(lo, TILE)
             wide = expander(heads, lo, TILE)
-            al_tile = sum(dot(v[part], wide) for v in al_parts)
-            be_tile = sum(dot(v[part], wide) for v in be_parts)
+            spread = dot(halves[b], jnp.concatenate([wide, wide], axis=0))
+            al_tile, be_tile = spread[:BLOCK], spread[BLOCK:]
             g = g_ref[at, here].astype(F32)
             u = dy_ref[at, here].astype(F32) * g * logistic(g)
             qq_ref[1, at, here] = (u * al_tile).astype(BF16)
@@ -138,7 +142,7 @@
 
 
 def kernel_states(
-    w_ref, wt_ref, r_ref, rt_ref, qq_ref, wide_ref, small_ref,
+    w_ref, wt_ref, r_ref, rt_ref, qq_ref, wide_ref,
     turned_ref, up_ref, down_ref, h_ref,
 ):
     cols = qq_ref.shape[2]
@@ -148,9 +152,9 @@
     reads = jnp.concatenate([r_ref[...], rt_ref[...]], axis=0)
     turned_ref[0] = writes
     turned_ref[1] = reads
-    for lo in range(0, cols, BLOCK):
-        here = pl.ds(lo, BLOCK)
-        state = jnp.zeros((STATE, BLOCK), F32)
+    for lo in range(0, cols, TILE):
+        here = pl.ds(lo, TILE)
+        state = jnp.zeros((STATE, TILE), F32)
         adjoint = state
         for b in range(blocks):
             at = at_block(b)
@@ -159,15 +163,18 @@
             adjoint += dot(reads[:, part], qq_ref[1, at, here]) * wide_ref[b : b + 1, here]
         state = state.astype(BF16)
         adjoint = adjoint.astype(BF16)
-        up_ref[here, :] = jnp.where(place < 3, state, adjoint)
-        down_ref[here, :] = jnp.where(place < 1, state, adjoint)
-        h_ref[here, :] = jnp.where(place < 2, state, adjoint)
-    heads = small_ref.shape[1]
+        up = jnp.where(place < 3, state, adjoint)
+        down = jnp.where(place < 1, state, adjoint)
+        mid = jnp.where(place < 2, state, adjoint)
+        for k in range(0, TILE, BLOCK):
+            there = pl.ds(lo + k, BLOCK)
+            up_ref[there, :] = up[:, k : k + BLOCK]
+            down_ref[there, :] = down[:, k : k + BLOCK]
+            h_ref[there, :] = mid[:, k : k + BLOCK]
     total = jnp.concatenate(
-        [small_ref[5:6], jnp.zeros((1, STATE - heads), F32)], axis=1
-    )
-    parts = [part.astype(F32) for part in pieces(total, 3)]
-    totals = jnp.concatenate(parts + [jnp.zeros((13, STATE), F32)], axis=0).astype(BF16)
+        [wide_ref[5:6, pl.ds(lo, BLOCK)] for lo in range(0, cols, BLOCK)], axis=0
+    )
+    totals = jnp.concatenate([part.astype(F32) for part in pieces(total, 2)], axis=0).astype(BF16)
     for ref in (up_ref, down_ref, h_ref):
         ref[pl.ds(cols, 16), :] = totals
 
@@ -292,15 +299,14 @@
     dw_ref[:, at_block(1)] = dot(rt[1], m11)
 
 
-def total_of(ref, cols, heads):
+def total_of(ref, cols):
     parts = ref[pl.ds(cols, 16), :].astype(F32)
-    return (parts[0:1] + parts[1:2] + parts[2:3])[:, :heads]
+    return parts[:8] + parts[8:]
 
 
 def kernel_sums(
     up_ref, down_ref, h_ref, probe_ref, local_ref,
     sums_ref, both_ref, cross_ref,
-    coef_e,
 ):
     cols = both_ref.shape[2]
     heads = local_ref.shape[1]
@@ -308,16 +314,15 @@
     inner = (place == 1) | (place == 2)
     mine = (place >= 2).astype(jnp.int32)
     even = lax.rem(place, 2) == 0
-    t_up, t_down, th = (total_of(ref, cols, heads) for ref in (up_ref, down_ref, h_ref))
+    t_up, t_down, th = (total_of(ref, cols) for ref in (up_ref, down_ref, h_ref))
     te, tf = jnp.where(even, t_up, t_down), jnp.where(even, t_down, t_up)
-    coef = jnp.concatenate(
-        [jnp.where(inner, 1.0, tf * th), jnp.where(inner, te, tf)] + [jnp.zeros_like(te)] * 6,
-        axis=0,
-    )
-    coef_parts = pieces(coef, 3)
-    for lo in range(0, cols, TILE):
-        wide = expander(heads, lo, TILE)
-        coef_e[:, pl.ds(lo, TILE)] = sum(dot(part, wide) for part in coef_parts)
+    coef_e = jnp.where(inner, 1.0, tf * th)
+    coef_f = jnp.where(inner, jnp.zeros_like(te), 1.0)
+    coef_h = jnp.where(inner, te, tf)
+    coef_up = jnp.where(even, coef_e, coef_f)
+    coef_down = jnp.where(even, coef_f, coef_e)
+    y_up = jnp.where(inner & ~even, 1.0, 0.0)
+    y_down = jnp.where(inner & even, 1.0, 0.0)
 
     def folded(v):
         return jnp.sum(v.reshape(STATE // 8, 8, BLOCK), axis=0)
@@ -325,14 +330,14 @@
     rows, select = [], []
     for lo in range(0, cols, BLOCK):
         here = pl.ds(lo, BLOCK)
+        k = lo // BLOCK
         up, down = up_ref[here, :].astype(F32), down_ref[here, :].astype(F32)
-        got_f = jnp.where(even, down, up)
         x = (
-            jnp.where(even, up, down) * coef_e[0:1, here]
-            + h_ref[here, :].astype(F32) * coef_e[1:2, here]
-            + jnp.where(inner, 0.0, got_f)
+            up * coef_up[k : k + 1]
+            + down * coef_down[k : k + 1]
+            + h_ref[here, :].astype(F32) * coef_h[k : k + 1]
         )
-        y = jnp.where(inner, got_f, 0.0)
+        y = up * y_up + down * y_down
         both_ref[mine, :, here] = x.astype(BF16)
         both_ref[1 - mine, :, here] = y.astype(BF16)
         products = [
@@ -515,7 +520,7 @@
     turned, send_up, send_down, send_h = call(
         kernel_states,
         [((2, STATE, rows), BF16), payload, payload, payload],
-        [w, wt, r, rt, qq, wide, small],
+        [w, wt, r, rt, qq, wide],
     )
     got_up, got_down = cycle(send_up, "context", 1), cycle(send_down, "context", -1)
     got_h = exchange(send_h, "context", 2)
@@ -529,8 +534,7 @@
         us=4.0,
     )
     sums, both, cross = call(
-        kernel_sums, [tiny, state, tiny], [got_up, got_down, got_h, probe, local],
-        [V((8, cols), F32)], us=0.5,
+        kernel_sums, [tiny, state, tiny], [got_up, got_down, got_h, probe, local], us=0.5,
     )
     others = [exchange(sums, "context", mask) for mask in (1, 2, 3)]
     keep, send = call(

time: 37.5 us -> 37.1 us (0.989)
  Pallas kernels: 11.7 us -> 11.3 us
    pallas_call x8, Pallas kernels: 11.7 us -> 11.3 us  [call(): pl.pallas_call(kernel, out_shape=[jax.ShapeDtypeStruct(s, d) for s, d in...]
  transfers between devices with their start and end apart: 12 -> 12, of which waited for: 5 -> 5; matrix products, arithmetic and copies ran while one was open for 0% -> 0% of each run, Pallas kernels for 26% -> 25%
where the time goes in v7:
time: 37.1 us; the launch traced here: 36.9 us
  starting transfers between devices  14.5 us (39%)
  Pallas kernels  11.3 us (30%)
  waiting for transfers between devices  10.3 us (28%)
  between operations  0.73 us (2%)
    pallas_call x8, Pallas kernels, call(): pl.pallas_call(kernel, out_shape=[jax.ShapeDtypeStruct(s, d) for s, d in...  11.3 us
    ppermute x10, starting transfers between devices, exchange(): return lax.ppermute(array, axis, pairs)  11.2 us
    ppermute x10, waiting for transfers between devices, exchange(): return lax.ppermute(array, axis, pairs)  5.19 us
    ppermute x2, waiting for transfers between devices, cycle(): lax.ppermute(array, axis, [(i, (i + by) % count) for i in range(count)])  5.15 us
    ppermute x2, starting transfers between devices, cycle(): lax.ppermute(array, axis, [(i, (i + by) % count) for i in range(count)])  3.31 us
  transfers between devices with their start and end apart: 12, of which 5 were waited for; matrix products, arithmetic and copies ran while one was open for 0% of the time, Pallas kernels for 25%

profile of v7, /device:TPU:224, one launch (start us, length us, event | category | flops | bytes accessed | tf_op | source)
XLA Modules:
  0.0 36.9 jit_solution(9378325696560272529)
XLA Ops:
  0.6 0.1 collective-permute-start
  0.7 0.5 %collective-permute-start.1 = (bf16[64,256]{1,0:T(8,128)(2,1)}, bf16[64,256]{1,0:T(8,128)(2,1)S(1)}, u32[]{:S(2)}, u32[]{:S(2)}) collective-permute-start(bf16[64,256]{1,0:T(8,128)(2,1)} %bitcast.34), channel_id=1, source_target_pairs={{0,1},{1,0},{2,3},{3,2},{4,5},{5,4},{6,7},{7,6},{8,9},{9,8},{10,11... | collective-permute-start | bytes 98312 | tf_op jit(solution)/shard_map/ppermute | solution.py:476
  1.2 1.9 %shard_map.152 = (bf16[256,1024]{1,0:T(8,128)(2,1)S(1)}, bf16[256,1024]{1,0:T(8,128)(2,1)S(1)}, bf16[256,1024]{1,0:T(8,128)(2,1)S(1)}, bf16[64,256]{1,0:T(8,128)...) custom-call(bf16[256,1024]{1,0:T(8,128)(2,1)} %bitcast.29, ...), custom_call_target="tpu_custom_call" | custom-call | flops 3000000000 | bytes 3000000 | tf_op jit(solution)/shard_map/pallas_call | solution.py:459
  3.2 0.0 collective-permute-done.wt_ref
  3.2 0.0 collective-permute-done.1.rt_ref
  3.2 0.5 %shard_map.153 = (bf16[2,128,256]{2,1,0:T(8,128)(2,1)S(1)}, bf16[1040,128]{1,0:T(8,128)(2,1)S(1)}, bf16[1040,128]{1,0:T(8,128)(2,1)S(1)}, bf16[1040,128]{1,0:T(8,128)(2,1)S(1)}) custom-call(bf16[64,256]{1,0:T(8,128)(2,1)S(1)} %get-tuple-element.49.w_ref, bf16[64,256]{1,0:T(8,128)(2,1)S(1)} %collective-permute-done.wt_ref, ...), custom_call_target="tpu_custom_call" | custom-call | flops 3000000000 | bytes 3000000 | tf_op jit(solution)/shard_map/pallas_call | solution.py:459
  3.7 1.7 %collective-permute-start.2 = (bf16[1040,128]{1,0:T(8,128)(2,1)S(1)}, bf16[1040,128]{1,0:T(8,128)(2,1)S(1)}, u32[]{:S(2)}, u32[]{:S(2)}) collective-permute-start(bf16[1040,128]{1,0:T(8,128)(2,1)S(1)} %get-tuple-element.53), channel_id=1, source_target_pairs={{0,16},{16,32},{32,48},{48,0},{1,17},{17,33},{33,49},{49,1},{2,18}... | collective-permute-start | bytes 798728 | tf_op jit(solution)/shard_map/ppermute | solution.py:481
  5.3 1.7 %collective-permute-start.3 = (bf16[1040,128]{1,0:T(8,128)(2,1)S(1)}, bf16[1040,128]{1,0:T(8,128)(2,1)S(1)}, u32[]{:S(2)}, u32[]{:S(2)}) collective-permute-start(bf16[1040,128]{1,0:T(8,128)(2,1)S(1)} %get-tuple-element.54), channel_id=1, source_target_pairs={{0,48},{16,0},{32,16},{48,32},{1,49},{17,1},{33,17},{49,33},{2,50}... | collective-permute-start | bytes 798728 | tf_op jit(solution)/shard_map/ppermute | solution.py:481
  7.0 2.0 %collective-permute-start.4 = (bf16[1040,128]{1,0:T(8,128)(2,1)S(1)}, bf16[1040,128]{1,0:T(8,128)(2,1)S(1)}, u32[]{:S(2)}, u32[]{:S(2)}) collective-permute-start(bf16[1040,128]{1,0:T(8,128)(2,1)S(1)} %get-tuple-element.55), channel_id=1, source_target_pairs={{0,32},{16,48},{32,0},{48,16},{1,33},{17,49},{33,1},{49,17},{2,34}... | collective-permute-start | bytes 798728 | tf_op jit(solution)/shard_map/ppermute | solution.py:476
  9.0 4.4 %shard_map.154 = (bf16[256,1024]{1,0:T(8,128)(2,1)S(1)}, bf16[256,1024]{1,0:T(8,128)(2,1)S(1)}, bf16[256,1024]{1,0:T(8,128)(2,1)S(1)}, bf16[256,1024]{1,0:T(8,12...) custom-call(bf16[256,1024]{1,0:T(8,128)(2,1)S(1)} %get-tuple-element, ...), custom_call_target="tpu_custom_call" | custom-call | flops 4000000000 | bytes 4000000 | tf_op jit(solution)/shard_map/pallas_call | solution.py:459
  13.3 0.1 collective-permute-done.2.up_ref
  13.4 5.1 %collective-permute-done.3.down_ref = bf16[1040,128]{1,0:T(8,128)(2,1)S(1)} collective-permute-done((bf16[1040,128]{1,0:T(8,128)(2,1)S(1)}, bf16[1040,128]{1,0:T(8,128)(2,1)S(1)}, u32[]{:S(2)}, u32[]{:S(2)}) %collective-permute-start.3) | collective-permute-done | bytes 266272 | tf_op jit(solution)/shard_map/ppermute | solution.py:481
  18.5 1.8 %collective-permute-done.4.h_ref = bf16[1040,128]{1,0:T(8,128)(2,1)S(1)} collective-permute-done((bf16[1040,128]{1,0:T(8,128)(2,1)S(1)}, bf16[1040,128]{1,0:T(8,128)(2,1)S(1)}, u32[]{:S(2)}, u32[]{:S(2)}) %collective-permute-start.4) | collective-permute-done | bytes 266272 | tf_op jit(solution)/shard_map/ppermute | solution.py:476
  20.3 0.9 %shard_map.155 = (f32[8,16]{1,0:T(8,128)S(1)}, bf16[2,128,1024]{2,1,0:T(8,128)(2,1)S(1)}, f32[8,16]{1,0:T(8,128)S(1)}) custom-call(bf16[1040,128]{1,0:T(8,128)(2,1)S(1)} %collective-permute-done.2.up_ref, bf16[1040,128]{1,0:T(8,128)(2,1)S(1)} %collective-permute-done.3.down_ref, bf16[1040,128]{1,0:T(8,128)(2,1)S(1)} %collective-permute-done.4.h_ref, ...), custom_call_target="tpu_custom_call" | custom-call | flops 500000000 | bytes 500000 | tf_op jit(solution)/shard_map/pallas_call | solution.py:459
  21.2 2.0 %collective-permute-start.8 = (f32[8,16]{1,0:T(8,128)S(1)}, f32[8,16]{1,0:T(8,128)S(1)}, u32[]{:S(2)}, u32[]{:S(2)}) collective-permute-start(f32[8,16]{1,0:T(8,128)S(1)} %get-tuple-element.83.a_ref), channel_id=1, source_target_pairs={{0,48},{16,32},{32,16},{48,0},{1,49},{17,33},{33,17},{49,1},{2,50}... | collective-permute-start | bytes 1544 | tf_op jit(solution)/shard_map/ppermute | solution.py:476
  23.2 1.3 %collective-permute-start.7 = (f32[8,16]{1,0:T(8,128)S(1)}, f32[8,16]{1,0:T(8,128)S(1)}, u32[]{:S(2)}, u32[]{:S(2)}) collective-permute-start(f32[8,16]{1,0:T(8,128)S(1)} %get-tuple-element.83.a_ref), channel_id=1, source_target_pairs={{0,32},{16,48},{32,0},{48,16},{1,33},{17,49},{33,1},{49,17},{2,34}... | collective-permute-start | bytes 1544 | tf_op jit(solution)/shard_map/ppermute | solution.py:476
  24.5 0.9 %collective-permute-start.6 = (f32[8,16]{1,0:T(8,128)S(1)}, f32[8,16]{1,0:T(8,128)S(1)}, u32[]{:S(2)}, u32[]{:S(2)}) collective-permute-start(f32[8,16]{1,0:T(8,128)S(1)} %get-tuple-element.83.a_ref), channel_id=1, source_target_pairs={{0,16},{16,0},{32,48},{48,32},{1,17},{17,1},{33,49},{49,33},{2,18}... | collective-permute-start | bytes 1544 | tf_op jit(solution)/shard_map/ppermute | solution.py:476
  25.4 0.5 %shard_map.157 = (f32[128,256]{1,0:T(8,128)S(1)}, bf16[128,256]{1,0:T(8,128)(2,1)S(1)}) custom-call(bf16[2,128,1024]{2,1,0:T(8,128)(2,1)S(1)} %get-tuple-element.68.both_ref, bf16[2,256,1024]{2,1,0:T(8,128)(2,1)S(1)} %get-tuple-element.51.qq_ref, f32[8,1024]{1,0:T(8,128)S(1)} %get-tuple-element.52.wide_ref, f32[128,256]{1,0:T(8,128)S(1)} %get-tuple-element.79.dr_ref, ...), custom_call_target="tpu_custom_call" | custom-call | flops 1000000000 | bytes 1000000 | tf_op jit(solution)/shard_map/pallas_call | solution.py:459
  25.9 0.3 collective-permute-start.5
  26.2 0.0 collective-permute-done.8.d_ref
  26.2 2.1 %collective-permute-done.7.c_ref = f32[8,16]{1,0:T(8,128)S(1)} collective-permute-done((f32[8,16]{1,0:T(8,128)S(1)}, f32[8,16]{1,0:T(8,128)S(1)}, u32[]{:S(2)}, u32[]{:S(2)}) %collective-permute-start.7) | collective-permute-done | bytes 544 | tf_op jit(solution)/shard_map/ppermute | solution.py:476
  28.3 0.0 collective-permute-done.6.b_ref
  28.3 2.8 %collective-permute-start.11 = (f32[8,16]{1,0:T(8,128)S(1)}, f32[8,16]{1,0:T(8,128)S(1)}, u32[]{:S(2)}, u32[]{:S(2)}) collective-permute-start(f32[8,16]{1,0:T(8,128)S(1)} %shard_map.158.a_ref), channel_id=1, source_target_pairs={{0,192},{64,128},{128,64},{192,0},{1,193},{65,129},{129,65},{193,1... | collective-permute-start | bytes 1544 | tf_op jit(solution)/shard_map/ppermute | solution.py:476
  31.1 0.8 %collective-permute-start.10 = (f32[8,16]{1,0:T(8,128)S(1)}, f32[8,16]{1,0:T(8,128)S(1)}, u32[]{:S(2)}, u32[]{:S(2)}) collective-permute-start(f32[8,16]{1,0:T(8,128)S(1)} %shard_map.158.a_ref), channel_id=1, source_target_pairs={{0,128},{64,192},{128,0},{192,64},{1,129},{65,193},{129,1},{193,65... | collective-permute-start | bytes 1544 | tf_op jit(solution)/shard_map/ppermute | solution.py:476
  31.9 0.5 %collective-permute-start.9 = (f32[8,16]{1,0:T(8,128)S(1)}, f32[8,16]{1,0:T(8,128)S(1)}, u32[]{:S(2)}, u32[]{:S(2)}) collective-permute-start(f32[8,16]{1,0:T(8,128)S(1)} %shard_map.158.a_ref), channel_id=1, source_target_pairs={{0,64},{64,0},{128,192},{192,128},{1,65},{65,1},{129,193},{193,129... | collective-permute-start | bytes 1544 | tf_op jit(solution)/shard_map/ppermute | solution.py:476
  32.5 2.5 %shard_map.156 = (bf16[256,1024]{1,0:T(8,128)(2,1)}, bf16[256,1024]{1,0:T(8,128)(2,1)}, f32[16,256]{1,0:T(8,128)}) custom-call(bf16[2,128,1024]{2,1,0:T(8,128)(2,1)S(1)} %get-tuple-element.68.both_ref, bf16[2,256,128]{2,1,0:T(8,128)(2,1)S(1)} %get-tuple-element.69.keys_ref, bf16[2,256,1024]{2,1,0:T(8,128)(2,1)S(1)} %get-tuple-element.51.qq_ref, ...), custom_call_target="tpu_custom_call" | custom-call | flops 2000000000 | bytes 2000000 | tf_op jit(solution)/shard_map/pallas_call | solution.py:459
  34.9 0.0 collective-permute-done.11.d_ref
  35.0 1.3 %collective-permute-done.10.c_ref = f32[8,16]{1,0:T(8,128)S(1)} collective-permute-done((f32[8,16]{1,0:T(8,128)S(1)}, f32[8,16]{1,0:T(8,128)S(1)}, u32[]{:S(2)}, u32[]{:S(2)}) %collective-permute-start.10) | collective-permute-done | bytes 544 | tf_op jit(solution)/shard_map/ppermute | solution.py:476
  36.2 0.0 collective-permute-done.9.b_ref
  36.2 0.0 collective-permute-done.5.got_ref
  36.2 0.7 %shard_map.159 = (f32[64,256]{1,0:T(8,128)}, f32[64,256]{1,0:T(8,128)}, f32[1,16]{1,0:T(1,128)}, f32[1,16]{1,0:T(1,128)}, f32[1,16]{1,0:T(1,128)}) custom-call(f32[128,256]{1,0:T(8,128)S(1)} %get-tuple-element.81.keep_ref, bf16[128,256]{1,0:T(8,128)(2,1)S(1)} %collective-permute-done.5.got_ref, f32[8,16]{1,0:T(8,128)S(1)} %shard_map.158.a_ref, ...), custom_call_target="tpu_custom_call" | custom-call | flops 200000000 | bytes 200000 | tf_op jit(solution)/shard_map/pallas_call | solution.py:459
  (1 shorter events, 0.0 us)
Async XLA Ops:
  0.6 2.5 %collective-permute-start = (bf16[64,256]{1,0:T(8,128)(2,1)}, bf16[64,256]{1,0:T(8,128)(2,1)S(1)}, u32[]{:S(2)}, u32[]{:S(2)}) collective-permute-start(bf16[64,256]{1,0:T(8,128)(2,1)} %bitcast.32), channel_id=1, source_target_pairs={{0,1},{1,0},{2,3},{3,2},{4,5},{5,4},{6,7},{7,6},{8,9},{9,8},{10,11... | collective-permute-start | bytes 98312 | tf_op jit(solution)/shard_map/ppermute | solution.py:476
  0.7 2.4 %collective-permute-start.1 = (bf16[64,256]{1,0:T(8,128)(2,1)}, bf16[64,256]{1,0:T(8,128)(2,1)S(1)}, u32[]{:S(2)}, u32[]{:S(2)}) collective-permute-start(bf16[64,256]{1,0:T(8,128)(2,1)} %bitcast.34), channel_id=1, source_target_pairs={{0,1},{1,0},{2,3},{3,2},{4,5},{5,4},{6,7},{7,6},{8,9},{9,8},{10,11... | collective-permute-start | bytes 98312 | tf_op jit(solution)/shard_map/ppermute | solution.py:476
  3.7 9.7 %collective-permute-start.2 = (bf16[1040,128]{1,0:T(8,128)(2,1)S(1)}, bf16[1040,128]{1,0:T(8,128)(2,1)S(1)}, u32[]{:S(2)}, u32[]{:S(2)}) collective-permute-start(bf16[1040,128]{1,0:T(8,128)(2,1)S(1)} %get-tuple-element.53), channel_id=1, source_target_pairs={{0,16},{16,32},{32,48},{48,0},{1,17},{17,33},{33,49},{49,1},{2,18}... | collective-permute-start | bytes 798728 | tf_op jit(solution)/shard_map/ppermute | solution.py:481
  5.3 13.2 %collective-permute-start.3 = (bf16[1040,128]{1,0:T(8,128)(2,1)S(1)}, bf16[1040,128]{1,0:T(8,128)(2,1)S(1)}, u32[]{:S(2)}, u32[]{:S(2)}) collective-permute-start(bf16[1040,128]{1,0:T(8,128)(2,1)S(1)} %get-tuple-element.54), channel_id=1, source_target_pairs={{0,48},{16,0},{32,16},{48,32},{1,49},{17,1},{33,17},{49,33},{2,50}... | collective-permute-start | bytes 798728 | tf_op jit(solution)/shard_map/ppermute | solution.py:481
  7.0 13.3 %collective-permute-start.4 = (bf16[1040,128]{1,0:T(8,128)(2,1)S(1)}, bf16[1040,128]{1,0:T(8,128)(2,1)S(1)}, u32[]{:S(2)}, u32[]{:S(2)}) collective-permute-start(bf16[1040,128]{1,0:T(8,128)(2,1)S(1)} %get-tuple-element.55), channel_id=1, source_target_pairs={{0,32},{16,48},{32,0},{48,16},{1,33},{17,49},{33,1},{49,17},{2,34}... | collective-permute-start | bytes 798728 | tf_op jit(solution)/shard_map/ppermute | solution.py:476
  21.2 5.0 %collective-permute-start.8 = (f32[8,16]{1,0:T(8,128)S(1)}, f32[8,16]{1,0:T(8,128)S(1)}, u32[]{:S(2)}, u32[]{:S(2)}) collective-permute-start(f32[8,16]{1,0:T(8,128)S(1)} %get-tuple-element.83.a_ref), channel_id=1, source_target_pairs={{0,48},{16,32},{32,16},{48,0},{1,49},{17,33},{33,17},{49,1},{2,50}... | collective-permute-start | bytes 1544 | tf_op jit(solution)/shard_map/ppermute | solution.py:476
  23.2 5.1 %collective-permute-start.7 = (f32[8,16]{1,0:T(8,128)S(1)}, f32[8,16]{1,0:T(8,128)S(1)}, u32[]{:S(2)}, u32[]{:S(2)}) collective-permute-start(f32[8,16]{1,0:T(8,128)S(1)} %get-tuple-element.83.a_ref), channel_id=1, source_target_pairs={{0,32},{16,48},{32,0},{48,16},{1,33},{17,49},{33,1},{49,17},{2,34}... | collective-permute-start | bytes 1544 | tf_op jit(solution)/shard_map/ppermute | solution.py:476
  24.5 3.8 %collective-permute-start.6 = (f32[8,16]{1,0:T(8,128)S(1)}, f32[8,16]{1,0:T(8,128)S(1)}, u32[]{:S(2)}, u32[]{:S(2)}) collective-permute-start(f32[8,16]{1,0:T(8,128)S(1)} %get-tuple-element.83.a_ref), channel_id=1, source_target_pairs={{0,16},{16,0},{32,48},{48,32},{1,17},{17,1},{33,49},{49,33},{2,18}... | collective-permute-start | bytes 1544 | tf_op jit(solution)/shard_map/ppermute | solution.py:476
  25.9 10.4 %collective-permute-start.5 = (bf16[128,256]{1,0:T(8,128)(2,1)S(1)}, bf16[128,256]{1,0:T(8,128)(2,1)S(1)}, u32[]{:S(2)}, u32[]{:S(2)}) collective-permute-start(bf16[128,256]{1,0:T(8,128)(2,1)S(1)} %get-tuple-element.82), channel_id=1, source_target_pairs={{0,1},{1,0},{2,3},{3,2},{4,5},{5,4},{6,7},{7,6},{8,9},{9,8},{10,11... | collective-permute-start | bytes 196616 | tf_op jit(solution)/shard_map/ppermute | solution.py:476
  28.3 6.7 %collective-permute-start.11 = (f32[8,16]{1,0:T(8,128)S(1)}, f32[8,16]{1,0:T(8,128)S(1)}, u32[]{:S(2)}, u32[]{:S(2)}) collective-permute-start(f32[8,16]{1,0:T(8,128)S(1)} %shard_map.158.a_ref), channel_id=1, source_target_pairs={{0,192},{64,128},{128,64},{192,0},{1,193},{65,129},{129,65},{193,1... | collective-permute-start | bytes 1544 | tf_op jit(solution)/shard_map/ppermute | solution.py:476
  31.1 5.1 %collective-permute-start.10 = (f32[8,16]{1,0:T(8,128)S(1)}, f32[8,16]{1,0:T(8,128)S(1)}, u32[]{:S(2)}, u32[]{:S(2)}) collective-permute-start(f32[8,16]{1,0:T(8,128)S(1)} %shard_map.158.a_ref), channel_id=1, source_target_pairs={{0,128},{64,192},{128,0},{192,64},{1,129},{65,193},{129,1},{193,65... | collective-permute-start | bytes 1544 | tf_op jit(solution)/shard_map/ppermute | solution.py:476
  31.9 4.3 %collective-permute-start.9 = (f32[8,16]{1,0:T(8,128)S(1)}, f32[8,16]{1,0:T(8,128)S(1)}, u32[]{:S(2)}, u32[]{:S(2)}) collective-permute-start(f32[8,16]{1,0:T(8,128)S(1)} %shard_map.158.a_ref), channel_id=1, source_target_pairs={{0,64},{64,0},{128,192},{192,128},{1,65},{65,1},{129,193},{193,129... | collective-permute-start | bytes 1544 | tf_op jit(solution)/shard_map/ppermute | solution.py:476

commit v8 on v7

--- a/solution.py
+++ b/solution.py
@@ -232,9 +232,8 @@
         here = pl.ds(lo, TILE)
         wide = expander(heads, lo, TILE)
         spread_ref[...] = dot(thin, jnp.concatenate([wide, wide], axis=0))
-        sel = selector(heads, lo, TILE)
-        selects += [sel] * 2
-        skip_selects += [sel] * 3
+        selects += [wide] * 2
+        skip_selects += [wide] * 3
         link = wide_ref[4:5, here]
         xb = [qq_ref[0, at_block(b), here] for b in range(2)]
         ua = [qq_ref[1, at_block(b), here] for b in range(2)]
@@ -275,12 +274,12 @@
             for n in range(2):
                 probe_ref[side, n, :, here] = totals[side][n]
         skip_parts += pieces(products, 3)
-    selects = jnp.concatenate(selects, axis=0)
+    selects = jnp.concatenate(selects, axis=1)
     p, q = (
-        jnp.concatenate([dot(jnp.concatenate(v, axis=1), selects) for v in parts], axis=0)
+        jnp.concatenate([dot(jnp.concatenate(v, axis=1), selects, nt) for v in parts], axis=0)
         for parts in (p_parts, q_parts)
     )
-    skips = dot(jnp.concatenate(skip_parts, axis=1), jnp.concatenate(skip_selects, axis=0))
+    skips = dot(jnp.concatenate(skip_parts, axis=1), jnp.concatenate(skip_selects, axis=1), nt)
     p_ref[...] = p
     q_ref[...] = q
     local = [
@@ -346,8 +345,8 @@
         ] + [folded(x * y), jnp.zeros((8, BLOCK), F32)]
         for part in pieces(jnp.concatenate(products, axis=0), 2):
             rows.append(part)
-            select.append(selector(heads, lo, BLOCK))
-    out = dot(jnp.concatenate(rows, axis=1), jnp.concatenate(select, axis=0))
+            select.append(expander(heads, lo, BLOCK))
+    out = dot(jnp.concatenate(rows, axis=1), jnp.concatenate(select, axis=1), ((1,), (1,)))
     rate, bias, cross = (
         jnp.sum(out[8 * n : 8 * n + 8], axis=0, keepdims=True) for n in range(3)
     )
@@ -412,12 +411,12 @@
             ).astype(BF16)
             for side, got in enumerate((z, v)):
                 parts[side] += pieces(qq_ref[side, at, here].astype(F32) * got, 2)
-            select += [selector(heads, lo, TILE)] * 2
+            select += [expander(heads, lo, TILE)] * 2
         leave(grad_gate_ref.at[at], grad_gate_out.at[at])
         leave(grad_in_ref.at[at], grad_in_out.at[at])
-        select = jnp.concatenate(select, axis=0)
+        select = jnp.concatenate(select, axis=1)
         sums.append([
-            dot(jnp.concatenate(parts[side], axis=1), select)
+            dot(jnp.concatenate(parts[side], axis=1), select, ((1,), (1,)))
             * small_ref[(2 if side == 0 else 0) + b : (3 if side == 0 else 1) + b]
             for side in range(2)
         ])

time: 37.1 us -> 37.2 us (level)
  waiting for transfers between devices: 10.3 us -> 10.9 us
  Pallas kernels: 11.3 us -> 10.9 us
    pallas_call x8, Pallas kernels: 11.3 us -> 10.9 us  [call(): pl.pallas_call(kernel, out_shape=[jax.ShapeDtypeStruct(s, d) for s, d in...]
  transfers between devices with their start and end apart: 12 -> 12, of which waited for: 5 -> 6; matrix products, arithmetic and copies ran while one was open for 0% -> 0% of each run, Pallas kernels for 25% -> 24%
where the time goes in v8:
time: 37.2 us; the launch traced here: 37.1 us
  starting transfers between devices  14.5 us (39%)
  Pallas kernels  10.9 us (29%)
  waiting for transfers between devices  10.9 us (29%)
  between operations  0.73 us (2%)
    ppermute x10, starting transfers between devices, exchange(): return lax.ppermute(array, axis, pairs)  11.2 us
    pallas_call x8, Pallas kernels, call(): pl.pallas_call(kernel, out_shape=[jax.ShapeDtypeStruct(s, d) for s, d in...  10.9 us
    ppermute x2, waiting for transfers between devices, cycle(): lax.ppermute(array, axis, [(i, (i + by) % count) for i in range(count)])  5.47 us
    ppermute x10, waiting for transfers between devices, exchange(): return lax.ppermute(array, axis, pairs)  5.42 us
    ppermute x2, starting transfers between devices, cycle(): lax.ppermute(array, axis, [(i, (i + by) % count) for i in range(count)])  3.31 us
  transfers between devices with their start and end apart: 12, of which 6 were waited for; matrix products, arithmetic and copies ran while one was open for 0% of the time, Pallas kernels for 24%

profile of v8, /device:TPU:224, one launch (start us, length us, event | category | flops | bytes accessed | tf_op | source)
XLA Modules:
  0.0 37.1 jit_solution(5380328219465536682)
XLA Ops:
  0.6 0.1 collective-permute-start
  0.7 0.5 %collective-permute-start.1 = (bf16[64,256]{1,0:T(8,128)(2,1)}, bf16[64,256]{1,0:T(8,128)(2,1)S(1)}, u32[]{:S(2)}, u32[]{:S(2)}) collective-permute-start(bf16[64,256]{1,0:T(8,128)(2,1)} %bitcast.34), channel_id=1, source_target_pairs={{0,1},{1,0},{2,3},{3,2},{4,5},{5,4},{6,7},{7,6},{8,9},{9,8},{10,11... | collective-permute-start | bytes 98312 | tf_op jit(solution)/shard_map/ppermute | solution.py:475
  1.2 1.9 %shard_map.152 = (bf16[256,1024]{1,0:T(8,128)(2,1)S(1)}, bf16[256,1024]{1,0:T(8,128)(2,1)S(1)}, bf16[256,1024]{1,0:T(8,128)(2,1)S(1)}, bf16[64,256]{1,0:T(8,128)...) custom-call(bf16[256,1024]{1,0:T(8,128)(2,1)} %bitcast.29, ...), custom_call_target="tpu_custom_call" | custom-call | flops 3000000000 | bytes 3000000 | tf_op jit(solution)/shard_map/pallas_call | solution.py:458
  3.2 0.0 collective-permute-done.wt_ref
  3.2 0.0 collective-permute-done.1.rt_ref
  3.2 0.5 %shard_map.153 = (bf16[2,128,256]{2,1,0:T(8,128)(2,1)S(1)}, bf16[1040,128]{1,0:T(8,128)(2,1)S(1)}, bf16[1040,128]{1,0:T(8,128)(2,1)S(1)}, bf16[1040,128]{1,0:T(8,128)(2,1)S(1)}) custom-call(bf16[64,256]{1,0:T(8,128)(2,1)S(1)} %get-tuple-element.49.w_ref, bf16[64,256]{1,0:T(8,128)(2,1)S(1)} %collective-permute-done.wt_ref, ...), custom_call_target="tpu_custom_call" | custom-call | flops 3000000000 | bytes 3000000 | tf_op jit(solution)/shard_map/pallas_call | solution.py:458
  3.7 1.7 %collective-permute-start.2 = (bf16[1040,128]{1,0:T(8,128)(2,1)S(1)}, bf16[1040,128]{1,0:T(8,128)(2,1)S(1)}, u32[]{:S(2)}, u32[]{:S(2)}) collective-permute-start(bf16[1040,128]{1,0:T(8,128)(2,1)S(1)} %get-tuple-element.53), channel_id=1, source_target_pairs={{0,16},{16,32},{32,48},{48,0},{1,17},{17,33},{33,49},{49,1},{2,18}... | collective-permute-start | bytes 798728 | tf_op jit(solution)/shard_map/ppermute | solution.py:480
  5.3 1.7 %collective-permute-start.3 = (bf16[1040,128]{1,0:T(8,128)(2,1)S(1)}, bf16[1040,128]{1,0:T(8,128)(2,1)S(1)}, u32[]{:S(2)}, u32[]{:S(2)}) collective-permute-start(bf16[1040,128]{1,0:T(8,128)(2,1)S(1)} %get-tuple-element.54), channel_id=1, source_target_pairs={{0,48},{16,0},{32,16},{48,32},{1,49},{17,1},{33,17},{49,33},{2,50}... | collective-permute-start | bytes 798728 | tf_op jit(solution)/shard_map/ppermute | solution.py:480
  7.0 2.0 %collective-permute-start.4 = (bf16[1040,128]{1,0:T(8,128)(2,1)S(1)}, bf16[1040,128]{1,0:T(8,128)(2,1)S(1)}, u32[]{:S(2)}, u32[]{:S(2)}) collective-permute-start(bf16[1040,128]{1,0:T(8,128)(2,1)S(1)} %get-tuple-element.55), channel_id=1, source_target_pairs={{0,32},{16,48},{32,0},{48,16},{1,33},{17,49},{33,1},{49,17},{2,34}... | collective-permute-start | bytes 798728 | tf_op jit(solution)/shard_map/ppermute | solution.py:475
  9.0 4.1 %shard_map.154 = (bf16[256,1024]{1,0:T(8,128)(2,1)S(1)}, bf16[256,1024]{1,0:T(8,128)(2,1)S(1)}, bf16[256,1024]{1,0:T(8,128)(2,1)S(1)}, bf16[256,1024]{1,0:T(8,12...) custom-call(bf16[256,1024]{1,0:T(8,128)(2,1)S(1)} %get-tuple-element, ...), custom_call_target="tpu_custom_call" | custom-call | flops 4000000000 | bytes 4000000 | tf_op jit(solution)/shard_map/pallas_call | solution.py:458
  13.0 0.4 %collective-permute-done.2.up_ref = bf16[1040,128]{1,0:T(8,128)(2,1)S(1)} collective-permute-done((bf16[1040,128]{1,0:T(8,128)(2,1)S(1)}, bf16[1040,128]{1,0:T(8,128)(2,1)S(1)}, u32[]{:S(2)}, u32[]{:S(2)}) %collective-permute-start.2) | collective-permute-done | bytes 266272 | tf_op jit(solution)/shard_map/ppermute | solution.py:480
  13.4 5.1 %collective-permute-done.3.down_ref = bf16[1040,128]{1,0:T(8,128)(2,1)S(1)} collective-permute-done((bf16[1040,128]{1,0:T(8,128)(2,1)S(1)}, bf16[1040,128]{1,0:T(8,128)(2,1)S(1)}, u32[]{:S(2)}, u32[]{:S(2)}) %collective-permute-start.3) | collective-permute-done | bytes 266272 | tf_op jit(solution)/shard_map/ppermute | solution.py:480
  18.5 1.8 %collective-permute-done.4.h_ref = bf16[1040,128]{1,0:T(8,128)(2,1)S(1)} collective-permute-done((bf16[1040,128]{1,0:T(8,128)(2,1)S(1)}, bf16[1040,128]{1,0:T(8,128)(2,1)S(1)}, u32[]{:S(2)}, u32[]{:S(2)}) %collective-permute-start.4) | collective-permute-done | bytes 266272 | tf_op jit(solution)/shard_map/ppermute | solution.py:475
  20.3 0.8 %shard_map.155 = (f32[8,16]{1,0:T(8,128)S(1)}, bf16[2,128,1024]{2,1,0:T(8,128)(2,1)S(1)}, f32[8,16]{1,0:T(8,128)S(1)}) custom-call(bf16[1040,128]{1,0:T(8,128)(2,1)S(1)} %collective-permute-done.2.up_ref, bf16[1040,128]{1,0:T(8,128)(2,1)S(1)} %collective-permute-done.3.down_ref, bf16[1040,128]{1,0:T(8,128)(2,1)S(1)} %collective-permute-done.4.h_ref, ...), custom_call_target="tpu_custom_call" | custom-call | flops 500000000 | bytes 500000 | tf_op jit(solution)/shard_map/pallas_call | solution.py:458
  21.1 2.0 %collective-permute-start.8 = (f32[8,16]{1,0:T(8,128)S(1)}, f32[8,16]{1,0:T(8,128)S(1)}, u32[]{:S(2)}, u32[]{:S(2)}) collective-permute-start(f32[8,16]{1,0:T(8,128)S(1)} %get-tuple-element.83.a_ref), channel_id=1, source_target_pairs={{0,48},{16,32},{32,16},{48,0},{1,49},{17,33},{33,17},{49,1},{2,50}... | collective-permute-start | bytes 1544 | tf_op jit(solution)/shard_map/ppermute | solution.py:475
  23.1 1.3 %collective-permute-start.7 = (f32[8,16]{1,0:T(8,128)S(1)}, f32[8,16]{1,0:T(8,128)S(1)}, u32[]{:S(2)}, u32[]{:S(2)}) collective-permute-start(f32[8,16]{1,0:T(8,128)S(1)} %get-tuple-element.83.a_ref), channel_id=1, source_target_pairs={{0,32},{16,48},{32,0},{48,16},{1,33},{17,49},{33,1},{49,17},{2,34}... | collective-permute-start | bytes 1544 | tf_op jit(solution)/shard_map/ppermute | solution.py:475
  24.4 0.9 %collective-permute-start.6 = (f32[8,16]{1,0:T(8,128)S(1)}, f32[8,16]{1,0:T(8,128)S(1)}, u32[]{:S(2)}, u32[]{:S(2)}) collective-permute-start(f32[8,16]{1,0:T(8,128)S(1)} %get-tuple-element.83.a_ref), channel_id=1, source_target_pairs={{0,16},{16,0},{32,48},{48,32},{1,17},{17,1},{33,49},{49,33},{2,18}... | collective-permute-start | bytes 1544 | tf_op jit(solution)/shard_map/ppermute | solution.py:475
  25.3 0.5 %shard_map.157 = (f32[128,256]{1,0:T(8,128)S(1)}, bf16[128,256]{1,0:T(8,128)(2,1)S(1)}) custom-call(bf16[2,128,1024]{2,1,0:T(8,128)(2,1)S(1)} %get-tuple-element.68.both_ref, bf16[2,256,1024]{2,1,0:T(8,128)(2,1)S(1)} %get-tuple-element.51.qq_ref, f32[8,1024]{1,0:T(8,128)S(1)} %get-tuple-element.52.wide_ref, f32[128,256]{1,0:T(8,128)S(1)} %get-tuple-element.79.dr_ref, ...), custom_call_target="tpu_custom_call" | custom-call | flops 1000000000 | bytes 1000000 | tf_op jit(solution)/shard_map/pallas_call | solution.py:458
  25.8 0.1 collective-permute-start.5
  25.9 0.1 collective-permute-done.8.d_ref
  26.0 2.2 %collective-permute-done.7.c_ref = f32[8,16]{1,0:T(8,128)S(1)} collective-permute-done((f32[8,16]{1,0:T(8,128)S(1)}, f32[8,16]{1,0:T(8,128)S(1)}, u32[]{:S(2)}, u32[]{:S(2)}) %collective-permute-start.7) | collective-permute-done | bytes 544 | tf_op jit(solution)/shard_map/ppermute | solution.py:475
  28.2 0.0 collective-permute-done.6.b_ref
  28.2 3.0 %collective-permute-start.11 = (f32[8,16]{1,0:T(8,128)S(1)}, f32[8,16]{1,0:T(8,128)S(1)}, u32[]{:S(2)}, u32[]{:S(2)}) collective-permute-start(f32[8,16]{1,0:T(8,128)S(1)} %shard_map.158.a_ref), channel_id=1, source_target_pairs={{0,192},{64,128},{128,64},{192,0},{1,193},{65,129},{129,65},{193,1... | collective-permute-start | bytes 1544 | tf_op jit(solution)/shard_map/ppermute | solution.py:475
  31.2 0.8 %collective-permute-start.10 = (f32[8,16]{1,0:T(8,128)S(1)}, f32[8,16]{1,0:T(8,128)S(1)}, u32[]{:S(2)}, u32[]{:S(2)}) collective-permute-start(f32[8,16]{1,0:T(8,128)S(1)} %shard_map.158.a_ref), channel_id=1, source_target_pairs={{0,128},{64,192},{128,0},{192,64},{1,129},{65,193},{129,1},{193,65... | collective-permute-start | bytes 1544 | tf_op jit(solution)/shard_map/ppermute | solution.py:475
  32.0 0.5 %collective-permute-start.9 = (f32[8,16]{1,0:T(8,128)S(1)}, f32[8,16]{1,0:T(8,128)S(1)}, u32[]{:S(2)}, u32[]{:S(2)}) collective-permute-start(f32[8,16]{1,0:T(8,128)S(1)} %shard_map.158.a_ref), channel_id=1, source_target_pairs={{0,64},{64,0},{128,192},{192,128},{1,65},{65,1},{129,193},{193,129... | collective-permute-start | bytes 1544 | tf_op jit(solution)/shard_map/ppermute | solution.py:475
  32.6 2.4 %shard_map.156 = (bf16[256,1024]{1,0:T(8,128)(2,1)}, bf16[256,1024]{1,0:T(8,128)(2,1)}, f32[16,256]{1,0:T(8,128)}) custom-call(bf16[2,128,1024]{2,1,0:T(8,128)(2,1)S(1)} %get-tuple-element.68.both_ref, bf16[2,256,128]{2,1,0:T(8,128)(2,1)S(1)} %get-tuple-element.69.keys_ref, bf16[2,256,1024]{2,1,0:T(8,128)(2,1)S(1)} %get-tuple-element.51.qq_ref, ...), custom_call_target="tpu_custom_call" | custom-call | flops 2000000000 | bytes 2000000 | tf_op jit(solution)/shard_map/pallas_call | solution.py:458
  35.0 0.0 collective-permute-done.11.d_ref
  35.0 1.3 %collective-permute-done.10.c_ref = f32[8,16]{1,0:T(8,128)S(1)} collective-permute-done((f32[8,16]{1,0:T(8,128)S(1)}, f32[8,16]{1,0:T(8,128)S(1)}, u32[]{:S(2)}, u32[]{:S(2)}) %collective-permute-start.10) | collective-permute-done | bytes 544 | tf_op jit(solution)/shard_map/ppermute | solution.py:475
  36.4 0.0 collective-permute-done.9.b_ref
  36.4 0.0 collective-permute-done.5.got_ref
  36.4 0.7 %shard_map.159 = (f32[64,256]{1,0:T(8,128)}, f32[64,256]{1,0:T(8,128)}, f32[1,16]{1,0:T(1,128)}, f32[1,16]{1,0:T(1,128)}, f32[1,16]{1,0:T(1,128)}) custom-call(f32[128,256]{1,0:T(8,128)S(1)} %get-tuple-element.81.keep_ref, bf16[128,256]{1,0:T(8,128)(2,1)S(1)} %collective-permute-done.5.got_ref, f32[8,16]{1,0:T(8,128)S(1)} %shard_map.158.a_ref, ...), custom_call_target="tpu_custom_call" | custom-call | flops 200000000 | bytes 200000 | tf_op jit(solution)/shard_map/pallas_call | solution.py:458
  (1 shorter events, 0.0 us)
Async XLA Ops:
  0.6 2.5 %collective-permute-start = (bf16[64,256]{1,0:T(8,128)(2,1)}, bf16[64,256]{1,0:T(8,128)(2,1)S(1)}, u32[]{:S(2)}, u32[]{:S(2)}) collective-permute-start(bf16[64,256]{1,0:T(8,128)(2,1)} %bitcast.32), channel_id=1, source_target_pairs={{0,1},{1,0},{2,3},{3,2},{4,5},{5,4},{6,7},{7,6},{8,9},{9,8},{10,11... | collective-permute-start | bytes 98312 | tf_op jit(solution)/shard_map/ppermute | solution.py:475
  0.7 2.4 %collective-permute-start.1 = (bf16[64,256]{1,0:T(8,128)(2,1)}, bf16[64,256]{1,0:T(8,128)(2,1)S(1)}, u32[]{:S(2)}, u32[]{:S(2)}) collective-permute-start(bf16[64,256]{1,0:T(8,128)(2,1)} %bitcast.34), channel_id=1, source_target_pairs={{0,1},{1,0},{2,3},{3,2},{4,5},{5,4},{6,7},{7,6},{8,9},{9,8},{10,11... | collective-permute-start | bytes 98312 | tf_op jit(solution)/shard_map/ppermute | solution.py:475
  3.7 9.7 %collective-permute-start.2 = (bf16[1040,128]{1,0:T(8,128)(2,1)S(1)}, bf16[1040,128]{1,0:T(8,128)(2,1)S(1)}, u32[]{:S(2)}, u32[]{:S(2)}) collective-permute-start(bf16[1040,128]{1,0:T(8,128)(2,1)S(1)} %get-tuple-element.53), channel_id=1, source_target_pairs={{0,16},{16,32},{32,48},{48,0},{1,17},{17,33},{33,49},{49,1},{2,18}... | collective-permute-start | bytes 798728 | tf_op jit(solution)/shard_map/ppermute | solution.py:480
  5.3 13.2 %collective-permute-start.3 = (bf16[1040,128]{1,0:T(8,128)(2,1)S(1)}, bf16[1040,128]{1,0:T(8,128)(2,1)S(1)}, u32[]{:S(2)}, u32[]{:S(2)}) collective-permute-start(bf16[1040,128]{1,0:T(8,128)(2,1)S(1)} %get-tuple-element.54), channel_id=1, source_target_pairs={{0,48},{16,0},{32,16},{48,32},{1,49},{17,1},{33,17},{49,33},{2,50}... | collective-permute-start | bytes 798728 | tf_op jit(solution)/shard_map/ppermute | solution.py:480
  7.0 13.3 %collective-permute-start.4 = (bf16[1040,128]{1,0:T(8,128)(2,1)S(1)}, bf16[1040,128]{1,0:T(8,128)(2,1)S(1)}, u32[]{:S(2)}, u32[]{:S(2)}) collective-permute-start(bf16[1040,128]{1,0:T(8,128)(2,1)S(1)} %get-tuple-element.55), channel_id=1, source_target_pairs={{0,32},{16,48},{32,0},{48,16},{1,33},{17,49},{33,1},{49,17},{2,34}... | collective-permute-start | bytes 798728 | tf_op jit(solution)/shard_map/ppermute | solution.py:475
  21.1 4.9 %collective-permute-start.8 = (f32[8,16]{1,0:T(8,128)S(1)}, f32[8,16]{1,0:T(8,128)S(1)}, u32[]{:S(2)}, u32[]{:S(2)}) collective-permute-start(f32[8,16]{1,0:T(8,128)S(1)} %get-tuple-element.83.a_ref), channel_id=1, source_target_pairs={{0,48},{16,32},{32,16},{48,0},{1,49},{17,33},{33,17},{49,1},{2,50}... | collective-permute-start | bytes 1544 | tf_op jit(solution)/shard_map/ppermute | solution.py:475
  23.1 5.1 %collective-permute-start.7 = (f32[8,16]{1,0:T(8,128)S(1)}, f32[8,16]{1,0:T(8,128)S(1)}, u32[]{:S(2)}, u32[]{:S(2)}) collective-permute-start(f32[8,16]{1,0:T(8,128)S(1)} %get-tuple-element.83.a_ref), channel_id=1, source_target_pairs={{0,32},{16,48},{32,0},{48,16},{1,33},{17,49},{33,1},{49,17},{2,34}... | collective-permute-start | bytes 1544 | tf_op jit(solution)/shard_map/ppermute | solution.py:475
  24.4 3.8 %collective-permute-start.6 = (f32[8,16]{1,0:T(8,128)S(1)}, f32[8,16]{1,0:T(8,128)S(1)}, u32[]{:S(2)}, u32[]{:S(2)}) collective-permute-start(f32[8,16]{1,0:T(8,128)S(1)} %get-tuple-element.83.a_ref), channel_id=1, source_target_pairs={{0,16},{16,0},{32,48},{48,32},{1,17},{17,1},{33,49},{49,33},{2,18}... | collective-permute-start | bytes 1544 | tf_op jit(solution)/shard_map/ppermute | solution.py:475
  25.8 10.5 %collective-permute-start.5 = (bf16[128,256]{1,0:T(8,128)(2,1)S(1)}, bf16[128,256]{1,0:T(8,128)(2,1)S(1)}, u32[]{:S(2)}, u32[]{:S(2)}) collective-permute-start(bf16[128,256]{1,0:T(8,128)(2,1)S(1)} %get-tuple-element.82), channel_id=1, source_target_pairs={{0,1},{1,0},{2,3},{3,2},{4,5},{5,4},{6,7},{7,6},{8,9},{9,8},{10,11... | collective-permute-start | bytes 196616 | tf_op jit(solution)/shard_map/ppermute | solution.py:475
  28.2 6.8 %collective-permute-start.11 = (f32[8,16]{1,0:T(8,128)S(1)}, f32[8,16]{1,0:T(8,128)S(1)}, u32[]{:S(2)}, u32[]{:S(2)}) collective-permute-start(f32[8,16]{1,0:T(8,128)S(1)} %shard_map.158.a_ref), channel_id=1, source_target_pairs={{0,192},{64,128},{128,64},{192,0},{1,193},{65,129},{129,65},{193,1... | collective-permute-start | bytes 1544 | tf_op jit(solution)/shard_map/ppermute | solution.py:475
  31.2 5.1 %collective-permute-start.10 = (f32[8,16]{1,0:T(8,128)S(1)}, f32[8,16]{1,0:T(8,128)S(1)}, u32[]{:S(2)}, u32[]{:S(2)}) collective-permute-start(f32[8,16]{1,0:T(8,128)S(1)} %shard_map.158.a_ref), channel_id=1, source_target_pairs={{0,128},{64,192},{128,0},{192,64},{1,129},{65,193},{129,1},{193,65... | collective-permute-start | bytes 1544 | tf_op jit(solution)/shard_map/ppermute | solution.py:475
  32.0 4.3 %collective-permute-start.9 = (f32[8,16]{1,0:T(8,128)S(1)}, f32[8,16]{1,0:T(8,128)S(1)}, u32[]{:S(2)}, u32[]{:S(2)}) collective-permute-start(f32[8,16]{1,0:T(8,128)S(1)} %shard_map.158.a_ref), channel_id=1, source_target_pairs={{0,64},{64,0},{128,192},{192,128},{1,65},{65,1},{129,193},{193,129... | collective-permute-start | bytes 1544 | tf_op jit(solution)/shard_map/ppermute | solution.py:475

commit v9 on v7

--- a/solution.py
+++ b/solution.py
@@ -273,7 +273,7 @@
                     )
         for side in range(2):
             for n in range(2):
-                probe_ref[side, n, :, here] = totals[side][n]
+                probe_ref[side, n, :, here] = totals[side][n].astype(BF16)
         skip_parts += pieces(products, 3)
     selects = jnp.concatenate(selects, axis=0)
     p, q = (
@@ -528,7 +528,7 @@
     gate, gate_f, inp, inp_f, dr, dw, keys, p, q, probe, local = call(
         kernel_within,
         [big] * 4 + [((STATE, rows), F32)] * 2
-        + [((2, rows, STATE), BF16), thin, thin, ((2, 2, STATE, cols), F32), tiny],
+        + [((2, rows, STATE), BF16), thin, thin, ((2, 2, STATE, cols), BF16), tiny],
         [x, g, dy, skip, turned, qq, al, be, wide, z, rate, small],
         [V((6 * rows + 8, TILE), F32)],
         us=4.0,

time: 37.1 us -> 37.2 us (level)
  no operation moved by 1% of the time
where the time goes in v9:
time: 37.2 us; the launch traced here: 37 us
  starting transfers between devices  14.5 us (39%)
  Pallas kernels  11.3 us (30%)
  waiting for transfers between devices  10.4 us (28%)
  between operations  0.73 us (2%)
    pallas_call x8, Pallas kernels, call(): pl.pallas_call(kernel, out_shape=[jax.ShapeDtypeStruct(s, d) for s, d in...  11.3 us
    ppermute x10, starting transfers between devices, exchange(): return lax.ppermute(array, axis, pairs)  11.2 us
    ppermute x2, waiting for transfers between devices, cycle(): lax.ppermute(array, axis, [(i, (i + by) % count) for i in range(count)])  5.2 us
    ppermute x10, waiting for transfers between devices, exchange(): return lax.ppermute(array, axis, pairs)  5.19 us
    ppermute x2, starting transfers between devices, cycle(): lax.ppermute(array, axis, [(i, (i + by) % count) for i in range(count)])  3.31 us
  transfers between devices with their start and end apart: 12, of which 5 were waited for; matrix products, arithmetic and copies ran while one was open for 0% of the time, Pallas kernels for 25%

profile of v9, /device:TPU:224, one launch (start us, length us, event | category | flops | bytes accessed | tf_op | source)
XLA Modules:
  0.0 37.0 jit_solution(2569008871553608580)
XLA Ops:
  0.6 0.1 collective-permute-start
  0.7 0.5 %collective-permute-start.1 = (bf16[64,256]{1,0:T(8,128)(2,1)}, bf16[64,256]{1,0:T(8,128)(2,1)S(1)}, u32[]{:S(2)}, u32[]{:S(2)}) collective-permute-start(bf16[64,256]{1,0:T(8,128)(2,1)} %bitcast.34), channel_id=1, source_target_pairs={{0,1},{1,0},{2,3},{3,2},{4,5},{5,4},{6,7},{7,6},{8,9},{9,8},{10,11... | collective-permute-start | bytes 98312 | tf_op jit(solution)/shard_map/ppermute | solution.py:476
  1.2 1.9 %shard_map.152 = (bf16[256,1024]{1,0:T(8,128)(2,1)S(1)}, bf16[256,1024]{1,0:T(8,128)(2,1)S(1)}, bf16[256,1024]{1,0:T(8,128)(2,1)S(1)}, bf16[64,256]{1,0:T(8,128)...) custom-call(bf16[256,1024]{1,0:T(8,128)(2,1)} %bitcast.29, ...), custom_call_target="tpu_custom_call" | custom-call | flops 3000000000 | bytes 3000000 | tf_op jit(solution)/shard_map/pallas_call | solution.py:459
  3.2 0.0 collective-permute-done.wt_ref
  3.2 0.0 collective-permute-done.1.rt_ref
  3.2 0.5 %shard_map.153 = (bf16[2,128,256]{2,1,0:T(8,128)(2,1)S(1)}, bf16[1040,128]{1,0:T(8,128)(2,1)S(1)}, bf16[1040,128]{1,0:T(8,128)(2,1)S(1)}, bf16[1040,128]{1,0:T(8,128)(2,1)S(1)}) custom-call(bf16[64,256]{1,0:T(8,128)(2,1)S(1)} %get-tuple-element.49.w_ref, bf16[64,256]{1,0:T(8,128)(2,1)S(1)} %collective-permute-done.wt_ref, ...), custom_call_target="tpu_custom_call" | custom-call | flops 3000000000 | bytes 3000000 | tf_op jit(solution)/shard_map/pallas_call | solution.py:459
  3.7 1.7 %collective-permute-start.2 = (bf16[1040,128]{1,0:T(8,128)(2,1)S(1)}, bf16[1040,128]{1,0:T(8,128)(2,1)S(1)}, u32[]{:S(2)}, u32[]{:S(2)}) collective-permute-start(bf16[1040,128]{1,0:T(8,128)(2,1)S(1)} %get-tuple-element.53), channel_id=1, source_target_pairs={{0,16},{16,32},{32,48},{48,0},{1,17},{17,33},{33,49},{49,1},{2,18}... | collective-permute-start | bytes 798728 | tf_op jit(solution)/shard_map/ppermute | solution.py:481
  5.3 1.7 %collective-permute-start.3 = (bf16[1040,128]{1,0:T(8,128)(2,1)S(1)}, bf16[1040,128]{1,0:T(8,128)(2,1)S(1)}, u32[]{:S(2)}, u32[]{:S(2)}) collective-permute-start(bf16[1040,128]{1,0:T(8,128)(2,1)S(1)} %get-tuple-element.54), channel_id=1, source_target_pairs={{0,48},{16,0},{32,16},{48,32},{1,49},{17,1},{33,17},{49,33},{2,50}... | collective-permute-start | bytes 798728 | tf_op jit(solution)/shard_map/ppermute | solution.py:481
  7.0 2.0 %collective-permute-start.4 = (bf16[1040,128]{1,0:T(8,128)(2,1)S(1)}, bf16[1040,128]{1,0:T(8,128)(2,1)S(1)}, u32[]{:S(2)}, u32[]{:S(2)}) collective-permute-start(bf16[1040,128]{1,0:T(8,128)(2,1)S(1)} %get-tuple-element.55), channel_id=1, source_target_pairs={{0,32},{16,48},{32,0},{48,16},{1,33},{17,49},{33,1},{49,17},{2,34}... | collective-permute-start | bytes 798728 | tf_op jit(solution)/shard_map/ppermute | solution.py:476
  9.0 4.3 %shard_map.154 = (bf16[256,1024]{1,0:T(8,128)(2,1)S(1)}, bf16[256,1024]{1,0:T(8,128)(2,1)S(1)}, bf16[256,1024]{1,0:T(8,128)(2,1)S(1)}, bf16[256,1024]{1,0:T(8,12...) custom-call(bf16[256,1024]{1,0:T(8,128)(2,1)S(1)} %get-tuple-element, ...), custom_call_target="tpu_custom_call" | custom-call | flops 4000000000 | bytes 4000000 | tf_op jit(solution)/shard_map/pallas_call | solution.py:459
  13.3 0.1 collective-permute-done.2.up_ref
  13.4 5.1 %collective-permute-done.3.down_ref = bf16[1040,128]{1,0:T(8,128)(2,1)S(1)} collective-permute-done((bf16[1040,128]{1,0:T(8,128)(2,1)S(1)}, bf16[1040,128]{1,0:T(8,128)(2,1)S(1)}, u32[]{:S(2)}, u32[]{:S(2)}) %collective-permute-start.3) | collective-permute-done | bytes 266272 | tf_op jit(solution)/shard_map/ppermute | solution.py:481
  18.5 1.8 %collective-permute-done.4.h_ref = bf16[1040,128]{1,0:T(8,128)(2,1)S(1)} collective-permute-done((bf16[1040,128]{1,0:T(8,128)(2,1)S(1)}, bf16[1040,128]{1,0:T(8,128)(2,1)S(1)}, u32[]{:S(2)}, u32[]{:S(2)}) %collective-permute-start.4) | collective-permute-done | bytes 266272 | tf_op jit(solution)/shard_map/ppermute | solution.py:476
  20.3 1.0 %shard_map.155 = (f32[8,16]{1,0:T(8,128)S(1)}, bf16[2,128,1024]{2,1,0:T(8,128)(2,1)S(1)}, f32[8,16]{1,0:T(8,128)S(1)}) custom-call(bf16[1040,128]{1,0:T(8,128)(2,1)S(1)} %collective-permute-done.2.up_ref, bf16[1040,128]{1,0:T(8,128)(2,1)S(1)} %collective-permute-done.3.down_ref, bf16[1040,128]{1,0:T(8,128)(2,1)S(1)} %collective-permute-done.4.h_ref, ...), custom_call_target="tpu_custom_call" | custom-call | flops 500000000 | bytes 500000 | tf_op jit(solution)/shard_map/pallas_call | solution.py:459
  21.3 2.0 %collective-permute-start.8 = (f32[8,16]{1,0:T(8,128)S(1)}, f32[8,16]{1,0:T(8,128)S(1)}, u32[]{:S(2)}, u32[]{:S(2)}) collective-permute-start(f32[8,16]{1,0:T(8,128)S(1)} %get-tuple-element.83.a_ref), channel_id=1, source_target_pairs={{0,48},{16,32},{32,16},{48,0},{1,49},{17,33},{33,17},{49,1},{2,50}... | collective-permute-start | bytes 1544 | tf_op jit(solution)/shard_map/ppermute | solution.py:476
  23.2 1.3 %collective-permute-start.7 = (f32[8,16]{1,0:T(8,128)S(1)}, f32[8,16]{1,0:T(8,128)S(1)}, u32[]{:S(2)}, u32[]{:S(2)}) collective-permute-start(f32[8,16]{1,0:T(8,128)S(1)} %get-tuple-element.83.a_ref), channel_id=1, source_target_pairs={{0,32},{16,48},{32,0},{48,16},{1,33},{17,49},{33,1},{49,17},{2,34}... | collective-permute-start | bytes 1544 | tf_op jit(solution)/shard_map/ppermute | solution.py:476
  24.5 0.9 %collective-permute-start.6 = (f32[8,16]{1,0:T(8,128)S(1)}, f32[8,16]{1,0:T(8,128)S(1)}, u32[]{:S(2)}, u32[]{:S(2)}) collective-permute-start(f32[8,16]{1,0:T(8,128)S(1)} %get-tuple-element.83.a_ref), channel_id=1, source_target_pairs={{0,16},{16,0},{32,48},{48,32},{1,17},{17,1},{33,49},{49,33},{2,18}... | collective-permute-start | bytes 1544 | tf_op jit(solution)/shard_map/ppermute | solution.py:476
  25.4 0.5 %shard_map.157 = (f32[128,256]{1,0:T(8,128)S(1)}, bf16[128,256]{1,0:T(8,128)(2,1)S(1)}) custom-call(bf16[2,128,1024]{2,1,0:T(8,128)(2,1)S(1)} %get-tuple-element.68.both_ref, bf16[2,256,1024]{2,1,0:T(8,128)(2,1)S(1)} %get-tuple-element.51.qq_ref, f32[8,1024]{1,0:T(8,128)S(1)} %get-tuple-element.52.wide_ref, f32[128,256]{1,0:T(8,128)S(1)} %get-tuple-element.79.dr_ref, ...), custom_call_target="tpu_custom_call" | custom-call | flops 1000000000 | bytes 1000000 | tf_op jit(solution)/shard_map/pallas_call | solution.py:459
  25.9 0.3 collective-permute-start.5
  26.2 0.0 collective-permute-done.8.d_ref
  26.2 2.1 %collective-permute-done.7.c_ref = f32[8,16]{1,0:T(8,128)S(1)} collective-permute-done((f32[8,16]{1,0:T(8,128)S(1)}, f32[8,16]{1,0:T(8,128)S(1)}, u32[]{:S(2)}, u32[]{:S(2)}) %collective-permute-start.7) | collective-permute-done | bytes 544 | tf_op jit(solution)/shard_map/ppermute | solution.py:476
  28.3 0.0 collective-permute-done.6.b_ref
  28.3 2.8 %collective-permute-start.11 = (f32[8,16]{1,0:T(8,128)S(1)}, f32[8,16]{1,0:T(8,128)S(1)}, u32[]{:S(2)}, u32[]{:S(2)}) collective-permute-start(f32[8,16]{1,0:T(8,128)S(1)} %shard_map.158.a_ref), channel_id=1, source_target_pairs={{0,192},{64,128},{128,64},{192,0},{1,193},{65,129},{129,65},{193,1... | collective-permute-start | bytes 1544 | tf_op jit(solution)/shard_map/ppermute | solution.py:476
  31.2 0.8 %collective-permute-start.10 = (f32[8,16]{1,0:T(8,128)S(1)}, f32[8,16]{1,0:T(8,128)S(1)}, u32[]{:S(2)}, u32[]{:S(2)}) collective-permute-start(f32[8,16]{1,0:T(8,128)S(1)} %shard_map.158.a_ref), channel_id=1, source_target_pairs={{0,128},{64,192},{128,0},{192,64},{1,129},{65,193},{129,1},{193,65... | collective-permute-start | bytes 1544 | tf_op jit(solution)/shard_map/ppermute | solution.py:476
  32.0 0.5 %collective-permute-start.9 = (f32[8,16]{1,0:T(8,128)S(1)}, f32[8,16]{1,0:T(8,128)S(1)}, u32[]{:S(2)}, u32[]{:S(2)}) collective-permute-start(f32[8,16]{1,0:T(8,128)S(1)} %shard_map.158.a_ref), channel_id=1, source_target_pairs={{0,64},{64,0},{128,192},{192,128},{1,65},{65,1},{129,193},{193,129... | collective-permute-start | bytes 1544 | tf_op jit(solution)/shard_map/ppermute | solution.py:476
  32.5 2.5 %shard_map.156 = (bf16[256,1024]{1,0:T(8,128)(2,1)}, bf16[256,1024]{1,0:T(8,128)(2,1)}, f32[16,256]{1,0:T(8,128)}) custom-call(bf16[2,128,1024]{2,1,0:T(8,128)(2,1)S(1)} %get-tuple-element.68.both_ref, bf16[2,256,128]{2,1,0:T(8,128)(2,1)S(1)} %get-tuple-element.69.keys_ref, bf16[2,256,1024]{2,1,0:T(8,128)(2,1)S(1)} %get-tuple-element.51.qq_ref, ...), custom_call_target="tpu_custom_call" | custom-call | flops 2000000000 | bytes 2000000 | tf_op jit(solution)/shard_map/pallas_call | solution.py:459
  35.0 0.0 collective-permute-done.11.d_ref
  35.0 1.3 %collective-permute-done.10.c_ref = f32[8,16]{1,0:T(8,128)S(1)} collective-permute-done((f32[8,16]{1,0:T(8,128)S(1)}, f32[8,16]{1,0:T(8,128)S(1)}, u32[]{:S(2)}, u32[]{:S(2)}) %collective-permute-start.10) | collective-permute-done | bytes 544 | tf_op jit(solution)/shard_map/ppermute | solution.py:476
  36.3 0.0 collective-permute-done.9.b_ref
  36.3 0.0 collective-permute-done.5.got_ref
  36.3 0.7 %shard_map.159 = (f32[64,256]{1,0:T(8,128)}, f32[64,256]{1,0:T(8,128)}, f32[1,16]{1,0:T(1,128)}, f32[1,16]{1,0:T(1,128)}, f32[1,16]{1,0:T(1,128)}) custom-call(f32[128,256]{1,0:T(8,128)S(1)} %get-tuple-element.81.keep_ref, bf16[128,256]{1,0:T(8,128)(2,1)S(1)} %collective-permute-done.5.got_ref, f32[8,16]{1,0:T(8,128)S(1)} %shard_map.158.a_ref, ...), custom_call_target="tpu_custom_call" | custom-call | flops 200000000 | bytes 200000 | tf_op jit(solution)/shard_map/pallas_call | solution.py:459
  (1 shorter events, 0.0 us)
Async XLA Ops:
  0.6 2.5 %collective-permute-start = (bf16[64,256]{1,0:T(8,128)(2,1)}, bf16[64,256]{1,0:T(8,128)(2,1)S(1)}, u32[]{:S(2)}, u32[]{:S(2)}) collective-permute-start(bf16[64,256]{1,0:T(8,128)(2,1)} %bitcast.32), channel_id=1, source_target_pairs={{0,1},{1,0},{2,3},{3,2},{4,5},{5,4},{6,7},{7,6},{8,9},{9,8},{10,11... | collective-permute-start | bytes 98312 | tf_op jit(solution)/shard_map/ppermute | solution.py:476
  0.7 2.4 %collective-permute-start.1 = (bf16[64,256]{1,0:T(8,128)(2,1)}, bf16[64,256]{1,0:T(8,128)(2,1)S(1)}, u32[]{:S(2)}, u32[]{:S(2)}) collective-permute-start(bf16[64,256]{1,0:T(8,128)(2,1)} %bitcast.34), channel_id=1, source_target_pairs={{0,1},{1,0},{2,3},{3,2},{4,5},{5,4},{6,7},{7,6},{8,9},{9,8},{10,11... | collective-permute-start | bytes 98312 | tf_op jit(solution)/shard_map/ppermute | solution.py:476
  3.7 9.7 %collective-permute-start.2 = (bf16[1040,128]{1,0:T(8,128)(2,1)S(1)}, bf16[1040,128]{1,0:T(8,128)(2,1)S(1)}, u32[]{:S(2)}, u32[]{:S(2)}) collective-permute-start(bf16[1040,128]{1,0:T(8,128)(2,1)S(1)} %get-tuple-element.53), channel_id=1, source_target_pairs={{0,16},{16,32},{32,48},{48,0},{1,17},{17,33},{33,49},{49,1},{2,18}... | collective-permute-start | bytes 798728 | tf_op jit(solution)/shard_map/ppermute | solution.py:481
  5.3 13.2 %collective-permute-start.3 = (bf16[1040,128]{1,0:T(8,128)(2,1)S(1)}, bf16[1040,128]{1,0:T(8,128)(2,1)S(1)}, u32[]{:S(2)}, u32[]{:S(2)}) collective-permute-start(bf16[1040,128]{1,0:T(8,128)(2,1)S(1)} %get-tuple-element.54), channel_id=1, source_target_pairs={{0,48},{16,0},{32,16},{48,32},{1,49},{17,1},{33,17},{49,33},{2,50}... | collective-permute-start | bytes 798728 | tf_op jit(solution)/shard_map/ppermute | solution.py:481
  7.0 13.3 %collective-permute-start.4 = (bf16[1040,128]{1,0:T(8,128)(2,1)S(1)}, bf16[1040,128]{1,0:T(8,128)(2,1)S(1)}, u32[]{:S(2)}, u32[]{:S(2)}) collective-permute-start(bf16[1040,128]{1,0:T(8,128)(2,1)S(1)} %get-tuple-element.55), channel_id=1, source_target_pairs={{0,32},{16,48},{32,0},{48,16},{1,33},{17,49},{33,1},{49,17},{2,34}... | collective-permute-start | bytes 798728 | tf_op jit(solution)/shard_map/ppermute | solution.py:476
  21.3 5.0 %collective-permute-start.8 = (f32[8,16]{1,0:T(8,128)S(1)}, f32[8,16]{1,0:T(8,128)S(1)}, u32[]{:S(2)}, u32[]{:S(2)}) collective-permute-start(f32[8,16]{1,0:T(8,128)S(1)} %get-tuple-element.83.a_ref), channel_id=1, source_target_pairs={{0,48},{16,32},{32,16},{48,0},{1,49},{17,33},{33,17},{49,1},{2,50}... | collective-permute-start | bytes 1544 | tf_op jit(solution)/shard_map/ppermute | solution.py:476
  23.2 5.1 %collective-permute-start.7 = (f32[8,16]{1,0:T(8,128)S(1)}, f32[8,16]{1,0:T(8,128)S(1)}, u32[]{:S(2)}, u32[]{:S(2)}) collective-permute-start(f32[8,16]{1,0:T(8,128)S(1)} %get-tuple-element.83.a_ref), channel_id=1, source_target_pairs={{0,32},{16,48},{32,0},{48,16},{1,33},{17,49},{33,1},{49,17},{2,34}... | collective-permute-start | bytes 1544 | tf_op jit(solution)/shard_map/ppermute | solution.py:476
  24.5 3.8 %collective-permute-start.6 = (f32[8,16]{1,0:T(8,128)S(1)}, f32[8,16]{1,0:T(8,128)S(1)}, u32[]{:S(2)}, u32[]{:S(2)}) collective-permute-start(f32[8,16]{1,0:T(8,128)S(1)} %get-tuple-element.83.a_ref), channel_id=1, source_target_pairs={{0,16},{16,0},{32,48},{48,32},{1,17},{17,1},{33,49},{49,33},{2,18}... | collective-permute-start | bytes 1544 | tf_op jit(solution)/shard_map/ppermute | solution.py:476
  25.9 10.4 %collective-permute-start.5 = (bf16[128,256]{1,0:T(8,128)(2,1)S(1)}, bf16[128,256]{1,0:T(8,128)(2,1)S(1)}, u32[]{:S(2)}, u32[]{:S(2)}) collective-permute-start(bf16[128,256]{1,0:T(8,128)(2,1)S(1)} %get-tuple-element.82), channel_id=1, source_target_pairs={{0,1},{1,0},{2,3},{3,2},{4,5},{5,4},{6,7},{7,6},{8,9},{9,8},{10,11... | collective-permute-start | bytes 196616 | tf_op jit(solution)/shard_map/ppermute | solution.py:476
  28.3 6.7 %collective-permute-start.11 = (f32[8,16]{1,0:T(8,128)S(1)}, f32[8,16]{1,0:T(8,128)S(1)}, u32[]{:S(2)}, u32[]{:S(2)}) collective-permute-start(f32[8,16]{1,0:T(8,128)S(1)} %shard_map.158.a_ref), channel_id=1, source_target_pairs={{0,192},{64,128},{128,64},{192,0},{1,193},{65,129},{129,65},{193,1... | collective-permute-start | bytes 1544 | tf_op jit(solution)/shard_map/ppermute | solution.py:476
  31.2 5.1 %collective-permute-start.10 = (f32[8,16]{1,0:T(8,128)S(1)}, f32[8,16]{1,0:T(8,128)S(1)}, u32[]{:S(2)}, u32[]{:S(2)}) collective-permute-start(f32[8,16]{1,0:T(8,128)S(1)} %shard_map.158.a_ref), channel_id=1, source_target_pairs={{0,128},{64,192},{128,0},{192,64},{1,129},{65,193},{129,1},{193,65... | collective-permute-start | bytes 1544 | tf_op jit(solution)/shard_map/ppermute | solution.py:476
  32.0 4.3 %collective-permute-start.9 = (f32[8,16]{1,0:T(8,128)S(1)}, f32[8,16]{1,0:T(8,128)S(1)}, u32[]{:S(2)}, u32[]{:S(2)}) collective-permute-start(f32[8,16]{1,0:T(8,128)S(1)} %shard_map.158.a_ref), channel_id=1, source_target_pairs={{0,64},{64,0},{128,192},{192,128},{1,65},{65,1},{129,193},{193,129... | collective-permute-start | bytes 1544 | tf_op jit(solution)/shard_map/ppermute | solution.py:476
